TPU v7x, 512 devices: a whole 4x8x8 slice. The times are simulated.
512 devices in a mesh: win: 8 (over x, y_lo), tile: 64 (over y_hi, z, core).
Axes of the slice: x: 4, y: 8 (y_hi: 4, y_lo: 2; y = y_hi * 2 + y_lo), z: 8, core: 2. Of those that a mesh axis runs over, the one named last changes fastest.
Arguments:
- increments: float32 [8, 16, 8192, 128], P('win', None, 'tile'), may hold values from -6 to 6
- multipliers: float32 [8, 16, 8192, 128], P('win', None, 'tile'), may hold values from -6 to 6
- departure_weight: float32 [8192, 128], P('tile'), may hold values from 0.2 to 0.8
- upstream: int32 [8192, 128], P('tile'), may hold values from -2 to 2
- level_offset: int32 [8192, 128], P('tile'), may hold values from -1 to 1
- diffusivity: float32 [8192, 128], P('tile'), may hold values from 0.02 to 0.24
- std_dev: float32 [8192, 128], P('tile'), may hold values from 0.5 to 2
- vertical_inverse: float32 [16, 16], replicated, may hold values from -0.1 to 1.2, as said below
Outputs:
- primal_out: float32 [8, 16, 8192, 128], P('win', None, 'tile')
- dual_out: float32 [8, 16, 8192, 128], P('win', None, 'tile')
Inputs may be any that keep to these rules, and one draw needn't show every extreme that they name: `vertical_inverse`: A full-rank matrix with a diagonal near one and small off-diagonal entries of both signs.
All inputs are finite; a program needn't handle non-finite values.
Results may differ from a plain program's by a relative error of at most 0.0001.
Values sent between devices are 32-bit elements; how exact they have to be, the bound alone decides.
No kernel may reach another device: no remote copies, remote signals or barrier semaphores. Data moves between devices by JAX's collectives and lax.ppermute only.
A program may use at most 64 MiB of HBM per device.

v0:
```python
import jax
import jax.numpy as jnp
from jax import lax
from jax.sharding import PartitionSpec as P

SWEEPS = 4


def with_halo(value, sides, width):
    for axis, dim in sides:
        size, length = (lax.axis_size(axis), value.shape[dim])
        up = [(i, (i + 1) % size) for i in range(size)]
        down = [(j, i) for i, j in up]
        last = lax.slice_in_dim(value, length - width, length, axis=dim)
        initial = lax.slice_in_dim(value, 0, width, axis=dim)
        before = lax.ppermute(last, axis, up)
        after = lax.ppermute(initial, axis, down)
        value = jnp.concatenate([before, value, after], axis=dim)
    return value


def from_behind(value, axis, by):
    size = lax.axis_size(axis)
    pairs = [(i, i + by) for i in range(size) if 0 <= i + by < size]
    return lax.ppermute(value, axis, pairs)


def level_shift(values, level_step):
    if level_step == 0:
        return values
    zero_row = jnp.zeros_like(values[:1])
    if level_step > 0:
        return jnp.concatenate([values[level_step:], zero_row], 0)
    return jnp.concatenate([zero_row, values[:level_step]], 0)


def advect_local(extended, table_inner):
    width_x = extended.shape[1] - 4
    center = extended[:, 2 : 2 + width_x]
    weight = table_inner[0, 2 : 2 + width_x]
    offset_code = table_inner[1, 2 : 2 + width_x]
    departed = jnp.zeros_like(center)
    for shift_x in range(-2, 3):
        window = extended[:, 2 + shift_x : 2 + shift_x + width_x]
        for shift_z in (-1, 0, 1):
            selector = (offset_code == float(3 * shift_x + shift_z + 7)).astype(jnp.float32)
            departed = departed + selector * level_shift(window, shift_z)
    return (1.0 - weight) * center + weight * departed


def adjoint_local(extended, table_inner):
    width_x = extended.shape[1] - 4
    center = extended[:, 2 : 2 + width_x]
    weight = table_inner[0, 2 : 2 + width_x]
    weight_ext = table_inner[0]
    code_ext = table_inner[1]
    returned = jnp.zeros_like(center)
    for shift_x in range(-2, 3):
        for shift_z in (-1, 0, 1):
            selector = (code_ext == float(3 * shift_x + shift_z + 7)).astype(jnp.float32)
            source = selector * weight_ext * level_shift(extended, -shift_z)
            returned = returned + source[:, 2 - shift_x : 2 - shift_x + width_x]
    return (1.0 - weight) * center + returned


def diffuse(extended, diffusion_ext, vertical_inverse):
    interior = extended[:, 1:-1]
    diffusion = diffusion_ext[1:-1]
    zero_row = jnp.zeros_like(interior[:, :, :1])
    northern = jnp.concatenate([interior[:, :, 1:], zero_row], 2)
    southern = jnp.concatenate([zero_row, interior[:, :, :-1]], 2)
    smooth = (
        interior
        + diffusion * (extended[:, 2:] + extended[:, :-2] - 2.0 * interior)
        + diffusion * (northern + southern - 2.0 * interior)
    )
    level_count, column_count, row_count = smooth.shape
    blended = jnp.dot(
        vertical_inverse,
        smooth.reshape(level_count, column_count * row_count),
        precision=lax.Precision.HIGHEST,
        preferred_element_type=jnp.float32,
    )
    return blended.reshape(level_count, column_count, row_count)


def per_device(
    increments,
    multipliers,
    departure_weight,
    upstream,
    level_offset,
    diffusivity,
    std_dev,
    vertical_inverse,
):
    increment = increments[0]
    multiplier = multipliers[0]
    width_x = increment.shape[1]
    offset_code = upstream.astype(jnp.float32) * 3.0 + level_offset.astype(jnp.float32) + 7.0
    columns = jnp.stack([departure_weight, offset_code, diffusivity])
    columns_ext = with_halo(columns, (("tile", 1),), 4)
    table_inner = columns_ext[:, 2 : 2 + width_x + 4]
    diffusion_ext = columns_ext[2]
    stacked = with_halo(jnp.stack([increment, multiplier]), (("tile", 2),), 2)
    carried = advect_local(stacked[0], table_inner)
    pulled = adjoint_local(stacked[1], table_inner)
    arrived = from_behind(carried, "win", 1)
    came_back = from_behind(pulled, "win", -1)
    smoothed = std_dev * multiplier
    for sweep_index in range(SWEEPS):
        extended = with_halo(smoothed, (("tile", 1),), 1)
        smoothed = diffuse(extended, diffusion_ext[3 : width_x + 5], vertical_inverse)
    primal_row = std_dev * smoothed + increment - arrived
    dual_row = multiplier - came_back
    return (primal_row[None], dual_row[None])


def solution(mesh):
    in_specs = (
        P("win", None, "tile", None),
        P("win", None, "tile", None),
        P("tile", None),
        P("tile", None),
        P("tile", None),
        P("tile", None),
        P("tile", None),
        P(),
    )
    out_specs = (P("win", None, "tile", None), P("win", None, "tile", None))
    return jax.shard_map(
        per_device, mesh=mesh, in_specs=in_specs, out_specs=out_specs, check_vma=False
    )
```

profile of v0, /device:TPU:6, one launch (start us, length us, event | category | flops | bytes accessed | tf_op | source)
XLA Modules:
  0.0 127.4 jit_solution(6244650803646587460)
XLA Ops:
  0.6 0.0 copy-start
  0.7 1.0 compare_convert_fusion.14
  1.6 0.7 pad_maximum_fusion.16
  2.4 1.9 %collective-permute-start.11 = (f32[3,4,128]{2,1,0:T(4,128)S(1)}, f32[3,4,128]{2,1,0:T(4,128)S(1)}, u32[]{:S(2)}, u32[]{:S(2)}) collective-permute-start(f32[3,4,128]{2,1,0:T(4,128)S(1)} %get-tuple-element.41), channel_id=1, source_target_pairs={{0,1},{1,2},{2,3},{3,4},{4,5},{5,6},{6,7},{7,8},{8,9},{9,10},{10,1... | collective-permute-start | bytes 18440 | tf_op jit(solution)/shard_map/ppermute | solution.py:16
  4.3 0.0 copy-start.4
  4.3 0.0 copy-start.3
  4.3 14.2 %collective-permute-start.12 = (f32[3,4,128]{2,1,0:T(4,128)S(1)}, f32[3,4,128]{2,1,0:T(4,128)S(1)}, u32[]{:S(2)}, u32[]{:S(2)}) collective-permute-start(f32[3,4,128]{2,1,0:T(4,128)S(1)} %get-tuple-element.42), channel_id=1, source_target_pairs={{1,0},{2,1},{3,2},{4,3},{5,4},{6,5},{7,6},{8,7},{9,8},{10,9},{11,1... | collective-permute-start | bytes 18440 | tf_op jit(solution)/shard_map/ppermute | solution.py:17
  18.5 1.3 %constant_dynamic-update-slice_fusion.1 = f32[2,16,128,128]{3,2,1,0:T(8,128)S(1)} fusion(f32[1,16,128,128]{3,2,1,0:T(8,128)} %param.8), kind=kLoop, calls=%fused_computation.141 | loop fusion | bytes 2097152
  19.9 0.1 constant_dynamic-update-slice_fusion
  20.0 1.9 %collective-permute-start.8 = (f32[2,16,2,128]{3,2,1,0:T(2,128)S(1)}, f32[2,16,2,128]{3,2,1,0:T(2,128)S(1)}, u32[]{:S(2)}, u32[]{:S(2)}) collective-permute-start(f32[2,16,2,128]{3,2,1,0:T(2,128)S(1)} %get-tuple-element.11), channel_id=1, source_target_pairs={{0,1},{1,2},{2,3},{3,4},{4,5},{5,6},{6,7},{7,8},{8,9},{9,10},{10,1... | collective-permute-start | bytes 98312 | tf_op jit(solution)/shard_map/ppermute | solution.py:16
  21.9 7.9 %collective-permute-start.9 = (f32[2,16,2,128]{3,2,1,0:T(2,128)S(1)}, f32[2,16,2,128]{3,2,1,0:T(2,128)S(1)}, u32[]{:S(2)}, u32[]{:S(2)}) collective-permute-start(f32[2,16,2,128]{3,2,1,0:T(2,128)S(1)} %get-tuple-element.12), channel_id=1, source_target_pairs={{1,0},{2,1},{3,2},{4,3},{5,4},{6,5},{7,6},{8,7},{9,8},{10,9},{11,1... | collective-permute-start | bytes 98312 | tf_op jit(solution)/shard_map/ppermute | solution.py:17
  29.8 0.0 collective-permute-done.11
  29.8 0.0 collective-permute-done.12
  29.9 0.1 select_bitcast_fusion.13
  30.2 0.0 collective-permute-done.8
  30.2 1.2 collective-permute-done.9
  31.4 0.2 pad_maximum_fusion
  31.6 0.1 slice_bitcast_fusion.3
  31.7 0.1 slice_bitcast_fusion
  31.9 2.1 %fusion.11 = f32[16,128,128]{2,1,0:T(8,128)S(1)} fusion(f32[15,132,128]{2,1,0:T(8,128)S(1)} %get-tuple-element.8, f32[16,132,128]{2,1,0:T(8,128)S(1)} %get-tuple-element.9, f32[15,132,128]{2,1,0:T(8,128)S(1)} %get-tuple-element.7, f32[128,128]{1,0:T(8,128)S(1)} %slice.378, f32[128,128]{1,0:T(8,128)S(1)} %slice.376, f32[128,128]{1,0:T(8,128)S(1)} %slice.375, ...), kind=kLoop, calls=%fused_computation.20 | loop fusion | flops 8126464 | bytes 9367552 | tf_op jit(solution)/shard_map/add | solution.py:63
  34.0 2.9 %collective-permute-start.13 = (f32[16,128,128]{2,1,0:T(8,128)S(1)}, f32[16,128,128]{2,1,0:T(8,128)S(1)}, u32[]{:S(2)}, u32[]{:S(2)}) collective-permute-start(f32[16,128,128]{2,1,0:T(8,128)S(1)} %fusion.11), channel_id=1, source_target_pairs={{64,0},{128,64},{192,128},{256,192},{320,256},{384,320},{448,384},... | collective-permute-start | bytes 3145736 | tf_op jit(solution)/shard_map/ppermute | solution.py:25
  36.9 0.1 compare_convert_fusion.13
  36.9 1.2 fusion.63
  38.1 0.0 copy-start.5
  38.2 1.7 %fusion.28 = f32[16,128,128]{2,1,0:T(8,128)S(1)} fusion(f32[16,132,128]{2,1,0:T(8,128)S(1)} %get-tuple-element.10, f32[15,128,128]{2,1,0:T(8,128)S(1)} %get-tuple-element.14, f32[15,128,128]{2,1,0:T(8,128)S(1)} %get-tuple-element.21, f32[15,128,128]{2,1,0:T(8,128)S(1)} %get-tuple-element.22, f32[15,128,128]{2,1,0:T(8,128)S(1)} %get-tuple-element.15, ...), kind=kLoop, calls=%fused_computation.51 | loop fusion | flops 8388608 | bytes 17235968 | tf_op jit(solution)/shard_map/add | solution.py:48
  39.9 3.1 %collective-permute-start.10 = (f32[16,128,128]{2,1,0:T(8,128)S(1)}, f32[16,128,128]{2,1,0:T(8,128)S(1)}, u32[]{:S(2)}, u32[]{:S(2)}) collective-permute-start(f32[16,128,128]{2,1,0:T(8,128)S(1)} %fusion.28), channel_id=1, source_target_pairs={{0,64},{64,128},{128,192},{192,256},{256,320},{320,384},{384,448},... | collective-permute-start | bytes 3145736 | tf_op jit(solution)/shard_map/ppermute | solution.py:25
  42.9 17.5 %collective-permute-done.13 = f32[16,128,128]{2,1,0:T(8,128)S(1)} collective-permute-done((f32[16,128,128]{2,1,0:T(8,128)S(1)}, f32[16,128,128]{2,1,0:T(8,128)S(1)}, u32[]{:S(2)}, u32[]{:S(2)}) %collective-permute-start.13) | collective-permute-done | bytes 1048608 | tf_op jit(solution)/shard_map/ppermute | solution.py:25
  60.5 1.2 fusion.61
  61.6 7.1 %collective-permute-start = (f32[16,1,128]{2,1,0:T(1,128)S(1)}, f32[16,1,128]{2,1,0:T(1,128)S(1)}, u32[]{:S(2)}, u32[]{:S(2)}) collective-permute-start(f32[16,1,128]{2,1,0:T(1,128)S(1)} %get-tuple-element.39), channel_id=1, source_target_pairs={{1,0},{2,1},{3,2},{4,3},{5,4},{6,5},{7,6},{8,7},{9,8},{10,9},{11,1... | collective-permute-start | bytes 24584 | tf_op jit(solution)/shard_map/ppermute | solution.py:17
  68.7 1.9 %collective-permute-start.1 = (f32[16,1,128]{2,1,0:T(1,128)S(1)}, f32[16,1,128]{2,1,0:T(1,128)S(1)}, u32[]{:S(2)}, u32[]{:S(2)}) collective-permute-start(f32[16,1,128]{2,1,0:T(1,128)S(1)} %get-tuple-element.40), channel_id=1, source_target_pairs={{0,1},{1,2},{2,3},{3,4},{4,5},{5,6},{6,7},{7,8},{8,9},{9,10},{10,1... | collective-permute-start | bytes 24584 | tf_op jit(solution)/shard_map/ppermute | solution.py:16
  70.7 0.4 fusion.70
  71.0 0.0 collective-permute-done
  71.0 12.0 %collective-permute-done.1 = f32[16,1,128]{2,1,0:T(1,128)S(1)} collective-permute-done((f32[16,1,128]{2,1,0:T(1,128)S(1)}, f32[16,1,128]{2,1,0:T(1,128)S(1)}, u32[]{:S(2)}, u32[]{:S(2)}) %collective-permute-start.1) | collective-permute-done | bytes 8224 | tf_op jit(solution)/shard_map/ppermute | solution.py:16
  83.0 0.6 fusion.60
  83.6 1.6 %convolution_bitcast_fusion.3 = f32[2,8,128,128]{3,1,2,0:T(8,128)S(1)} fusion(f32[16,16]{1,0:T(8,128)S(1)} %copy-done, f32[2,8,128,128]{3,2,1,0:T(8,128)S(1)} %bitcast.101), kind=kOutput, calls=%fused_computation.4 | convolution fusion | flops 50331648 | bytes 2098176 | tf_op jit(solution)/shard_map/dot_general | solution.py:78
  85.2 0.2 copy.11
  85.5 1.9 %collective-permute-start.2 = (f32[16,1,128]{2,1,0:T(1,128)S(1)}, f32[16,1,128]{2,1,0:T(1,128)S(1)}, u32[]{:S(2)}, u32[]{:S(2)}) collective-permute-start(f32[16,1,128]{2,1,0:T(1,128)S(1)} %get-tuple-element.35), channel_id=1, source_target_pairs={{1,0},{2,1},{3,2},{4,3},{5,4},{6,5},{7,6},{8,7},{9,8},{10,9},{11,1... | collective-permute-start | bytes 24584 | tf_op jit(solution)/shard_map/ppermute | solution.py:17
  87.4 2.4 %collective-permute-start.3 = (f32[16,1,128]{2,1,0:T(1,128)S(1)}, f32[16,1,128]{2,1,0:T(1,128)S(1)}, u32[]{:S(2)}, u32[]{:S(2)}) collective-permute-start(f32[16,1,128]{2,1,0:T(1,128)S(1)} %get-tuple-element.36), channel_id=1, source_target_pairs={{0,1},{1,2},{2,3},{3,4},{4,5},{5,6},{6,7},{7,8},{8,9},{9,10},{10,1... | collective-permute-start | bytes 24584 | tf_op jit(solution)/shard_map/ppermute | solution.py:16
  89.8 0.4 fusion.68
  90.2 0.0 collective-permute-done.2
  90.2 6.4 %collective-permute-done.3 = f32[16,1,128]{2,1,0:T(1,128)S(1)} collective-permute-done((f32[16,1,128]{2,1,0:T(1,128)S(1)}, f32[16,1,128]{2,1,0:T(1,128)S(1)}, u32[]{:S(2)}, u32[]{:S(2)}) %collective-permute-start.3) | collective-permute-done | bytes 8224 | tf_op jit(solution)/shard_map/ppermute | solution.py:16
  96.6 0.6 fusion.55
  97.2 1.6 %convolution_bitcast_fusion.2 = f32[2,8,128,128]{3,1,2,0:T(8,128)S(1)} fusion(f32[16,16]{1,0:T(8,128)S(1)} %copy-done, f32[2,8,128,128]{3,2,1,0:T(8,128)S(1)} %bitcast.102), kind=kOutput, calls=%fused_computation.3 | convolution fusion | flops 50331648 | bytes 2098176 | tf_op jit(solution)/shard_map/dot_general | solution.py:78
  98.8 0.2 copy.13
  99.0 1.9 %collective-permute-start.4 = (f32[16,1,128]{2,1,0:T(1,128)S(1)}, f32[16,1,128]{2,1,0:T(1,128)S(1)}, u32[]{:S(2)}, u32[]{:S(2)}) collective-permute-start(f32[16,1,128]{2,1,0:T(1,128)S(1)} %get-tuple-element.31), channel_id=1, source_target_pairs={{1,0},{2,1},{3,2},{4,3},{5,4},{6,5},{7,6},{8,7},{9,8},{10,9},{11,1... | collective-permute-start | bytes 24584 | tf_op jit(solution)/shard_map/ppermute | solution.py:17
  101.0 2.6 %collective-permute-start.5 = (f32[16,1,128]{2,1,0:T(1,128)S(1)}, f32[16,1,128]{2,1,0:T(1,128)S(1)}, u32[]{:S(2)}, u32[]{:S(2)}) collective-permute-start(f32[16,1,128]{2,1,0:T(1,128)S(1)} %get-tuple-element.32), channel_id=1, source_target_pairs={{0,1},{1,2},{2,3},{3,4},{4,5},{5,6},{6,7},{7,8},{8,9},{9,10},{10,1... | collective-permute-start | bytes 24584 | tf_op jit(solution)/shard_map/ppermute | solution.py:16
  103.6 0.4 fusion.66
  103.9 0.0 collective-permute-done.4
  103.9 6.2 %collective-permute-done.5 = f32[16,1,128]{2,1,0:T(1,128)S(1)} collective-permute-done((f32[16,1,128]{2,1,0:T(1,128)S(1)}, f32[16,1,128]{2,1,0:T(1,128)S(1)}, u32[]{:S(2)}, u32[]{:S(2)}) %collective-permute-start.5) | collective-permute-done | bytes 8224 | tf_op jit(solution)/shard_map/ppermute | solution.py:16
  110.2 0.6 fusion.50
  110.8 1.6 %convolution_bitcast_fusion.1 = f32[2,8,128,128]{3,1,2,0:T(8,128)S(1)} fusion(f32[16,16]{1,0:T(8,128)S(1)} %copy-done, f32[2,8,128,128]{3,2,1,0:T(8,128)S(1)} %bitcast.103), kind=kOutput, calls=%fused_computation.2 | convolution fusion | flops 50331648 | bytes 2098176 | tf_op jit(solution)/shard_map/dot_general | solution.py:78
  112.4 0.2 copy.15
  112.6 1.9 %collective-permute-start.6 = (f32[16,1,128]{2,1,0:T(1,128)S(1)}, f32[16,1,128]{2,1,0:T(1,128)S(1)}, u32[]{:S(2)}, u32[]{:S(2)}) collective-permute-start(f32[16,1,128]{2,1,0:T(1,128)S(1)} %get-tuple-element.27), channel_id=1, source_target_pairs={{1,0},{2,1},{3,2},{4,3},{5,4},{6,5},{7,6},{8,7},{9,8},{10,9},{11,1... | collective-permute-start | bytes 24584 | tf_op jit(solution)/shard_map/ppermute | solution.py:17
  114.6 2.4 %collective-permute-start.7 = (f32[16,1,128]{2,1,0:T(1,128)S(1)}, f32[16,1,128]{2,1,0:T(1,128)S(1)}, u32[]{:S(2)}, u32[]{:S(2)}) collective-permute-start(f32[16,1,128]{2,1,0:T(1,128)S(1)} %get-tuple-element.28), channel_id=1, source_target_pairs={{0,1},{1,2},{2,3},{3,4},{4,5},{5,6},{6,7},{7,8},{8,9},{9,10},{10,1... | collective-permute-start | bytes 24584 | tf_op jit(solution)/shard_map/ppermute | solution.py:16
  117.0 0.4 fusion.64
  117.3 0.0 collective-permute-done.6
  117.3 6.4 %collective-permute-done.7 = f32[16,1,128]{2,1,0:T(1,128)S(1)} collective-permute-done((f32[16,1,128]{2,1,0:T(1,128)S(1)}, f32[16,1,128]{2,1,0:T(1,128)S(1)}, u32[]{:S(2)}, u32[]{:S(2)}) %collective-permute-start.7) | collective-permute-done | bytes 8224 | tf_op jit(solution)/shard_map/ppermute | solution.py:16
  123.7 0.6 fusion.45
  124.4 0.0 copy-start.2
  124.4 1.6 %convolution_bitcast_fusion = f32[2,8,128,128]{3,1,2,0:T(8,128)S(1)} fusion(f32[16,16]{1,0:T(8,128)S(1)} %copy-done, f32[2,8,128,128]{3,2,1,0:T(8,128)S(1)} %bitcast.104), kind=kOutput, calls=%fused_computation.1 | convolution fusion | flops 50331648 | bytes 2098176 | tf_op jit(solution)/shard_map/dot_general | solution.py:78
  126.0 0.2 copy.17
  126.2 0.0 collective-permute-done.10
  126.2 0.0 copy-done.2
  126.2 1.2 fusion.1
  (28 shorter events, 0.2 us)
Async XLA Ops:
  0.6 83.0 %copy-start = (f32[16,16]{1,0:T(8,128)S(1)}, f32[16,16]{1,0:T(8,128)}, u32[]{:S(2)}) copy-start(f32[16,16]{1,0:T(8,128)} %param.15) | copy-start | bytes 3076
  0.6 19.2 %copy-start.1 = (f32[1,16,128,128]{3,2,1,0:T(8,128)S(1)}, f32[1,16,128,128]{3,2,1,0:T(8,128)}, u32[]{:S(2)}) copy-start(f32[1,16,128,128]{3,2,1,0:T(8,128)} %param.9) | copy-start | bytes 3145732
  2.4 27.4 %collective-permute-start.11 = (f32[3,4,128]{2,1,0:T(4,128)S(1)}, f32[3,4,128]{2,1,0:T(4,128)S(1)}, u32[]{:S(2)}, u32[]{:S(2)}) collective-permute-start(f32[3,4,128]{2,1,0:T(4,128)S(1)} %get-tuple-element.41), channel_id=1, source_target_pairs={{0,1},{1,2},{2,3},{3,4},{4,5},{5,6},{6,7},{7,8},{8,9},{9,10},{10,1... | collective-permute-start | bytes 18440 | tf_op jit(solution)/shard_map/ppermute | solution.py:16
  4.3 25.5 %copy-start.4 = (f32[128,128]{1,0:T(8,128)S(1)}, f32[128,128]{1,0:T(8,128)}, u32[]{:S(2)}) copy-start(f32[128,128]{1,0:T(8,128)} %param.10) | copy-start | bytes 196612
  4.3 25.5 %copy-start.3 = (f32[128,128]{1,0:T(8,128)S(1)}, f32[128,128]{1,0:T(8,128)}, u32[]{:S(2)}) copy-start(f32[128,128]{1,0:T(8,128)} %param.13) | copy-start | bytes 196612
  4.3 25.5 %collective-permute-start.12 = (f32[3,4,128]{2,1,0:T(4,128)S(1)}, f32[3,4,128]{2,1,0:T(4,128)S(1)}, u32[]{:S(2)}, u32[]{:S(2)}) collective-permute-start(f32[3,4,128]{2,1,0:T(4,128)S(1)} %get-tuple-element.42), channel_id=1, source_target_pairs={{1,0},{2,1},{3,2},{4,3},{5,4},{6,5},{7,6},{8,7},{9,8},{10,9},{11,1... | collective-permute-start | bytes 18440 | tf_op jit(solution)/shard_map/ppermute | solution.py:17
  20.0 10.2 %collective-permute-start.8 = (f32[2,16,2,128]{3,2,1,0:T(2,128)S(1)}, f32[2,16,2,128]{3,2,1,0:T(2,128)S(1)}, u32[]{:S(2)}, u32[]{:S(2)}) collective-permute-start(f32[2,16,2,128]{3,2,1,0:T(2,128)S(1)} %get-tuple-element.11), channel_id=1, source_target_pairs={{0,1},{1,2},{2,3},{3,4},{4,5},{5,6},{6,7},{7,8},{8,9},{9,10},{10,1... | collective-permute-start | bytes 98312 | tf_op jit(solution)/shard_map/ppermute | solution.py:16
  21.9 9.4 %collective-permute-start.9 = (f32[2,16,2,128]{3,2,1,0:T(2,128)S(1)}, f32[2,16,2,128]{3,2,1,0:T(2,128)S(1)}, u32[]{:S(2)}, u32[]{:S(2)}) collective-permute-start(f32[2,16,2,128]{3,2,1,0:T(2,128)S(1)} %get-tuple-element.12), channel_id=1, source_target_pairs={{1,0},{2,1},{3,2},{4,3},{5,4},{6,5},{7,6},{8,7},{9,8},{10,9},{11,1... | collective-permute-start | bytes 98312 | tf_op jit(solution)/shard_map/ppermute | solution.py:17
  34.0 26.5 %collective-permute-start.13 = (f32[16,128,128]{2,1,0:T(8,128)S(1)}, f32[16,128,128]{2,1,0:T(8,128)S(1)}, u32[]{:S(2)}, u32[]{:S(2)}) collective-permute-start(f32[16,128,128]{2,1,0:T(8,128)S(1)} %fusion.11), channel_id=1, source_target_pairs={{64,0},{128,64},{192,128},{256,192},{320,256},{384,320},{448,384},... | collective-permute-start | bytes 3145736 | tf_op jit(solution)/shard_map/ppermute | solution.py:25
  38.1 22.3 %copy-start.5 = (f32[128,128]{1,0:T(8,128)S(1)}, f32[128,128]{1,0:T(8,128)}, u32[]{:S(2)}) copy-start(f32[128,128]{1,0:T(8,128)} %param.14) | copy-start | bytes 196612
  39.9 86.3 %collective-permute-start.10 = (f32[16,128,128]{2,1,0:T(8,128)S(1)}, f32[16,128,128]{2,1,0:T(8,128)S(1)}, u32[]{:S(2)}, u32[]{:S(2)}) collective-permute-start(f32[16,128,128]{2,1,0:T(8,128)S(1)} %fusion.28), channel_id=1, source_target_pairs={{0,64},{64,128},{128,192},{192,256},{256,320},{320,384},{384,448},... | collective-permute-start | bytes 3145736 | tf_op jit(solution)/shard_map/ppermute | solution.py:25
  61.6 9.4 %collective-permute-start = (f32[16,1,128]{2,1,0:T(1,128)S(1)}, f32[16,1,128]{2,1,0:T(1,128)S(1)}, u32[]{:S(2)}, u32[]{:S(2)}) collective-permute-start(f32[16,1,128]{2,1,0:T(1,128)S(1)} %get-tuple-element.39), channel_id=1, source_target_pairs={{1,0},{2,1},{3,2},{4,3},{5,4},{6,5},{7,6},{8,7},{9,8},{10,9},{11,1... | collective-permute-start | bytes 24584 | tf_op jit(solution)/shard_map/ppermute | solution.py:17
  68.7 14.3 %collective-permute-start.1 = (f32[16,1,128]{2,1,0:T(1,128)S(1)}, f32[16,1,128]{2,1,0:T(1,128)S(1)}, u32[]{:S(2)}, u32[]{:S(2)}) collective-permute-start(f32[16,1,128]{2,1,0:T(1,128)S(1)} %get-tuple-element.40), channel_id=1, source_target_pairs={{0,1},{1,2},{2,3},{3,4},{4,5},{5,6},{6,7},{7,8},{8,9},{9,10},{10,1... | collective-permute-start | bytes 24584 | tf_op jit(solution)/shard_map/ppermute | solution.py:16
  85.5 4.7 %collective-permute-start.2 = (f32[16,1,128]{2,1,0:T(1,128)S(1)}, f32[16,1,128]{2,1,0:T(1,128)S(1)}, u32[]{:S(2)}, u32[]{:S(2)}) collective-permute-start(f32[16,1,128]{2,1,0:T(1,128)S(1)} %get-tuple-element.35), channel_id=1, source_target_pairs={{1,0},{2,1},{3,2},{4,3},{5,4},{6,5},{7,6},{8,7},{9,8},{10,9},{11,1... | collective-permute-start | bytes 24584 | tf_op jit(solution)/shard_map/ppermute | solution.py:17
  87.4 9.2 %collective-permute-start.3 = (f32[16,1,128]{2,1,0:T(1,128)S(1)}, f32[16,1,128]{2,1,0:T(1,128)S(1)}, u32[]{:S(2)}, u32[]{:S(2)}) collective-permute-start(f32[16,1,128]{2,1,0:T(1,128)S(1)} %get-tuple-element.36), channel_id=1, source_target_pairs={{0,1},{1,2},{2,3},{3,4},{4,5},{5,6},{6,7},{7,8},{8,9},{9,10},{10,1... | collective-permute-start | bytes 24584 | tf_op jit(solution)/shard_map/ppermute | solution.py:16
  99.0 4.9 %collective-permute-start.4 = (f32[16,1,128]{2,1,0:T(1,128)S(1)}, f32[16,1,128]{2,1,0:T(1,128)S(1)}, u32[]{:S(2)}, u32[]{:S(2)}) collective-permute-start(f32[16,1,128]{2,1,0:T(1,128)S(1)} %get-tuple-element.31), channel_id=1, source_target_pairs={{1,0},{2,1},{3,2},{4,3},{5,4},{6,5},{7,6},{8,7},{9,8},{10,9},{11,1... | collective-permute-start | bytes 24584 | tf_op jit(solution)/shard_map/ppermute | solution.py:17
  101.0 9.2 %collective-permute-start.5 = (f32[16,1,128]{2,1,0:T(1,128)S(1)}, f32[16,1,128]{2,1,0:T(1,128)S(1)}, u32[]{:S(2)}, u32[]{:S(2)}) collective-permute-start(f32[16,1,128]{2,1,0:T(1,128)S(1)} %get-tuple-element.32), channel_id=1, source_target_pairs={{0,1},{1,2},{2,3},{3,4},{4,5},{5,6},{6,7},{7,8},{8,9},{9,10},{10,1... | collective-permute-start | bytes 24584 | tf_op jit(solution)/shard_map/ppermute | solution.py:16
  112.6 4.7 %collective-permute-start.6 = (f32[16,1,128]{2,1,0:T(1,128)S(1)}, f32[16,1,128]{2,1,0:T(1,128)S(1)}, u32[]{:S(2)}, u32[]{:S(2)}) collective-permute-start(f32[16,1,128]{2,1,0:T(1,128)S(1)} %get-tuple-element.27), channel_id=1, source_target_pairs={{1,0},{2,1},{3,2},{4,3},{5,4},{6,5},{7,6},{8,7},{9,8},{10,9},{11,1... | collective-permute-start | bytes 24584 | tf_op jit(solution)/shard_map/ppermute | solution.py:17
  114.6 9.2 %collective-permute-start.7 = (f32[16,1,128]{2,1,0:T(1,128)S(1)}, f32[16,1,128]{2,1,0:T(1,128)S(1)}, u32[]{:S(2)}, u32[]{:S(2)}) collective-permute-start(f32[16,1,128]{2,1,0:T(1,128)S(1)} %get-tuple-element.28), channel_id=1, source_target_pairs={{0,1},{1,2},{2,3},{3,4},{4,5},{5,6},{6,7},{7,8},{8,9},{9,10},{10,1... | collective-permute-start | bytes 24584 | tf_op jit(solution)/shard_map/ppermute | solution.py:16
  124.4 1.9 %copy-start.2 = (f32[1,16,128,128]{3,2,1,0:T(8,128)S(1)}, f32[1,16,128,128]{3,2,1,0:T(8,128)}, u32[]{:S(2)}) copy-start(f32[1,16,128,128]{3,2,1,0:T(8,128)} %param.8) | copy-start | bytes 3145732
where the time goes:
time: 128 us; the launch traced here: 127 us
  starting transfers between devices  54 us (42%)
  waiting for transfers between devices  49.7 us (39%)
  other arithmetic  10.7 us (8%)
  matrix products  6.43 us (5%)
  local copies, waits for them, and re-layouts  5.34 us (4%)
    ppermute x6, starting transfers between devices, with_halo(): after = lax.ppermute(initial, axis, down)  34.9 us
    ppermute x6, waiting for transfers between devices, with_halo(): before = lax.ppermute(last, axis, up)  31 us
    ppermute x2, waiting for transfers between devices, from_behind(): return lax.ppermute(value, axis, pairs)  17.5 us
    ppermute x6, starting transfers between devices, with_halo(): before = lax.ppermute(last, axis, up)  13.1 us
    dot_general x4, matrix products, diffuse(): jnp.dot(vertical_inverse, smooth.reshape(level_count, column_count * row_...  6.43 us
    ppermute x2, starting transfers between devices, from_behind(): return lax.ppermute(value, axis, pairs)  5.91 us
  transfers between devices with their start and end apart: 14, of which 6 were waited for; matrix products, arithmetic and copies ran while one was open for 13% of the time, Pallas kernels for 0%

commit v1 on v0

v1 whole, which is shorter than its diff:
```python
import functools

import jax
import jax.numpy as jnp
from jax import lax
from jax.experimental import pallas as pl
from jax.experimental.pallas import tpu as pltpu
from jax.sharding import PartitionSpec as P

SWEEPS = 4
REACH = 2
PAD = 8
EARLY = 1080
VMEM_LIMIT = 40 * 1024 * 1024
VMEM_WHOLE = 60 * 1024 * 1024


def moved(value, win_by, tile_by):
    wins, tiles = lax.axis_size("win"), lax.axis_size("tile")
    pairs = [
        (k * tiles + t, (k + win_by) * tiles + (t + tile_by) % tiles)
        for k in range(wins)
        for t in range(tiles)
        if 0 <= k + win_by < wins
    ]
    return lax.ppermute(value, ("win", "tile"), pairs)


def params():
    return pltpu.CompilerParams(vmem_limit_bytes=VMEM_LIMIT)


def cost(flops, touched):
    return pl.CostEstimate(flops=flops, bytes_accessed=touched, transcendentals=0)


class Rows:
    def __init__(self, levels):
        base = SWEEPS * levels
        self.std = slice(base, base + SWEEPS)
        self.kappa = slice(base + SWEEPS, base + 2 * SWEEPS)
        self.weight = slice(base + 2 * SWEEPS, base + 2 * SWEEPS + REACH)
        self.code = slice(base + 2 * SWEEPS + REACH, base + 2 * SWEEPS + 2 * REACH)
        self.fields = base + 4 * SWEEPS
        self.count = self.fields + REACH * levels

    def mul(self, l):
        return slice(SWEEPS * l, SWEEPS * (l + 1))

    def inc(self, l):
        return slice(self.fields + REACH * l, self.fields + REACH * (l + 1))


def pack_one(levels, refs, out, from_end):
    inc, mul, std, kappa, weight, up, lev = refs
    wide = slice(PAD - SWEEPS, PAD) if from_end else slice(0, SWEEPS)
    thin = slice(PAD - REACH, PAD) if from_end else slice(0, REACH)
    spot = Rows(levels)
    for l in range(levels):
        out[spot.mul(l)] = mul[0, l, wide]
        out[spot.inc(l)] = inc[0, l, thin]
    out[spot.std] = std[wide]
    out[spot.kappa] = kappa[wide]
    out[spot.weight] = weight[thin]
    out[spot.code] = up[thin].astype(jnp.float32) * 3.0 + lev[thin].astype(jnp.float32)
    gap = slice(spot.code.stop, spot.fields)
    out[gap] = jnp.zeros_like(out[gap])


def pack_both(levels, *refs):
    pack_one(levels, refs[0:7], refs[14], True)
    pack_one(levels, refs[7:14], refs[15], False)


def pack(inc, mul, std, kappa, weight, up, lev):
    _, levels, width, rows = mul.shape
    arrays = [inc, mul, std, kappa, weight, up, lev]
    specs = []
    for block in (width // PAD - 1, 0):
        for a in arrays:
            lead = a.shape[:-2]
            index = (0,) * len(lead) + (block, 0)
            specs.append(
                pl.BlockSpec((*lead, PAD, rows), functools.partial(lambda index, i: index, index))
            )
    height = Rows(levels).count
    return pl.pallas_call(
        functools.partial(pack_both, levels),
        grid=(1,),
        in_specs=specs,
        out_specs=[pl.BlockSpec((height, rows), lambda i: (0, 0))] * 2,
        out_shape=[jax.ShapeDtypeStruct((height, rows), jnp.float32)] * 2,
        compiler_params=pltpu.CompilerParams(vmem_limit_bytes=VMEM_WHOLE),
        cost_estimate=cost(1000, 1000),
    )(*(arrays * 2))


def forward_kernel(early, inc, mul, before, after, inc_out, mul_out):
    _, levels, width, rows = mul.shape
    spot = Rows(levels)
    base, half = levels * width - early, REACH * levels
    for l in range(levels):
        start = max(early - l * width, 0)
        if start < width:
            part = slice(l * width + start - early, (l + 1) * width - early)
            inc_out[part] = inc[0, l, start:]
            mul_out[part] = mul[0, l, start:]
    for l in range(levels):
        near = slice(base + REACH * l, base + REACH * (l + 1))
        far = slice(near.start + half, near.stop + half)
        first, last = before[spot.mul(l)], after[spot.mul(l)]
        mul_out[near] = first[SWEEPS - REACH :]
        mul_out[far] = last[:REACH]
        inc_out[near] = before[spot.inc(l)]
        inc_out[far] = after[spot.inc(l)]


def forward(early, inc, mul, before, after):
    _, levels, width, rows = mul.shape
    vmem = pl.BlockSpec(memory_space=pltpu.VMEM)
    height = levels * width - early + 2 * REACH * levels
    return pl.pallas_call(
        functools.partial(forward_kernel, early),
        in_specs=[vmem] * 4,
        out_specs=[vmem] * 2,
        out_shape=[jax.ShapeDtypeStruct((height, rows), jnp.float32)] * 2,
        compiler_params=params(),
        cost_estimate=cost(1000, 1000),
    )(inc, mul, before, after)


def covar_kernel(
    mul, inc, std, kappa, before, after, power, out, kappa_ext, field, smooth
):
    levels, width, rows = smooth.shape
    tall = width + 2 * PAD
    spot = Rows(levels)
    kappa_ext[...] = jnp.zeros_like(kappa_ext)
    field[...] = jnp.zeros_like(field)
    kappa_ext[PAD : PAD + width] = kappa[...]
    kappa_ext[PAD - SWEEPS : PAD] = before[spot.kappa]
    kappa_ext[PAD + width : PAD + width + SWEEPS] = after[spot.kappa]
    for l in range(levels):
        field[l, PAD - SWEEPS : PAD] = before[spot.std] * before[spot.mul(l)]
        field[l, PAD + width : PAD + width + SWEEPS] = after[spot.std] * after[spot.mul(l)]
    lane = lax.broadcasted_iota(jnp.int32, (tall, rows), 1)
    first, last = lane == 0, lane == rows - 1

    def one_level(l, carry):
        field[l, PAD : PAD + width] = std[...] * mul[0, l]
        value = field[l]
        for _ in range(SWEEPS):
            north = jnp.where(last, 0.0, pltpu.roll(value, rows - 1, 1))
            south = jnp.where(first, 0.0, pltpu.roll(value, 1, 1))
            around = pltpu.roll(value, 1, 0) + pltpu.roll(value, tall - 1, 0)
            value = value + kappa_ext[...] * ((around + (north + south)) - 4.0 * value)
        smooth[l] = value[PAD : PAD + width]
        return carry

    lax.fori_loop(0, levels, one_level, 0)
    step = 2 * PAD

    def one_block(b, carry):
        part = pl.ds(pl.multiple_of(b * step, step), step)
        fields = [smooth[m, part] for m in range(levels)]
        scale = std[part]
        for l in range(levels):
            total = power[l, 0] * fields[0]
            for m in range(1, levels):
                total = total + power[l, m] * fields[m]
            out[l, part] = scale * total + inc[0, l, part]
        return carry

    lax.fori_loop(0, width // step, one_block, 0)


def covar(mul, inc, std, kappa, before, after, power):
    _, levels, width, rows = mul.shape
    vmem = pl.BlockSpec(memory_space=pltpu.VMEM)
    return pl.pallas_call(
        covar_kernel,
        in_specs=[vmem] * 6 + [pl.BlockSpec(memory_space=pltpu.SMEM)],
        out_specs=vmem,
        out_shape=jax.ShapeDtypeStruct((levels, width, rows), jnp.float32),
        scratch_shapes=[
            pltpu.VMEM((width + 2 * PAD, rows), jnp.float32),
            pltpu.VMEM((levels, width + 2 * PAD, rows), jnp.float32),
            pltpu.VMEM((levels, width, rows), jnp.float32),
        ],
        compiler_params=params(),
        cost_estimate=cost(1000, 1000),
    )(mul, inc, std, kappa, before, after, power)


def fill_field(field, offset, width, first, rest):
    early = first.shape[0]
    levels = field.shape[0] - 2 * offset
    base, half = levels * width - early, REACH * levels
    for l in range(levels):
        begin, end = l * width, (l + 1) * width
        cut = min(max(early, begin), end)
        if cut > begin:
            field[l + offset, PAD : PAD + cut - begin] = first[begin:cut]
        if cut < end:
            part = slice(PAD + cut - begin, PAD + width)
            field[l + offset, part] = rest[cut - early : end - early]
        near = slice(base + REACH * l, base + REACH * (l + 1))
        field[l + offset, PAD - REACH : PAD] = rest[near]
        far = rest[near.start + half : near.stop + half]
        field[l + offset, PAD + width : PAD + width + REACH] = far


def primal_kernel(base, came_first, came, weight, up, lev, out, field, level_field):
    levels, width, rows = base.shape
    fill_field(field, 0, width, came_first, came)
    zero = jnp.zeros((width, rows), jnp.float32)
    level_field[0] = zero
    level_field[levels + 1] = zero

    def one_level(l, carry):
        step = up[...]
        total = field[l, PAD : PAD + width]
        for j in (-2, -1, 1, 2):
            total = jnp.where(step == j, field[l, PAD + j : PAD + j + width], total)
        level_field[l + 1] = total
        return carry

    lax.fori_loop(0, levels, one_level, 0)

    def combine(l, carry):
        pick = lev[...]
        departed = jnp.where(
            pick == 0,
            level_field[l + 1],
            jnp.where(pick == 1, level_field[l + 2], level_field[l]),
        )
        center = field[l, PAD : PAD + width]
        out[0, l] = base[l] - ((1.0 - weight[...]) * center + weight[...] * departed)
        return carry

    lax.fori_loop(0, levels, combine, 0)


def primal_final(base, came_first, came, weight, up, lev):
    levels, width, rows = base.shape
    vmem = pl.BlockSpec(memory_space=pltpu.VMEM)
    return pl.pallas_call(
        primal_kernel,
        in_specs=[vmem] * 6,
        out_specs=vmem,
        out_shape=jax.ShapeDtypeStruct((1, levels, width, rows), jnp.float32),
        scratch_shapes=[
            pltpu.VMEM((levels, width + 2 * PAD, rows), jnp.float32),
            pltpu.VMEM((levels + 2, width, rows), jnp.float32),
        ],
        compiler_params=params(),
        cost_estimate=cost(1000, 1000),
    )(base, came_first, came, weight, up, lev)


def dual_kernel(
    mul, came_first, came, before, after, weight, up, lev, out, field, weight_ext, up_ext, lev_ext
):
    _, levels, width, rows = mul.shape
    tall = width + 2 * PAD
    spot = Rows(levels)
    left, right = slice(PAD - REACH, PAD), slice(PAD + width, PAD + width + REACH)
    weight_ext[...] = jnp.zeros_like(weight_ext)
    up_ext[...] = jnp.zeros_like(up_ext)
    lev_ext[...] = jnp.zeros_like(lev_ext)
    weight_ext[PAD : PAD + width] = weight[...]
    up_ext[PAD : PAD + width] = up[...]
    lev_ext[PAD : PAD + width] = lev[...]
    zero = jnp.zeros((tall, rows), jnp.float32)
    field[0] = zero
    field[levels + 1] = zero
    for side, part in ((before, left), (after, right)):
        weight_ext[part] = side[spot.weight]
        code = side[spot.code]
        step = jnp.floor((code + 1.5) * (1.0 / 3.0))
        up_ext[part] = step.astype(jnp.int32)
        lev_ext[part] = (code - 3.0 * step).astype(jnp.int32)
    for l in range(levels):
        field[l + 1, :PAD] = zero[:PAD]
        field[l + 1, PAD + width :] = zero[:PAD]
    fill_field(field, 1, width, came_first, came)

    def one_level(l, carry):
        pick = lev_ext[...]
        lifted = jnp.where(
            pick == 0, field[l + 1], jnp.where(pick == 1, field[l], field[l + 2])
        )
        source = weight_ext[...] * lifted
        step = up_ext[...]
        total = jnp.where(step == 0, source, 0.0)
        for j in (-2, -1, 1, 2):
            total = total + pltpu.roll(jnp.where(step == j, source, 0.0), j % tall, 0)
        returned = total[PAD : PAD + width]
        center = field[l + 1, PAD : PAD + width]
        out[0, l] = mul[0, l] - ((1.0 - weight[...]) * center + returned)
        return carry

    lax.fori_loop(0, levels, one_level, 0)


def dual_final(mul, came_first, came, before, after, weight, up, lev):
    _, levels, width, rows = mul.shape
    vmem = pl.BlockSpec(memory_space=pltpu.VMEM)
    tall = width + 2 * PAD
    return pl.pallas_call(
        dual_kernel,
        in_specs=[vmem] * 8,
        out_specs=vmem,
        out_shape=jax.ShapeDtypeStruct((1, levels, width, rows), jnp.float32),
        scratch_shapes=[
            pltpu.VMEM((levels + 2, tall, rows), jnp.float32),
            pltpu.VMEM((tall, rows), jnp.float32),
            pltpu.VMEM((tall, rows), jnp.int32),
            pltpu.VMEM((tall, rows), jnp.int32),
        ],
        compiler_params=params(),
        cost_estimate=cost(1000, 1000),
    )(mul, came_first, came, before, after, weight, up, lev)


def per_device(
    increments,
    multipliers,
    departure_weight,
    upstream,
    level_offset,
    diffusivity,
    std_dev,
    vertical_inverse,
):
    columns = (departure_weight, upstream, level_offset)
    _, levels, width, rows = multipliers.shape
    early = EARLY * levels * width // 2048
    inc_first = moved(increments.reshape(-1, rows)[:early], 1, 0)
    mul_first = moved(multipliers.reshape(-1, rows)[:early], -1, 0)
    to_right, to_left = pack(increments, multipliers, std_dev, diffusivity, *columns)
    before = moved(to_right, 0, 1)
    after = moved(to_left, 0, -1)
    inc_out, mul_out = forward(early, increments, multipliers, before, after)
    inc_rest = moved(inc_out, 1, 0)
    mul_rest = moved(mul_out, -1, 0)

    exact = dict(precision=lax.Precision.HIGHEST, preferred_element_type=jnp.float32)
    power = jnp.dot(vertical_inverse, vertical_inverse, **exact)
    power = jnp.dot(power, power, **exact)
    base = covar(multipliers, increments, std_dev, diffusivity, before, after, power)
    primal = primal_final(base, inc_first, inc_rest, *columns)
    weight, primal = lax.optimization_barrier((departure_weight, primal))
    dual = dual_final(
        multipliers, mul_first, mul_rest, before, after, weight, upstream, level_offset
    )
    return (primal, dual)


def solution(mesh):
    in_specs = (
        P("win", None, "tile", None),
        P("win", None, "tile", None),
        P("tile", None),
        P("tile", None),
        P("tile", None),
        P("tile", None),
        P("tile", None),
        P(),
    )
    out_specs = (P("win", None, "tile", None), P("win", None, "tile", None))
    return jax.shard_map(
        per_device, mesh=mesh, in_specs=in_specs, out_specs=out_specs, check_vma=False
    )
```

time: 128 us -> 64.6 us (0.50)
  the two profiles are of different devices: /device:TPU:6 before, /device:TPU:50 now
where the time goes in v1:
time: 64.6 us; the launch traced here: 64.3 us
  starting transfers between devices  27.5 us (43%)
  waiting for transfers between devices  21 us (33%)
  Pallas kernels  14.6 us (23%)
  between operations  0.82 us (1%)
    ppermute x6, starting transfers between devices, moved(): return lax.ppermute(value, ('win', 'tile'), pairs)  27.5 us
    ppermute x6, waiting for transfers between devices, moved(): return lax.ppermute(value, ('win', 'tile'), pairs)  21 us
    pallas_call x1, Pallas kernels, covar(): pl.pallas_call(covar_kernel, in_specs=[vmem] * 6 + [pl.BlockSpec(memory_s...  8.44 us
    pallas_call x1, Pallas kernels, dual_final(): pl.pallas_call(dual_kernel, in_specs=[vmem] * 8, out_specs=vmem, out_shap...  2.36 us
    pallas_call x1, Pallas kernels, primal_final(): pl.pallas_call(primal_kernel, in_specs=[vmem] * 6, out_specs=vmem, out_sh...  1.91 us
    pallas_call x1, Pallas kernels, pack(): pl.pallas_call(functools.partial(pack_both, levels), grid=(1,), in_specs=...  1.8 us
  transfers between devices with their start and end apart: 6, of which 2 were waited for; matrix products, arithmetic and copies ran while one was open for 1% of the time, Pallas kernels for 16%

profile of v1, /device:TPU:50, one launch (start us, length us, event | category | flops | bytes accessed | tf_op | source)
XLA Modules:
  0.0 64.3 jit_solution(6017604369500319377)
XLA Ops:
  0.6 0.0 copy-start
  0.6 0.0 copy-start.2
  0.7 1.8 %shard_map.95 = (f32[112,128]{1,0:T(8,128)}, f32[112,128]{1,0:T(8,128)}) custom-call(f32[1,16,128,128]{3,2,1,0:T(8,128)} %inc.3, f32[1,16,128,128]{3,2,1,0:T(8,128)} %mul.5, f32[128,128]{1,0:T(8,128)} %std.1, f32[128,128]{1,0:T(8,128)} %kappa.1, f32[128,128]{1,0:T(8,128)} %weight.2, s32[128,128]{1,0:T(8,128)} %up.3, s32[128,128]{1,0:T(8,128)} %lev.3, ...), custom_call_target="tpu_custom_call" | custom-call | flops 1000 | bytes 1000 | tf_op jit(solution)/shard_map/pallas_call | solution.py:87
  2.5 0.0 copy-start.1
  2.5 2.0 %collective-permute-start = (f32[112,128]{1,0:T(8,128)}, f32[112,128]{1,0:T(8,128)S(1)}, u32[]{:S(2)}, u32[]{:S(2)}) collective-permute-start(f32[112,128]{1,0:T(8,128)} %get-tuple-element.8), channel_id=1, source_target_pairs={{0,1},{1,2},{2,3},{3,4},{4,5},{5,6},{6,7},{7,8},{8,9},{9,10},{10,1... | collective-permute-start | bytes 172040 | tf_op jit(solution)/shard_map/ppermute | solution.py:26
  4.5 12.0 %collective-permute-start.1 = (f32[112,128]{1,0:T(8,128)}, f32[112,128]{1,0:T(8,128)S(1)}, u32[]{:S(2)}, u32[]{:S(2)}) collective-permute-start(f32[112,128]{1,0:T(8,128)} %get-tuple-element.9), channel_id=1, source_target_pairs={{0,63},{1,0},{2,1},{3,2},{4,3},{5,4},{6,5},{7,6},{8,7},{9,8},{10,9... | collective-permute-start | bytes 172040 | tf_op jit(solution)/shard_map/ppermute | solution.py:26
  16.5 0.0 copy-done.2
  16.5 2.6 %collective-permute-start.2 = (f32[1080,128]{1,0:T(8,128)S(1)}, f32[1080,128]{1,0:T(8,128)S(1)}, u32[]{:S(2)}, u32[]{:S(2)}) collective-permute-start(f32[1080,128]{1,0:T(8,128)S(1)} %slice.8), channel_id=1, source_target_pairs={{0,64},{1,65},{2,66},{3,67},{4,68},{5,69},{6,70},{7,71},{8,72},{9,... | collective-permute-start | bytes 1658888 | tf_op jit(solution)/shard_map/ppermute | solution.py:26
  19.1 0.0 copy-done.1
  19.2 4.2 %collective-permute-start.4 = (f32[1080,128]{1,0:T(8,128)S(1)}, f32[1080,128]{1,0:T(8,128)S(1)}, u32[]{:S(2)}, u32[]{:S(2)}) collective-permute-start(f32[1080,128]{1,0:T(8,128)S(1)} %slice.9), channel_id=1, source_target_pairs={{64,0},{65,1},{66,2},{67,3},{68,4},{69,5},{70,6},{71,7},{72,8},{73... | collective-permute-start | bytes 1658888 | tf_op jit(solution)/shard_map/ppermute | solution.py:26
  23.3 0.0 collective-permute-done.before
  23.3 0.0 collective-permute-done.1.after
  23.4 0.0 copy-start.6
  23.4 0.0 copy-start.7
  23.4 0.1 shard_map.97
  23.5 1.9 %collective-permute-start.3 = (f32[1032,128]{1,0:T(8,128)S(1)}, f32[1032,128]{1,0:T(8,128)S(1)}, u32[]{:S(2)}, u32[]{:S(2)}) collective-permute-start(f32[1032,128]{1,0:T(8,128)S(1)} %get-tuple-element.10), channel_id=1, source_target_pairs={{0,64},{1,65},{2,66},{3,67},{4,68},{5,69},{6,70},{7,71},{8,72},{9,... | collective-permute-start | bytes 1585160 | tf_op jit(solution)/shard_map/ppermute | solution.py:26
  25.4 4.8 %collective-permute-start.5 = (f32[1032,128]{1,0:T(8,128)S(1)}, f32[1032,128]{1,0:T(8,128)S(1)}, u32[]{:S(2)}, u32[]{:S(2)}) collective-permute-start(f32[1032,128]{1,0:T(8,128)S(1)} %get-tuple-element.12), channel_id=1, source_target_pairs={{64,0},{65,1},{66,2},{67,3},{68,4},{69,5},{70,6},{71,7},{72,8},{73... | collective-permute-start | bytes 1585160 | tf_op jit(solution)/shard_map/ppermute | solution.py:26
  30.2 0.0 copy-done
  30.2 0.1 fusion
  30.4 0.1 fusion.1.power
  30.5 0.0 copy-done.6
  30.5 0.0 copy-done.7
  30.5 0.0 copy-start.3
  30.5 0.0 copy-start.4
  30.5 0.0 copy-start.5
  30.6 8.4 %shard_map.96.base = f32[16,128,128]{2,1,0:T(8,128)S(1)} custom-call(f32[1,16,128,128]{3,2,1,0:T(8,128)S(1)} %copy-done.1, f32[1,16,128,128]{3,2,1,0:T(8,128)S(1)} %copy-done.2, f32[128,128]{1,0:T(8,128)S(1)} %copy-done.6, f32[128,128]{1,0:T(8,128)S(1)} %copy-done.7, f32[112,128]{1,0:T(8,128)S(1)} %collective-permute-done.before, ...), custom_call_target="tpu_custom_call" | custom-call | flops 1000 | bytes 1000 | tf_op jit(solution)/shard_map/pallas_call | solution.py:180
  39.0 0.0 collective-permute-done.2.came_first
  39.0 17.3 %collective-permute-done.3.came = f32[1032,128]{1,0:T(8,128)S(1)} collective-permute-done((f32[1032,128]{1,0:T(8,128)S(1)}, f32[1032,128]{1,0:T(8,128)S(1)}, u32[]{:S(2)}, u32[]{:S(2)}) %collective-permute-start.3) | collective-permute-done | bytes 528416 | tf_op jit(solution)/shard_map/ppermute | solution.py:26
  56.3 0.0 copy-done.3
  56.3 0.0 copy-done.4
  56.3 0.0 copy-done.5
  56.3 1.9 %shard_map.98 = f32[1,16,128,128]{3,2,1,0:T(8,128)} custom-call(f32[16,128,128]{2,1,0:T(8,128)S(1)} %shard_map.96.base, f32[1080,128]{1,0:T(8,128)S(1)} %collective-permute-done.2.came_first, f32[1032,128]{1,0:T(8,128)S(1)} %collective-permute-done.3.came, f32[128,128]{1,0:T(8,128)S(1)} %copy-done.3, s32[128,128]{1,0:T(8,128)S(1)} %copy-done.4, ...), custom_call_target="tpu_custom_call" | custom-call | flops 1000 | bytes 1000 | tf_op jit(solution)/shard_map/pallas_call | solution.py:247
  58.2 0.0 collective-permute-done.4.came_first
  58.2 3.8 %collective-permute-done.5.came = f32[1032,128]{1,0:T(8,128)S(1)} collective-permute-done((f32[1032,128]{1,0:T(8,128)S(1)}, f32[1032,128]{1,0:T(8,128)S(1)}, u32[]{:S(2)}, u32[]{:S(2)}) %collective-permute-start.5) | collective-permute-done | bytes 528416 | tf_op jit(solution)/shard_map/ppermute | solution.py:26
  61.9 2.4 %shard_map.99 = f32[1,16,128,128]{3,2,1,0:T(8,128)} custom-call(f32[1,16,128,128]{3,2,1,0:T(8,128)S(1)} %copy-done.1, f32[1080,128]{1,0:T(8,128)S(1)} %collective-permute-done.4.came_first, f32[1032,128]{1,0:T(8,128)S(1)} %collective-permute-done.5.came, f32[112,128]{1,0:T(8,128)S(1)} %collective-permute-done.before, ...), custom_call_target="tpu_custom_call" | custom-call | flops 1000 | bytes 1000 | tf_op jit(solution)/shard_map/pallas_call | solution.py:310
  (2 shorter events, 0.1 us)
Async XLA Ops:
  0.6 29.6 %copy-start = (f32[16,16]{1,0:T(8,128)S(1)}, f32[16,16]{1,0:T(8,128)}, u32[]{:S(2)}) copy-start(f32[16,16]{1,0:T(8,128)} %param.15) | copy-start | bytes 3076
  0.6 15.8 %copy-start.2 = (f32[1,16,128,128]{3,2,1,0:T(8,128)S(1)}, f32[1,16,128,128]{3,2,1,0:T(8,128)}, u32[]{:S(2)}) copy-start(f32[1,16,128,128]{3,2,1,0:T(8,128)} %inc.3) | copy-start | bytes 3145732
  2.5 16.7 %copy-start.1 = (f32[1,16,128,128]{3,2,1,0:T(8,128)S(1)}, f32[1,16,128,128]{3,2,1,0:T(8,128)}, u32[]{:S(2)}) copy-start(f32[1,16,128,128]{3,2,1,0:T(8,128)} %mul.5) | copy-start | bytes 3145732
  2.5 20.9 %collective-permute-start = (f32[112,128]{1,0:T(8,128)}, f32[112,128]{1,0:T(8,128)S(1)}, u32[]{:S(2)}, u32[]{:S(2)}) collective-permute-start(f32[112,128]{1,0:T(8,128)} %get-tuple-element.8), channel_id=1, source_target_pairs={{0,1},{1,2},{2,3},{3,4},{4,5},{5,6},{6,7},{7,8},{8,9},{9,10},{10,1... | collective-permute-start | bytes 172040 | tf_op jit(solution)/shard_map/ppermute | solution.py:26
  4.5 18.8 %collective-permute-start.1 = (f32[112,128]{1,0:T(8,128)}, f32[112,128]{1,0:T(8,128)S(1)}, u32[]{:S(2)}, u32[]{:S(2)}) collective-permute-start(f32[112,128]{1,0:T(8,128)} %get-tuple-element.9), channel_id=1, source_target_pairs={{0,63},{1,0},{2,1},{3,2},{4,3},{5,4},{6,5},{7,6},{8,7},{9,8},{10,9... | collective-permute-start | bytes 172040 | tf_op jit(solution)/shard_map/ppermute | solution.py:26
  16.5 22.5 %collective-permute-start.2 = (f32[1080,128]{1,0:T(8,128)S(1)}, f32[1080,128]{1,0:T(8,128)S(1)}, u32[]{:S(2)}, u32[]{:S(2)}) collective-permute-start(f32[1080,128]{1,0:T(8,128)S(1)} %slice.8), channel_id=1, source_target_pairs={{0,64},{1,65},{2,66},{3,67},{4,68},{5,69},{6,70},{7,71},{8,72},{9,... | collective-permute-start | bytes 1658888 | tf_op jit(solution)/shard_map/ppermute | solution.py:26
  19.2 39.0 %collective-permute-start.4 = (f32[1080,128]{1,0:T(8,128)S(1)}, f32[1080,128]{1,0:T(8,128)S(1)}, u32[]{:S(2)}, u32[]{:S(2)}) collective-permute-start(f32[1080,128]{1,0:T(8,128)S(1)} %slice.9), channel_id=1, source_target_pairs={{64,0},{65,1},{66,2},{67,3},{68,4},{69,5},{70,6},{71,7},{72,8},{73... | collective-permute-start | bytes 1658888 | tf_op jit(solution)/shard_map/ppermute | solution.py:26
  23.4 7.1 %copy-start.6 = (f32[128,128]{1,0:T(8,128)S(1)}, f32[128,128]{1,0:T(8,128)}, u32[]{:S(2)}) copy-start(f32[128,128]{1,0:T(8,128)} %std.1) | copy-start | bytes 196612
  23.4 7.1 %copy-start.7 = (f32[128,128]{1,0:T(8,128)S(1)}, f32[128,128]{1,0:T(8,128)}, u32[]{:S(2)}) copy-start(f32[128,128]{1,0:T(8,128)} %kappa.1) | copy-start | bytes 196612
  23.5 32.8 %collective-permute-start.3 = (f32[1032,128]{1,0:T(8,128)S(1)}, f32[1032,128]{1,0:T(8,128)S(1)}, u32[]{:S(2)}, u32[]{:S(2)}) collective-permute-start(f32[1032,128]{1,0:T(8,128)S(1)} %get-tuple-element.10), channel_id=1, source_target_pairs={{0,64},{1,65},{2,66},{3,67},{4,68},{5,69},{6,70},{7,71},{8,72},{9,... | collective-permute-start | bytes 1585160 | tf_op jit(solution)/shard_map/ppermute | solution.py:26
  25.4 36.5 %collective-permute-start.5 = (f32[1032,128]{1,0:T(8,128)S(1)}, f32[1032,128]{1,0:T(8,128)S(1)}, u32[]{:S(2)}, u32[]{:S(2)}) collective-permute-start(f32[1032,128]{1,0:T(8,128)S(1)} %get-tuple-element.12), channel_id=1, source_target_pairs={{64,0},{65,1},{66,2},{67,3},{68,4},{69,5},{70,6},{71,7},{72,8},{73... | collective-permute-start | bytes 1585160 | tf_op jit(solution)/shard_map/ppermute | solution.py:26
  30.5 25.7 %copy-start.3 = (f32[128,128]{1,0:T(8,128)S(1)}, f32[128,128]{1,0:T(8,128)}, u32[]{:S(2)}) copy-start(f32[128,128]{1,0:T(8,128)} %weight.2) | copy-start | bytes 196612
  30.5 25.7 %copy-start.4 = (s32[128,128]{1,0:T(8,128)S(1)}, s32[128,128]{1,0:T(8,128)}, u32[]{:S(2)}) copy-start(s32[128,128]{1,0:T(8,128)} %up.3) | copy-start | bytes 196612
  30.5 25.7 %copy-start.5 = (s32[128,128]{1,0:T(8,128)S(1)}, s32[128,128]{1,0:T(8,128)}, u32[]{:S(2)}) copy-start(s32[128,128]{1,0:T(8,128)} %lev.3) | copy-start | bytes 196612

commit v2 on v1

--- a/solution.py
+++ b/solution.py
@@ -11,6 +11,7 @@
 REACH = 2
 PAD = 8
 EARLY = 1080
+LEAD = 1280
 VMEM_LIMIT = 40 * 1024 * 1024
 VMEM_WHOLE = 60 * 1024 * 1024
 
@@ -95,35 +96,37 @@
     )(*(arrays * 2))
 
 
-def forward_kernel(early, inc, mul, before, after, inc_out, mul_out):
+def forward_kernel(inc_early, mul_early, inc, mul, before, after, inc_out, mul_out):
     _, levels, width, rows = mul.shape
     spot = Rows(levels)
-    base, half = levels * width - early, REACH * levels
-    for l in range(levels):
-        start = max(early - l * width, 0)
-        if start < width:
-            part = slice(l * width + start - early, (l + 1) * width - early)
-            inc_out[part] = inc[0, l, start:]
-            mul_out[part] = mul[0, l, start:]
-    for l in range(levels):
-        near = slice(base + REACH * l, base + REACH * (l + 1))
-        far = slice(near.start + half, near.stop + half)
-        first, last = before[spot.mul(l)], after[spot.mul(l)]
-        mul_out[near] = first[SWEEPS - REACH :]
-        mul_out[far] = last[:REACH]
-        inc_out[near] = before[spot.inc(l)]
-        inc_out[far] = after[spot.inc(l)]
-
-
-def forward(early, inc, mul, before, after):
+    half = REACH * levels
+    for early, source, target in ((inc_early, inc, inc_out), (mul_early, mul, mul_out)):
+        base = levels * width - early
+        for l in range(levels):
+            start = max(early - l * width, 0)
+            if start < width:
+                part = slice(l * width + start - early, (l + 1) * width - early)
+                target[part] = source[0, l, start:]
+            near = slice(base + REACH * l, base + REACH * (l + 1))
+            far = slice(near.start + half, near.stop + half)
+            if source is inc:
+                target[near] = before[spot.inc(l)]
+                target[far] = after[spot.inc(l)]
+            else:
+                first, last = before[spot.mul(l)], after[spot.mul(l)]
+                target[near] = first[SWEEPS - REACH :]
+                target[far] = last[:REACH]
+
+
+def forward(inc_early, mul_early, inc, mul, before, after):
     _, levels, width, rows = mul.shape
     vmem = pl.BlockSpec(memory_space=pltpu.VMEM)
-    height = levels * width - early + 2 * REACH * levels
-    return pl.pallas_call(
-        functools.partial(forward_kernel, early),
+    heights = [levels * width - early + 2 * REACH * levels for early in (inc_early, mul_early)]
+    return pl.pallas_call(
+        functools.partial(forward_kernel, inc_early, mul_early),
         in_specs=[vmem] * 4,
         out_specs=[vmem] * 2,
-        out_shape=[jax.ShapeDtypeStruct((height, rows), jnp.float32)] * 2,
+        out_shape=[jax.ShapeDtypeStruct((h, rows), jnp.float32) for h in heights],
         compiler_params=params(),
         cost_estimate=cost(1000, 1000),
     )(inc, mul, before, after)
@@ -192,18 +195,20 @@
     )(mul, inc, std, kappa, before, after, power)
 
 
-def fill_field(field, offset, width, first, rest):
-    early = first.shape[0]
+def fill_field(field, offset, width, *pieces):
     levels = field.shape[0] - 2 * offset
-    base, half = levels * width - early, REACH * levels
+    rest, half = pieces[-1], REACH * levels
+    base = rest.shape[0] - 2 * half
+    start = 0
+    for piece in pieces:
+        stop = start + (base if piece is rest else piece.shape[0])
+        for l in range(levels):
+            begin, end = max(l * width, start), min((l + 1) * width, stop)
+            if begin < end:
+                part = slice(PAD + begin - l * width, PAD + end - l * width)
+                field[l + offset, part] = piece[begin - start : end - start]
+        start = stop
     for l in range(levels):
-        begin, end = l * width, (l + 1) * width
-        cut = min(max(early, begin), end)
-        if cut > begin:
-            field[l + offset, PAD : PAD + cut - begin] = first[begin:cut]
-        if cut < end:
-            part = slice(PAD + cut - begin, PAD + width)
-            field[l + offset, part] = rest[cut - early : end - early]
         near = slice(base + REACH * l, base + REACH * (l + 1))
         field[l + offset, PAD - REACH : PAD] = rest[near]
         far = rest[near.start + half : near.stop + half]
@@ -335,13 +340,16 @@
 ):
     columns = (departure_weight, upstream, level_offset)
     _, levels, width, rows = multipliers.shape
-    early = EARLY * levels * width // 2048
-    inc_first = moved(increments.reshape(-1, rows)[:early], 1, 0)
-    mul_first = moved(multipliers.reshape(-1, rows)[:early], -1, 0)
+    inc_early, mul_early = (n * levels * width // 2048 for n in (LEAD, EARLY))
+    inc_rows, mul_rows = increments.reshape(-1, rows), multipliers.reshape(-1, rows)
+    inc_first = moved(inc_rows[:inc_early], 1, 0)
+    mul_first = moved(mul_rows[:mul_early], -1, 0)
     to_right, to_left = pack(increments, multipliers, std_dev, diffusivity, *columns)
     before = moved(to_right, 0, 1)
     after = moved(to_left, 0, -1)
-    inc_out, mul_out = forward(early, increments, multipliers, before, after)
+    inc_out, mul_out = forward(
+        inc_early, mul_early, increments, multipliers, before, after
+    )
     inc_rest = moved(inc_out, 1, 0)
     mul_rest = moved(mul_out, -1, 0)
 

time: 64.6 us -> 59.5 us (0.921)
  the two profiles are of different devices: /device:TPU:50 before, /device:TPU:52 now
where the time goes in v2:
time: 59.5 us; the launch traced here: 59.1 us
  starting transfers between devices  26.4 us (44%)
  waiting for transfers between devices  15.8 us (27%)
  Pallas kernels  14.6 us (25%)
  local copies, waits for them, and re-layouts  1.23 us (2%)
  between operations  0.79 us (1%)
    ppermute x6, starting transfers between devices, moved(): return lax.ppermute(value, ('win', 'tile'), pairs)  26.4 us
    ppermute x6, waiting for transfers between devices, moved(): return lax.ppermute(value, ('win', 'tile'), pairs)  15.8 us
    pallas_call x1, Pallas kernels, covar(): pl.pallas_call(covar_kernel, in_specs=[vmem] * 6 + [pl.BlockSpec(memory_s...  8.45 us
    pallas_call x1, Pallas kernels, dual_final(): pl.pallas_call(dual_kernel, in_specs=[vmem] * 8, out_specs=vmem, out_shap...  2.36 us
    pallas_call x1, Pallas kernels, primal_final(): pl.pallas_call(primal_kernel, in_specs=[vmem] * 6, out_specs=vmem, out_sh...  1.99 us
    pallas_call x1, Pallas kernels, pack(): pl.pallas_call(functools.partial(pack_both, levels), grid=(1,), in_specs=...  1.73 us
  transfers between devices with their start and end apart: 6, of which 2 were waited for; matrix products, arithmetic and copies ran while one was open for 1% of the time, Pallas kernels for 21%

profile of v2, /device:TPU:52, one launch (start us, length us, event | category | flops | bytes accessed | tf_op | source)
XLA Modules:
  0.0 59.1 jit_solution(9320120813175256967)
XLA Ops:
  0.6 0.0 copy-start
  0.6 1.1 %slice.9 = f32[1,10,128,128]{3,2,1,0:T(8,128)S(1)} slice(f32[1,16,128,128]{3,2,1,0:T(8,128)} %inc.3), slice={[0:1], [0:10], [0:128], [0:128]} | slice | bytes 1310720 | tf_op jit(solution)/shard_map/slice | solution.py:345
  1.8 0.0 copy-start.1
  1.8 2.7 %collective-permute-start.2 = (f32[1280,128]{1,0:T(8,128)S(1)}, f32[1280,128]{1,0:T(8,128)S(1)}, u32[]{:S(2)}, u32[]{:S(2)}) collective-permute-start(f32[1280,128]{1,0:T(8,128)S(1)} %bitcast.7), channel_id=1, source_target_pairs={{0,64},{1,65},{2,66},{3,67},{4,68},{5,69},{6,70},{7,71},{8,72},{9,... | collective-permute-start | bytes 1966088 | tf_op jit(solution)/shard_map/ppermute | solution.py:27
  4.5 1.7 %shard_map.95 = (f32[112,128]{1,0:T(8,128)}, f32[112,128]{1,0:T(8,128)}) custom-call(f32[1,16,128,128]{3,2,1,0:T(8,128)} %inc.3, f32[1,16,128,128]{3,2,1,0:T(8,128)} %mul.5, f32[128,128]{1,0:T(8,128)} %std.1, f32[128,128]{1,0:T(8,128)} %kappa.1, f32[128,128]{1,0:T(8,128)} %weight.2, s32[128,128]{1,0:T(8,128)} %up.3, s32[128,128]{1,0:T(8,128)} %lev.3, ...), custom_call_target="tpu_custom_call" | custom-call | flops 1000 | bytes 1000 | tf_op jit(solution)/shard_map/pallas_call | solution.py:88
  6.3 0.0 copy-start.2
  6.3 2.0 %collective-permute-start = (f32[112,128]{1,0:T(8,128)}, f32[112,128]{1,0:T(8,128)S(1)}, u32[]{:S(2)}, u32[]{:S(2)}) collective-permute-start(f32[112,128]{1,0:T(8,128)} %get-tuple-element.8), channel_id=1, source_target_pairs={{0,1},{1,2},{2,3},{3,4},{4,5},{5,6},{6,7},{7,8},{8,9},{9,10},{10,1... | collective-permute-start | bytes 172040 | tf_op jit(solution)/shard_map/ppermute | solution.py:27
  8.3 11.7 %collective-permute-start.1 = (f32[112,128]{1,0:T(8,128)}, f32[112,128]{1,0:T(8,128)S(1)}, u32[]{:S(2)}, u32[]{:S(2)}) collective-permute-start(f32[112,128]{1,0:T(8,128)} %get-tuple-element.9), channel_id=1, source_target_pairs={{0,63},{1,0},{2,1},{3,2},{4,3},{5,4},{6,5},{7,6},{8,7},{9,8},{10,9... | collective-permute-start | bytes 172040 | tf_op jit(solution)/shard_map/ppermute | solution.py:27
  20.0 0.0 copy-done.1
  20.0 4.2 %collective-permute-start.4 = (f32[1080,128]{1,0:T(8,128)S(1)}, f32[1080,128]{1,0:T(8,128)S(1)}, u32[]{:S(2)}, u32[]{:S(2)}) collective-permute-start(f32[1080,128]{1,0:T(8,128)S(1)} %slice.12), channel_id=1, source_target_pairs={{64,0},{65,1},{66,2},{67,3},{68,4},{69,5},{70,6},{71,7},{72,8},{73... | collective-permute-start | bytes 1658888 | tf_op jit(solution)/shard_map/ppermute | solution.py:27
  24.2 6.0 %collective-permute-done.before = f32[112,128]{1,0:T(8,128)S(1)} collective-permute-done((f32[112,128]{1,0:T(8,128)}, f32[112,128]{1,0:T(8,128)S(1)}, u32[]{:S(2)}, u32[]{:S(2)}) %collective-permute-start) | collective-permute-done | bytes 57376 | tf_op jit(solution)/shard_map/ppermute | solution.py:27
  30.3 0.0 collective-permute-done.1.after
  30.3 0.0 copy-done.2
  30.3 0.0 copy-start.6
  30.3 0.0 copy-start.7
  30.3 0.1 shard_map.97
  30.4 1.9 %collective-permute-start.5 = (f32[1032,128]{1,0:T(8,128)S(1)}, f32[1032,128]{1,0:T(8,128)S(1)}, u32[]{:S(2)}, u32[]{:S(2)}) collective-permute-start(f32[1032,128]{1,0:T(8,128)S(1)} %get-tuple-element.12), channel_id=1, source_target_pairs={{64,0},{65,1},{66,2},{67,3},{68,4},{69,5},{70,6},{71,7},{72,8},{73... | collective-permute-start | bytes 1585160 | tf_op jit(solution)/shard_map/ppermute | solution.py:27
  32.3 3.9 %collective-permute-start.3 = (f32[832,128]{1,0:T(8,128)S(1)}, f32[832,128]{1,0:T(8,128)S(1)}, u32[]{:S(2)}, u32[]{:S(2)}) collective-permute-start(f32[832,128]{1,0:T(8,128)S(1)} %get-tuple-element.10), channel_id=1, source_target_pairs={{0,64},{1,65},{2,66},{3,67},{4,68},{5,69},{6,70},{7,71},{8,72},{9,... | collective-permute-start | bytes 1277960 | tf_op jit(solution)/shard_map/ppermute | solution.py:27
  36.2 0.0 copy-done
  36.2 0.1 fusion
  36.4 0.1 fusion.1.power
  36.5 0.0 copy-done.6
  36.5 0.0 copy-done.7
  36.5 0.0 copy-start.3
  36.5 0.0 copy-start.4
  36.5 0.0 copy-start.5
  36.5 8.4 %shard_map.96.base = f32[16,128,128]{2,1,0:T(8,128)S(1)} custom-call(f32[1,16,128,128]{3,2,1,0:T(8,128)S(1)} %copy-done.1, f32[1,16,128,128]{3,2,1,0:T(8,128)S(1)} %copy-done.2, f32[128,128]{1,0:T(8,128)S(1)} %copy-done.6, f32[128,128]{1,0:T(8,128)S(1)} %copy-done.7, f32[112,128]{1,0:T(8,128)S(1)} %collective-permute-done.before, ...), custom_call_target="tpu_custom_call" | custom-call | flops 1000 | bytes 1000 | tf_op jit(solution)/shard_map/pallas_call | solution.py:183
  45.0 9.7 %collective-permute-done.3.came = f32[832,128]{1,0:T(8,128)S(1)} collective-permute-done((f32[832,128]{1,0:T(8,128)S(1)}, f32[832,128]{1,0:T(8,128)S(1)}, u32[]{:S(2)}, u32[]{:S(2)}) %collective-permute-start.3) | collective-permute-done | bytes 426016 | tf_op jit(solution)/shard_map/ppermute | solution.py:27
  54.7 0.0 collective-permute-done.2.came_first
  54.7 0.0 copy-done.3
  54.7 0.0 copy-done.4
  54.7 0.0 copy-done.5
  54.8 2.0 %shard_map.98 = f32[1,16,128,128]{3,2,1,0:T(8,128)} custom-call(f32[16,128,128]{2,1,0:T(8,128)S(1)} %shard_map.96.base, f32[1280,128]{1,0:T(8,128)S(1)} %collective-permute-done.2.came_first, f32[832,128]{1,0:T(8,128)S(1)} %collective-permute-done.3.came, f32[128,128]{1,0:T(8,128)S(1)} %copy-done.3, s32[128,128]{1,0:T(8,128)S(1)} %copy-done.4, ...), custom_call_target="tpu_custom_call" | custom-call | flops 1000 | bytes 1000 | tf_op jit(solution)/shard_map/pallas_call | solution.py:252
  56.7 0.0 collective-permute-done.4.came_first
  56.7 0.0 collective-permute-done.5.came
  56.7 2.4 %shard_map.99 = f32[1,16,128,128]{3,2,1,0:T(8,128)} custom-call(f32[1,16,128,128]{3,2,1,0:T(8,128)S(1)} %copy-done.1, f32[1080,128]{1,0:T(8,128)S(1)} %collective-permute-done.4.came_first, f32[1032,128]{1,0:T(8,128)S(1)} %collective-permute-done.5.came, f32[112,128]{1,0:T(8,128)S(1)} %collective-permute-done.before, ...), custom_call_target="tpu_custom_call" | custom-call | flops 1000 | bytes 1000 | tf_op jit(solution)/shard_map/pallas_call | solution.py:315
  (1 shorter events, 0.0 us)
Async XLA Ops:
  0.6 35.6 %copy-start = (f32[16,16]{1,0:T(8,128)S(1)}, f32[16,16]{1,0:T(8,128)}, u32[]{:S(2)}) copy-start(f32[16,16]{1,0:T(8,128)} %param.15) | copy-start | bytes 3076
  1.8 18.2 %copy-start.1 = (f32[1,16,128,128]{3,2,1,0:T(8,128)S(1)}, f32[1,16,128,128]{3,2,1,0:T(8,128)}, u32[]{:S(2)}) copy-start(f32[1,16,128,128]{3,2,1,0:T(8,128)} %mul.5) | copy-start | bytes 3145732
  1.8 52.9 %collective-permute-start.2 = (f32[1280,128]{1,0:T(8,128)S(1)}, f32[1280,128]{1,0:T(8,128)S(1)}, u32[]{:S(2)}, u32[]{:S(2)}) collective-permute-start(f32[1280,128]{1,0:T(8,128)S(1)} %bitcast.7), channel_id=1, source_target_pairs={{0,64},{1,65},{2,66},{3,67},{4,68},{5,69},{6,70},{7,71},{8,72},{9,... | collective-permute-start | bytes 1966088 | tf_op jit(solution)/shard_map/ppermute | solution.py:27
  6.3 24.0 %copy-start.2 = (f32[1,16,128,128]{3,2,1,0:T(8,128)S(1)}, f32[1,16,128,128]{3,2,1,0:T(8,128)}, u32[]{:S(2)}) copy-start(f32[1,16,128,128]{3,2,1,0:T(8,128)} %inc.3) | copy-start | bytes 3145732
  6.3 24.0 %collective-permute-start = (f32[112,128]{1,0:T(8,128)}, f32[112,128]{1,0:T(8,128)S(1)}, u32[]{:S(2)}, u32[]{:S(2)}) collective-permute-start(f32[112,128]{1,0:T(8,128)} %get-tuple-element.8), channel_id=1, source_target_pairs={{0,1},{1,2},{2,3},{3,4},{4,5},{5,6},{6,7},{7,8},{8,9},{9,10},{10,1... | collective-permute-start | bytes 172040 | tf_op jit(solution)/shard_map/ppermute | solution.py:27
  8.3 21.9 %collective-permute-start.1 = (f32[112,128]{1,0:T(8,128)}, f32[112,128]{1,0:T(8,128)S(1)}, u32[]{:S(2)}, u32[]{:S(2)}) collective-permute-start(f32[112,128]{1,0:T(8,128)} %get-tuple-element.9), channel_id=1, source_target_pairs={{0,63},{1,0},{2,1},{3,2},{4,3},{5,4},{6,5},{7,6},{8,7},{9,8},{10,9... | collective-permute-start | bytes 172040 | tf_op jit(solution)/shard_map/ppermute | solution.py:27
  20.0 36.7 %collective-permute-start.4 = (f32[1080,128]{1,0:T(8,128)S(1)}, f32[1080,128]{1,0:T(8,128)S(1)}, u32[]{:S(2)}, u32[]{:S(2)}) collective-permute-start(f32[1080,128]{1,0:T(8,128)S(1)} %slice.12), channel_id=1, source_target_pairs={{64,0},{65,1},{66,2},{67,3},{68,4},{69,5},{70,6},{71,7},{72,8},{73... | collective-permute-start | bytes 1658888 | tf_op jit(solution)/shard_map/ppermute | solution.py:27
  30.3 6.2 %copy-start.6 = (f32[128,128]{1,0:T(8,128)S(1)}, f32[128,128]{1,0:T(8,128)}, u32[]{:S(2)}) copy-start(f32[128,128]{1,0:T(8,128)} %std.1) | copy-start | bytes 196612
  30.3 6.2 %copy-start.7 = (f32[128,128]{1,0:T(8,128)S(1)}, f32[128,128]{1,0:T(8,128)}, u32[]{:S(2)}) copy-start(f32[128,128]{1,0:T(8,128)} %kappa.1) | copy-start | bytes 196612
  30.4 26.4 %collective-permute-start.5 = (f32[1032,128]{1,0:T(8,128)S(1)}, f32[1032,128]{1,0:T(8,128)S(1)}, u32[]{:S(2)}, u32[]{:S(2)}) collective-permute-start(f32[1032,128]{1,0:T(8,128)S(1)} %get-tuple-element.12), channel_id=1, source_target_pairs={{64,0},{65,1},{66,2},{67,3},{68,4},{69,5},{70,6},{71,7},{72,8},{73... | collective-permute-start | bytes 1585160 | tf_op jit(solution)/shard_map/ppermute | solution.py:27
  32.3 22.4 %collective-permute-start.3 = (f32[832,128]{1,0:T(8,128)S(1)}, f32[832,128]{1,0:T(8,128)S(1)}, u32[]{:S(2)}, u32[]{:S(2)}) collective-permute-start(f32[832,128]{1,0:T(8,128)S(1)} %get-tuple-element.10), channel_id=1, source_target_pairs={{0,64},{1,65},{2,66},{3,67},{4,68},{5,69},{6,70},{7,71},{8,72},{9,... | collective-permute-start | bytes 1277960 | tf_op jit(solution)/shard_map/ppermute | solution.py:27
  36.5 18.2 %copy-start.3 = (f32[128,128]{1,0:T(8,128)S(1)}, f32[128,128]{1,0:T(8,128)}, u32[]{:S(2)}) copy-start(f32[128,128]{1,0:T(8,128)} %weight.2) | copy-start | bytes 196612
  36.5 18.2 %copy-start.4 = (s32[128,128]{1,0:T(8,128)S(1)}, s32[128,128]{1,0:T(8,128)}, u32[]{:S(2)}) copy-start(s32[128,128]{1,0:T(8,128)} %up.3) | copy-start | bytes 196612
  36.5 18.2 %copy-start.5 = (s32[128,128]{1,0:T(8,128)S(1)}, s32[128,128]{1,0:T(8,128)}, u32[]{:S(2)}) copy-start(s32[128,128]{1,0:T(8,128)} %lev.3) | copy-start | bytes 196612

commit v3 on v2

--- a/solution.py
+++ b/solution.py
@@ -11,7 +11,7 @@
 REACH = 2
 PAD = 8
 EARLY = 1080
-LEAD = 1280
+LEAD = 1536
 VMEM_LIMIT = 40 * 1024 * 1024
 VMEM_WHOLE = 60 * 1024 * 1024
 
@@ -357,11 +357,9 @@
     power = jnp.dot(vertical_inverse, vertical_inverse, **exact)
     power = jnp.dot(power, power, **exact)
     base = covar(multipliers, increments, std_dev, diffusivity, before, after, power)
-    primal = primal_final(base, inc_first, inc_rest, *columns)
-    weight, primal = lax.optimization_barrier((departure_weight, primal))
-    dual = dual_final(
-        multipliers, mul_first, mul_rest, before, after, weight, upstream, level_offset
-    )
+    dual = dual_final(multipliers, mul_first, mul_rest, before, after, *columns)
+    weight, dual = lax.optimization_barrier((departure_weight, dual))
+    primal = primal_final(base, inc_first, inc_rest, weight, upstream, level_offset)
     return (primal, dual)
 
 

time: 59.5 us -> 57 us (0.958)
  waiting for transfers between devices: 15.8 us -> 13.4 us
    ppermute x6, waiting for transfers between devices: 15.8 us -> 13.4 us  [moved(): return lax.ppermute(value, ('win', 'tile'), pairs)]
  transfers between devices with their start and end apart: 6 -> 6, of which waited for: 2 -> 3; matrix products, arithmetic and copies ran while one was open for 1% -> 1% of each run, Pallas kernels for 21% -> 22%
where the time goes in v3:
time: 57 us; the launch traced here: 56.7 us
  starting transfers between devices  26.4 us (46%)
  Pallas kernels  14.5 us (25%)
  waiting for transfers between devices  13.4 us (24%)
  local copies, waits for them, and re-layouts  1.29 us (2%)
  between operations  0.79 us (1%)
    ppermute x6, starting transfers between devices, moved(): return lax.ppermute(value, ('win', 'tile'), pairs)  26.4 us
    ppermute x6, waiting for transfers between devices, moved(): return lax.ppermute(value, ('win', 'tile'), pairs)  13.4 us
    pallas_call x1, Pallas kernels, covar(): pl.pallas_call(covar_kernel, in_specs=[vmem] * 6 + [pl.BlockSpec(memory_s...  8.45 us
    pallas_call x1, Pallas kernels, dual_final(): pl.pallas_call(dual_kernel, in_specs=[vmem] * 8, out_specs=vmem, out_shap...  2.36 us
    pallas_call x1, Pallas kernels, primal_final(): pl.pallas_call(primal_kernel, in_specs=[vmem] * 6, out_specs=vmem, out_sh...  1.91 us
    pallas_call x1, Pallas kernels, pack(): pl.pallas_call(functools.partial(pack_both, levels), grid=(1,), in_specs=...  1.73 us
    slice x1, local copies, waits for them, and re-layouts, per_device(): inc_first = moved(inc_rows[:inc_early], 1, 0)  1.19 us
  transfers between devices with their start and end apart: 6, of which 3 were waited for; matrix products, arithmetic and copies ran while one was open for 1% of the time, Pallas kernels for 22%

profile of v3, /device:TPU:52, one launch (start us, length us, event | category | flops | bytes accessed | tf_op | source)
XLA Modules:
  0.0 56.7 jit_solution(5271823040383011450)
XLA Ops:
  0.6 0.0 copy-start
  0.6 1.2 %slice.9 = f32[1,12,128,128]{3,2,1,0:T(8,128)S(1)} slice(f32[1,16,128,128]{3,2,1,0:T(8,128)} %inc.3), slice={[0:1], [0:12], [0:128], [0:128]} | slice | bytes 1572864 | tf_op jit(solution)/shard_map/slice | solution.py:345
  1.8 0.0 copy-start.1
  1.9 2.7 %collective-permute-start.2 = (f32[1536,128]{1,0:T(8,128)S(1)}, f32[1536,128]{1,0:T(8,128)S(1)}, u32[]{:S(2)}, u32[]{:S(2)}) collective-permute-start(f32[1536,128]{1,0:T(8,128)S(1)} %bitcast.7), channel_id=1, source_target_pairs={{0,64},{1,65},{2,66},{3,67},{4,68},{5,69},{6,70},{7,71},{8,72},{9,... | collective-permute-start | bytes 2359304 | tf_op jit(solution)/shard_map/ppermute | solution.py:27
  4.6 1.7 %shard_map.95 = (f32[112,128]{1,0:T(8,128)}, f32[112,128]{1,0:T(8,128)}) custom-call(f32[1,16,128,128]{3,2,1,0:T(8,128)} %inc.3, f32[1,16,128,128]{3,2,1,0:T(8,128)} %mul.5, f32[128,128]{1,0:T(8,128)} %std.1, f32[128,128]{1,0:T(8,128)} %kappa.1, f32[128,128]{1,0:T(8,128)} %weight.2, s32[128,128]{1,0:T(8,128)} %up.3, s32[128,128]{1,0:T(8,128)} %lev.3, ...), custom_call_target="tpu_custom_call" | custom-call | flops 1000 | bytes 1000 | tf_op jit(solution)/shard_map/pallas_call | solution.py:88
  6.3 0.0 copy-start.2
  6.3 2.0 %collective-permute-start = (f32[112,128]{1,0:T(8,128)}, f32[112,128]{1,0:T(8,128)S(1)}, u32[]{:S(2)}, u32[]{:S(2)}) collective-permute-start(f32[112,128]{1,0:T(8,128)} %get-tuple-element.8), channel_id=1, source_target_pairs={{0,1},{1,2},{2,3},{3,4},{4,5},{5,6},{6,7},{7,8},{8,9},{9,10},{10,1... | collective-permute-start | bytes 172040 | tf_op jit(solution)/shard_map/ppermute | solution.py:27
  8.4 11.7 %collective-permute-start.1 = (f32[112,128]{1,0:T(8,128)}, f32[112,128]{1,0:T(8,128)S(1)}, u32[]{:S(2)}, u32[]{:S(2)}) collective-permute-start(f32[112,128]{1,0:T(8,128)} %get-tuple-element.9), channel_id=1, source_target_pairs={{0,63},{1,0},{2,1},{3,2},{4,3},{5,4},{6,5},{7,6},{8,7},{9,8},{10,9... | collective-permute-start | bytes 172040 | tf_op jit(solution)/shard_map/ppermute | solution.py:27
  20.0 0.0 copy-done.1
  20.1 4.2 %collective-permute-start.4 = (f32[1080,128]{1,0:T(8,128)S(1)}, f32[1080,128]{1,0:T(8,128)S(1)}, u32[]{:S(2)}, u32[]{:S(2)}) collective-permute-start(f32[1080,128]{1,0:T(8,128)S(1)} %slice.12), channel_id=1, source_target_pairs={{64,0},{65,1},{66,2},{67,3},{68,4},{69,5},{70,6},{71,7},{72,8},{73... | collective-permute-start | bytes 1658888 | tf_op jit(solution)/shard_map/ppermute | solution.py:27
  24.3 8.8 %collective-permute-done.before = f32[112,128]{1,0:T(8,128)S(1)} collective-permute-done((f32[112,128]{1,0:T(8,128)}, f32[112,128]{1,0:T(8,128)S(1)}, u32[]{:S(2)}, u32[]{:S(2)}) %collective-permute-start) | collective-permute-done | bytes 57376 | tf_op jit(solution)/shard_map/ppermute | solution.py:27
  33.1 0.0 collective-permute-done.1.after
  33.1 0.0 copy-done.2
  33.1 0.0 copy-start.6
  33.1 0.0 copy-start.7
  33.1 0.1 shard_map.97
  33.2 1.9 %collective-permute-start.5 = (f32[1032,128]{1,0:T(8,128)S(1)}, f32[1032,128]{1,0:T(8,128)S(1)}, u32[]{:S(2)}, u32[]{:S(2)}) collective-permute-start(f32[1032,128]{1,0:T(8,128)S(1)} %get-tuple-element.11), channel_id=1, source_target_pairs={{64,0},{65,1},{66,2},{67,3},{68,4},{69,5},{70,6},{71,7},{72,8},{73... | collective-permute-start | bytes 1585160 | tf_op jit(solution)/shard_map/ppermute | solution.py:27
  35.1 3.9 %collective-permute-start.3 = (f32[576,128]{1,0:T(8,128)S(1)}, f32[576,128]{1,0:T(8,128)S(1)}, u32[]{:S(2)}, u32[]{:S(2)}) collective-permute-start(f32[576,128]{1,0:T(8,128)S(1)} %get-tuple-element.10), channel_id=1, source_target_pairs={{0,64},{1,65},{2,66},{3,67},{4,68},{5,69},{6,70},{7,71},{8,72},{9,... | collective-permute-start | bytes 884744 | tf_op jit(solution)/shard_map/ppermute | solution.py:27
  39.1 0.0 copy-done
  39.1 0.1 fusion
  39.2 0.1 fusion.1.power
  39.3 0.0 copy-done.6
  39.3 0.0 copy-done.7
  39.4 0.0 copy-start.3
  39.4 0.0 copy-start.4
  39.4 0.0 copy-start.5
  39.4 8.4 %shard_map.96.base = f32[16,128,128]{2,1,0:T(8,128)S(1)} custom-call(f32[1,16,128,128]{3,2,1,0:T(8,128)S(1)} %copy-done.1, f32[1,16,128,128]{3,2,1,0:T(8,128)S(1)} %copy-done.2, f32[128,128]{1,0:T(8,128)S(1)} %copy-done.6, f32[128,128]{1,0:T(8,128)S(1)} %copy-done.7, f32[112,128]{1,0:T(8,128)S(1)} %collective-permute-done.before, ...), custom_call_target="tpu_custom_call" | custom-call | flops 1000 | bytes 1000 | tf_op jit(solution)/shard_map/pallas_call | solution.py:183
  47.8 0.0 collective-permute-done.4.came_first
  47.9 2.2 %collective-permute-done.5.came = f32[1032,128]{1,0:T(8,128)S(1)} collective-permute-done((f32[1032,128]{1,0:T(8,128)S(1)}, f32[1032,128]{1,0:T(8,128)S(1)}, u32[]{:S(2)}, u32[]{:S(2)}) %collective-permute-start.5) | collective-permute-done | bytes 528416 | tf_op jit(solution)/shard_map/ppermute | solution.py:27
  50.0 0.0 copy-done.3
  50.0 0.0 copy-done.4
  50.1 0.0 copy-done.5
  50.1 2.4 %shard_map.98 = f32[1,16,128,128]{3,2,1,0:T(8,128)} custom-call(f32[1,16,128,128]{3,2,1,0:T(8,128)S(1)} %copy-done.1, f32[1080,128]{1,0:T(8,128)S(1)} %collective-permute-done.4.came_first, f32[1032,128]{1,0:T(8,128)S(1)} %collective-permute-done.5.came, f32[112,128]{1,0:T(8,128)S(1)} %collective-permute-done.before, ...), custom_call_target="tpu_custom_call" | custom-call | flops 1000 | bytes 1000 | tf_op jit(solution)/shard_map/pallas_call | solution.py:315
  52.4 2.4 %collective-permute-done.3.came = f32[576,128]{1,0:T(8,128)S(1)} collective-permute-done((f32[576,128]{1,0:T(8,128)S(1)}, f32[576,128]{1,0:T(8,128)S(1)}, u32[]{:S(2)}, u32[]{:S(2)}) %collective-permute-start.3) | collective-permute-done | bytes 294944 | tf_op jit(solution)/shard_map/ppermute | solution.py:27
  54.8 0.0 collective-permute-done.2.came_first
  54.8 1.9 %shard_map.99 = f32[1,16,128,128]{3,2,1,0:T(8,128)} custom-call(f32[16,128,128]{2,1,0:T(8,128)S(1)} %shard_map.96.base, f32[1536,128]{1,0:T(8,128)S(1)} %collective-permute-done.2.came_first, f32[576,128]{1,0:T(8,128)S(1)} %collective-permute-done.3.came, f32[128,128]{1,0:T(8,128)S(1)} %copy-done.3, s32[128,128]{1,0:T(8,128)S(1)} %copy-done.4, ...), custom_call_target="tpu_custom_call" | custom-call | flops 1000 | bytes 1000 | tf_op jit(solution)/shard_map/pallas_call | solution.py:252
  (1 shorter events, 0.0 us)
Async XLA Ops:
  0.6 38.4 %copy-start = (f32[16,16]{1,0:T(8,128)S(1)}, f32[16,16]{1,0:T(8,128)}, u32[]{:S(2)}) copy-start(f32[16,16]{1,0:T(8,128)} %param.15) | copy-start | bytes 3076
  1.8 18.2 %copy-start.1 = (f32[1,16,128,128]{3,2,1,0:T(8,128)S(1)}, f32[1,16,128,128]{3,2,1,0:T(8,128)}, u32[]{:S(2)}) copy-start(f32[1,16,128,128]{3,2,1,0:T(8,128)} %mul.5) | copy-start | bytes 3145732
  1.9 52.9 %collective-permute-start.2 = (f32[1536,128]{1,0:T(8,128)S(1)}, f32[1536,128]{1,0:T(8,128)S(1)}, u32[]{:S(2)}, u32[]{:S(2)}) collective-permute-start(f32[1536,128]{1,0:T(8,128)S(1)} %bitcast.7), channel_id=1, source_target_pairs={{0,64},{1,65},{2,66},{3,67},{4,68},{5,69},{6,70},{7,71},{8,72},{9,... | collective-permute-start | bytes 2359304 | tf_op jit(solution)/shard_map/ppermute | solution.py:27
  6.3 26.8 %copy-start.2 = (f32[1,16,128,128]{3,2,1,0:T(8,128)S(1)}, f32[1,16,128,128]{3,2,1,0:T(8,128)}, u32[]{:S(2)}) copy-start(f32[1,16,128,128]{3,2,1,0:T(8,128)} %inc.3) | copy-start | bytes 3145732
  6.3 26.8 %collective-permute-start = (f32[112,128]{1,0:T(8,128)}, f32[112,128]{1,0:T(8,128)S(1)}, u32[]{:S(2)}, u32[]{:S(2)}) collective-permute-start(f32[112,128]{1,0:T(8,128)} %get-tuple-element.8), channel_id=1, source_target_pairs={{0,1},{1,2},{2,3},{3,4},{4,5},{5,6},{6,7},{7,8},{8,9},{9,10},{10,1... | collective-permute-start | bytes 172040 | tf_op jit(solution)/shard_map/ppermute | solution.py:27
  8.4 24.8 %collective-permute-start.1 = (f32[112,128]{1,0:T(8,128)}, f32[112,128]{1,0:T(8,128)S(1)}, u32[]{:S(2)}, u32[]{:S(2)}) collective-permute-start(f32[112,128]{1,0:T(8,128)} %get-tuple-element.9), channel_id=1, source_target_pairs={{0,63},{1,0},{2,1},{3,2},{4,3},{5,4},{6,5},{7,6},{8,7},{9,8},{10,9... | collective-permute-start | bytes 172040 | tf_op jit(solution)/shard_map/ppermute | solution.py:27
  20.1 27.7 %collective-permute-start.4 = (f32[1080,128]{1,0:T(8,128)S(1)}, f32[1080,128]{1,0:T(8,128)S(1)}, u32[]{:S(2)}, u32[]{:S(2)}) collective-permute-start(f32[1080,128]{1,0:T(8,128)S(1)} %slice.12), channel_id=1, source_target_pairs={{64,0},{65,1},{66,2},{67,3},{68,4},{69,5},{70,6},{71,7},{72,8},{73... | collective-permute-start | bytes 1658888 | tf_op jit(solution)/shard_map/ppermute | solution.py:27
  33.1 6.2 %copy-start.6 = (f32[128,128]{1,0:T(8,128)S(1)}, f32[128,128]{1,0:T(8,128)}, u32[]{:S(2)}) copy-start(f32[128,128]{1,0:T(8,128)} %std.1) | copy-start | bytes 196612
  33.1 6.2 %copy-start.7 = (f32[128,128]{1,0:T(8,128)S(1)}, f32[128,128]{1,0:T(8,128)}, u32[]{:S(2)}) copy-start(f32[128,128]{1,0:T(8,128)} %kappa.1) | copy-start | bytes 196612
  33.2 16.8 %collective-permute-start.5 = (f32[1032,128]{1,0:T(8,128)S(1)}, f32[1032,128]{1,0:T(8,128)S(1)}, u32[]{:S(2)}, u32[]{:S(2)}) collective-permute-start(f32[1032,128]{1,0:T(8,128)S(1)} %get-tuple-element.11), channel_id=1, source_target_pairs={{64,0},{65,1},{66,2},{67,3},{68,4},{69,5},{70,6},{71,7},{72,8},{73... | collective-permute-start | bytes 1585160 | tf_op jit(solution)/shard_map/ppermute | solution.py:27
  35.1 19.6 %collective-permute-start.3 = (f32[576,128]{1,0:T(8,128)S(1)}, f32[576,128]{1,0:T(8,128)S(1)}, u32[]{:S(2)}, u32[]{:S(2)}) collective-permute-start(f32[576,128]{1,0:T(8,128)S(1)} %get-tuple-element.10), channel_id=1, source_target_pairs={{0,64},{1,65},{2,66},{3,67},{4,68},{5,69},{6,70},{7,71},{8,72},{9,... | collective-permute-start | bytes 884744 | tf_op jit(solution)/shard_map/ppermute | solution.py:27
  39.4 10.7 %copy-start.3 = (f32[128,128]{1,0:T(8,128)S(1)}, f32[128,128]{1,0:T(8,128)}, u32[]{:S(2)}) copy-start(f32[128,128]{1,0:T(8,128)} %weight.2) | copy-start | bytes 196612
  39.4 10.7 %copy-start.4 = (s32[128,128]{1,0:T(8,128)S(1)}, s32[128,128]{1,0:T(8,128)}, u32[]{:S(2)}) copy-start(s32[128,128]{1,0:T(8,128)} %up.3) | copy-start | bytes 196612
  39.4 10.7 %copy-start.5 = (s32[128,128]{1,0:T(8,128)S(1)}, s32[128,128]{1,0:T(8,128)}, u32[]{:S(2)}) copy-start(s32[128,128]{1,0:T(8,128)} %lev.3) | copy-start | bytes 196612

commit v4 on v3

--- a/solution.py
+++ b/solution.py
@@ -10,21 +10,33 @@
 SWEEPS = 4
 REACH = 2
 PAD = 8
-EARLY = 1080
-LEAD = 1536
+NEAR = 1408
+FAR = 1088
+GROUPS = 4
 VMEM_LIMIT = 40 * 1024 * 1024
 VMEM_WHOLE = 60 * 1024 * 1024
 
 
-def moved(value, win_by, tile_by):
-    wins, tiles = lax.axis_size("win"), lax.axis_size("tile")
-    pairs = [
-        (k * tiles + t, (k + win_by) * tiles + (t + tile_by) % tiles)
-        for k in range(wins)
-        for t in range(tiles)
-        if 0 <= k + win_by < wins
-    ]
-    return lax.ppermute(value, ("win", "tile"), pairs)
+def shift_tile(value, by):
+    tiles = lax.axis_size("tile")
+    return lax.ppermute(value, "tile", [(t, (t + by) % tiles) for t in range(tiles)])
+
+
+def swap_in_pair(value):
+    wins = lax.axis_size("win")
+    return lax.ppermute(value, "win", [(k, k ^ 1) for k in range(wins)])
+
+
+def across_pairs(value):
+    wins = lax.axis_size("win")
+    pairs = [(k, k - 1 if k % 2 == 0 else k + 1) for k in range(1, wins - 1)]
+    return lax.ppermute(value, "win", pairs)
+
+
+def on_even(body_even, body_odd):
+    odd = lax.rem(lax.axis_index("win"), 2)
+    pl.when(odd == 0)(body_even)
+    pl.when(odd == 1)(body_odd)
 
 
 def params():
@@ -96,34 +108,74 @@
     )(*(arrays * 2))
 
 
-def forward_kernel(inc_early, mul_early, inc, mul, before, after, inc_out, mul_out):
+def pick_kernel(even_source, odd_source, out, sems):
+    size = out.shape[0] // GROUPS
+
+    def copy(source):
+        parts = [pl.ds(g * size, size) for g in range(GROUPS)]
+        copies = [
+            pltpu.make_async_copy(source.at[part], out.at[part], sems.at[g])
+            for g, part in enumerate(parts)
+        ]
+        for moving in copies:
+            moving.start()
+        for moving in copies:
+            moving.wait()
+
+    on_even(lambda: copy(even_source), lambda: copy(odd_source))
+
+
+def pick(even_source, odd_source, count):
+    return pl.pallas_call(
+        pick_kernel,
+        in_specs=[pl.BlockSpec(memory_space=pl.ANY)] * 2,
+        out_specs=pl.BlockSpec(memory_space=pltpu.VMEM),
+        out_shape=jax.ShapeDtypeStruct((count, even_source.shape[1]), jnp.float32),
+        scratch_shapes=[pltpu.SemaphoreType.DMA((GROUPS,))],
+        compiler_params=pltpu.CompilerParams(vmem_limit_bytes=VMEM_WHOLE),
+        cost_estimate=cost(1000, 1000),
+    )(even_source, odd_source)
+
+
+def forward_kernel(near_early, far_early, inc, mul, before, after, near_out, far_out):
     _, levels, width, rows = mul.shape
     spot = Rows(levels)
     half = REACH * levels
-    for early, source, target in ((inc_early, inc, inc_out), (mul_early, mul, mul_out)):
+
+    def copy(early, source, target):
         base = levels * width - early
         for l in range(levels):
             start = max(early - l * width, 0)
             if start < width:
                 part = slice(l * width + start - early, (l + 1) * width - early)
                 target[part] = source[0, l, start:]
-            near = slice(base + REACH * l, base + REACH * (l + 1))
-            far = slice(near.start + half, near.stop + half)
+            left = slice(base + REACH * l, base + REACH * (l + 1))
+            right = slice(left.start + half, left.stop + half)
             if source is inc:
-                target[near] = before[spot.inc(l)]
-                target[far] = after[spot.inc(l)]
+                target[left] = before[spot.inc(l)]
+                target[right] = after[spot.inc(l)]
             else:
                 first, last = before[spot.mul(l)], after[spot.mul(l)]
-                target[near] = first[SWEEPS - REACH :]
-                target[far] = last[:REACH]
-
-
-def forward(inc_early, mul_early, inc, mul, before, after):
+                target[left] = first[SWEEPS - REACH :]
+                target[right] = last[:REACH]
+
+    def even():
+        copy(near_early, inc, near_out)
+        copy(far_early, mul, far_out)
+
+    def odd():
+        copy(near_early, mul, near_out)
+        copy(far_early, inc, far_out)
+
+    on_even(even, odd)
+
+
+def forward(near_early, far_early, inc, mul, before, after):
     _, levels, width, rows = mul.shape
     vmem = pl.BlockSpec(memory_space=pltpu.VMEM)
-    heights = [levels * width - early + 2 * REACH * levels for early in (inc_early, mul_early)]
+    heights = [levels * width - early + 2 * REACH * levels for early in (near_early, far_early)]
     return pl.pallas_call(
-        functools.partial(forward_kernel, inc_early, mul_early),
+        functools.partial(forward_kernel, near_early, far_early),
         in_specs=[vmem] * 4,
         out_specs=[vmem] * 2,
         out_shape=[jax.ShapeDtypeStruct((h, rows), jnp.float32) for h in heights],
@@ -195,10 +247,13 @@
     )(mul, inc, std, kappa, before, after, power)
 
 
-def fill_field(field, offset, width, *pieces):
-    levels = field.shape[0] - 2 * offset
+def fill_field(field, width, *pieces):
+    levels = field.shape[0] - 2
     rest, half = pieces[-1], REACH * levels
     base = rest.shape[0] - 2 * half
+    zero = jnp.zeros_like(field[0])
+    field[0] = zero
+    field[levels + 1] = zero
     start = 0
     for piece in pieces:
         stop = start + (base if piece is rest else piece.shape[0])
@@ -206,91 +261,80 @@
             begin, end = max(l * width, start), min((l + 1) * width, stop)
             if begin < end:
                 part = slice(PAD + begin - l * width, PAD + end - l * width)
-                field[l + offset, part] = piece[begin - start : end - start]
+                field[l + 1, part] = piece[begin - start : end - start]
         start = stop
     for l in range(levels):
         near = slice(base + REACH * l, base + REACH * (l + 1))
-        field[l + offset, PAD - REACH : PAD] = rest[near]
+        field[l + 1, :PAD] = zero[:PAD]
+        field[l + 1, PAD + width :] = zero[:PAD]
+        field[l + 1, PAD - REACH : PAD] = rest[near]
         far = rest[near.start + half : near.stop + half]
-        field[l + offset, PAD + width : PAD + width + REACH] = far
-
-
-def primal_kernel(base, came_first, came, weight, up, lev, out, field, level_field):
+        field[l + 1, PAD + width : PAD + width + REACH] = far
+
+
+def in_groups(levels, body, staged, out, sems):
+    size = levels // GROUPS
+    copies = []
+    for g in range(GROUPS):
+        lax.fori_loop(g * size, (g + 1) * size, lambda l, carry: body(l) or carry, 0)
+        part = pl.ds(g * size, size)
+        copy = pltpu.make_async_copy(staged.at[part], out.at[0, part], sems.at[g])
+        copy.start()
+        copies.append(copy)
+    for copy in copies:
+        copy.wait()
+
+
+def primal_levels(base, weight, up, lev, field, level_field, staged, out, sems):
     levels, width, rows = base.shape
-    fill_field(field, 0, width, came_first, came)
     zero = jnp.zeros((width, rows), jnp.float32)
     level_field[0] = zero
     level_field[levels + 1] = zero
 
     def one_level(l, carry):
         step = up[...]
-        total = field[l, PAD : PAD + width]
+        total = field[l + 1, PAD : PAD + width]
         for j in (-2, -1, 1, 2):
-            total = jnp.where(step == j, field[l, PAD + j : PAD + j + width], total)
+            total = jnp.where(step == j, field[l + 1, PAD + j : PAD + j + width], total)
         level_field[l + 1] = total
         return carry
 
     lax.fori_loop(0, levels, one_level, 0)
 
-    def combine(l, carry):
+    def combine(l):
         pick = lev[...]
         departed = jnp.where(
             pick == 0,
             level_field[l + 1],
             jnp.where(pick == 1, level_field[l + 2], level_field[l]),
         )
-        center = field[l, PAD : PAD + width]
-        out[0, l] = base[l] - ((1.0 - weight[...]) * center + weight[...] * departed)
-        return carry
-
-    lax.fori_loop(0, levels, combine, 0)
-
-
-def primal_final(base, came_first, came, weight, up, lev):
-    levels, width, rows = base.shape
-    vmem = pl.BlockSpec(memory_space=pltpu.VMEM)
-    return pl.pallas_call(
-        primal_kernel,
-        in_specs=[vmem] * 6,
-        out_specs=vmem,
-        out_shape=jax.ShapeDtypeStruct((1, levels, width, rows), jnp.float32),
-        scratch_shapes=[
-            pltpu.VMEM((levels, width + 2 * PAD, rows), jnp.float32),
-            pltpu.VMEM((levels + 2, width, rows), jnp.float32),
-        ],
-        compiler_params=params(),
-        cost_estimate=cost(1000, 1000),
-    )(base, came_first, came, weight, up, lev)
-
-
-def dual_kernel(
-    mul, came_first, came, before, after, weight, up, lev, out, field, weight_ext, up_ext, lev_ext
+        center = field[l + 1, PAD : PAD + width]
+        staged[l] = base[l] - ((1.0 - weight[...]) * center + weight[...] * departed)
+
+    in_groups(levels, combine, staged, out, sems)
+
+
+def dual_levels(
+    mul, before, after, weight, up, lev, field, weight_ext, up_ext, lev_ext, staged, out, sems
 ):
     _, levels, width, rows = mul.shape
     tall = width + 2 * PAD
     spot = Rows(levels)
-    left, right = slice(PAD - REACH, PAD), slice(PAD + width, PAD + width + REACH)
     weight_ext[...] = jnp.zeros_like(weight_ext)
     up_ext[...] = jnp.zeros_like(up_ext)
     lev_ext[...] = jnp.zeros_like(lev_ext)
     weight_ext[PAD : PAD + width] = weight[...]
     up_ext[PAD : PAD + width] = up[...]
     lev_ext[PAD : PAD + width] = lev[...]
-    zero = jnp.zeros((tall, rows), jnp.float32)
-    field[0] = zero
-    field[levels + 1] = zero
+    left, right = slice(PAD - REACH, PAD), slice(PAD + width, PAD + width + REACH)
     for side, part in ((before, left), (after, right)):
         weight_ext[part] = side[spot.weight]
         code = side[spot.code]
         step = jnp.floor((code + 1.5) * (1.0 / 3.0))
         up_ext[part] = step.astype(jnp.int32)
         lev_ext[part] = (code - 3.0 * step).astype(jnp.int32)
-    for l in range(levels):
-        field[l + 1, :PAD] = zero[:PAD]
-        field[l + 1, PAD + width :] = zero[:PAD]
-    fill_field(field, 1, width, came_first, came)
-
-    def one_level(l, carry):
+
+    def one_level(l):
         pick = lev_ext[...]
         lifted = jnp.where(
             pick == 0, field[l + 1], jnp.where(pick == 1, field[l], field[l + 2])
@@ -302,30 +346,55 @@
             total = total + pltpu.roll(jnp.where(step == j, source, 0.0), j % tall, 0)
         returned = total[PAD : PAD + width]
         center = field[l + 1, PAD : PAD + width]
-        out[0, l] = mul[0, l] - ((1.0 - weight[...]) * center + returned)
-        return carry
-
-    lax.fori_loop(0, levels, one_level, 0)
-
-
-def dual_final(mul, came_first, came, before, after, weight, up, lev):
+        staged[l] = mul[0, l] - ((1.0 - weight[...]) * center + returned)
+
+    in_groups(levels, one_level, staged, out, sems)
+
+
+def final_kernel(primal_on_even, last, base, mul, first, rest, before, after, weight, up, lev, *refs):
+    if last:
+        refs = refs[2:]
+    primal, dual, field, level_field, weight_ext, up_ext, lev_ext, staged, sems = refs
+    fill_field(field, mul.shape[2], first, rest)
+
+    def make_primal():
+        primal_levels(base, weight, up, lev, field, level_field, staged, primal, sems)
+
+    def make_dual():
+        dual_levels(
+            mul, before, after, weight, up, lev, field, weight_ext, up_ext, lev_ext,
+            staged, dual, sems,
+        )
+
+    if primal_on_even:
+        on_even(make_primal, make_dual)
+    else:
+        on_even(make_dual, make_primal)
+
+
+def final(primal_on_even, base, mul, pieces, before, after, columns, done=()):
     _, levels, width, rows = mul.shape
     vmem = pl.BlockSpec(memory_space=pltpu.VMEM)
+    anywhere = pl.BlockSpec(memory_space=pl.ANY)
     tall = width + 2 * PAD
     return pl.pallas_call(
-        dual_kernel,
-        in_specs=[vmem] * 8,
-        out_specs=vmem,
-        out_shape=jax.ShapeDtypeStruct((1, levels, width, rows), jnp.float32),
+        functools.partial(final_kernel, primal_on_even, bool(done)),
+        in_specs=[vmem] * 9 + [anywhere] * len(done),
+        out_specs=[anywhere] * 2,
+        out_shape=[jax.ShapeDtypeStruct(mul.shape, jnp.float32)] * 2,
+        input_output_aliases={9: 0, 10: 1} if done else {},
         scratch_shapes=[
             pltpu.VMEM((levels + 2, tall, rows), jnp.float32),
+            pltpu.VMEM((levels + 2, width, rows), jnp.float32),
             pltpu.VMEM((tall, rows), jnp.float32),
             pltpu.VMEM((tall, rows), jnp.int32),
             pltpu.VMEM((tall, rows), jnp.int32),
+            pltpu.VMEM((levels, width, rows), jnp.float32),
+            pltpu.SemaphoreType.DMA((GROUPS,)),
         ],
         compiler_params=params(),
         cost_estimate=cost(1000, 1000),
-    )(mul, came_first, came, before, after, weight, up, lev)
+    )(base, mul, *pieces, before, after, *columns, *done)
 
 
 def per_device(
@@ -340,26 +409,25 @@
 ):
     columns = (departure_weight, upstream, level_offset)
     _, levels, width, rows = multipliers.shape
-    inc_early, mul_early = (n * levels * width // 2048 for n in (LEAD, EARLY))
+    near_early, far_early = (n * levels * width // 2048 for n in (NEAR, FAR))
     inc_rows, mul_rows = increments.reshape(-1, rows), multipliers.reshape(-1, rows)
-    inc_first = moved(inc_rows[:inc_early], 1, 0)
-    mul_first = moved(mul_rows[:mul_early], -1, 0)
+    near_first = swap_in_pair(pick(inc_rows, mul_rows, near_early))
+    far_first = across_pairs(pick(mul_rows, inc_rows, far_early))
     to_right, to_left = pack(increments, multipliers, std_dev, diffusivity, *columns)
-    before = moved(to_right, 0, 1)
-    after = moved(to_left, 0, -1)
-    inc_out, mul_out = forward(
-        inc_early, mul_early, increments, multipliers, before, after
-    )
-    inc_rest = moved(inc_out, 1, 0)
-    mul_rest = moved(mul_out, -1, 0)
+    before = shift_tile(to_right, 1)
+    after = shift_tile(to_left, -1)
+    near_out, far_out = forward(near_early, far_early, increments, multipliers, before, after)
+    near_rest = swap_in_pair(near_out)
+    far_rest = across_pairs(far_out)
 
     exact = dict(precision=lax.Precision.HIGHEST, preferred_element_type=jnp.float32)
     power = jnp.dot(vertical_inverse, vertical_inverse, **exact)
     power = jnp.dot(power, power, **exact)
     base = covar(multipliers, increments, std_dev, diffusivity, before, after, power)
-    dual = dual_final(multipliers, mul_first, mul_rest, before, after, *columns)
-    weight, dual = lax.optimization_barrier((departure_weight, dual))
-    primal = primal_final(base, inc_first, inc_rest, weight, upstream, level_offset)
+    done = final(True, base, multipliers, (far_first, far_rest), before, after, columns)
+    primal, dual = final(
+        False, base, multipliers, (near_first, near_rest), before, after, columns, done
+    )
     return (primal, dual)
 
 

time: 57 us -> 57.4 us (level)
  Pallas kernels: 14.5 us -> 18.2 us
  waiting for transfers between devices: 13.4 us -> 11.7 us
  local copies, waits for them, and re-layouts: 1.29 us -> 0.06 us
    pallas_call x3 -> x5, Pallas kernels: 4.33 us -> 7.97 us  [the longest x2 4.06 us: pick(): pl.pallas_call(pick_kernel, in_specs=[pl.BlockSpec(memory_space=pl.ANY)]...]
    ppermute x6, waiting for transfers between devices: 13.4 us -> 11.7 us  [the longest x2 6.64 us: shift_tile(): lax.ppermute(value, 'tile', [(t, (t + by) % tiles) for t in range(tiles)])]
    slice x2 -> x0, local copies, waits for them, and re-layouts: 1.23 us -> none  [the longest x1 1.19 us: per_device(): inc_first = moved(inc_rows[:inc_early], 1, 0)]
  transfers between devices with their start and end apart: 6 -> 6, of which waited for: 3 -> 3; matrix products, arithmetic and copies ran while one was open for 1% -> 0% of each run, Pallas kernels for 22% -> 24%
where the time goes in v4:
time: 57.4 us; the launch traced here: 57 us
  starting transfers between devices  26 us (45%)
  Pallas kernels  18.2 us (32%)
  waiting for transfers between devices  11.7 us (20%)
  between operations  0.81 us (1%)
    ppermute x2, starting transfers between devices, shift_tile(): lax.ppermute(value, 'tile', [(t, (t + by) % tiles) for t in range(tiles)])  13.7 us
    pallas_call x1, Pallas kernels, covar(): pl.pallas_call(covar_kernel, in_specs=[vmem] * 6 + [pl.BlockSpec(memory_s...  8.45 us
    ppermute x2, starting transfers between devices, swap_in_pair(): return lax.ppermute(value, 'win', [(k, k ^ 1) for k in range(wins)])  7.15 us
    ppermute x2, waiting for transfers between devices, shift_tile(): lax.ppermute(value, 'tile', [(t, (t + by) % tiles) for t in range(tiles)])  6.64 us
    ppermute x2, starting transfers between devices, across_pairs(): return lax.ppermute(value, 'win', pairs)  5.15 us
    pallas_call x2, Pallas kernels, pick(): pl.pallas_call(pick_kernel, in_specs=[pl.BlockSpec(memory_space=pl.ANY)]...  4.06 us
    pallas_call x2, Pallas kernels, final(): pl.pallas_call(functools.partial(final_kernel, primal_on_even, bool(done)...  3.82 us
    ppermute x2, waiting for transfers between devices, across_pairs(): return lax.ppermute(value, 'win', pairs)  2.87 us
  transfers between devices with their start and end apart: 6, of which 3 were waited for; matrix products, arithmetic and copies ran while one was open for 0% of the time, Pallas kernels for 24%

profile of v4, /device:TPU:52, one launch (start us, length us, event | category | flops | bytes accessed | tf_op | source)
XLA Modules:
  0.0 57.0 jit_solution(14071907641851684908)
XLA Ops:
  0.6 0.0 copy-start
  0.6 2.1 %shard_map.97 = f32[1408,128]{1,0:T(8,128)} custom-call(f32[2048,128]{1,0:T(8,128)} %bitcast.8, f32[2048,128]{1,0:T(8,128)} %bitcast.6), custom_call_target="tpu_custom_call" | custom-call | flops 1000 | bytes 1000 | tf_op jit(solution)/shard_map/pallas_call | solution.py:129
  2.8 2.6 %collective-permute-start.2 = (f32[1408,128]{1,0:T(8,128)}, f32[1408,128]{1,0:T(8,128)S(1)}, u32[]{:S(2)}, u32[]{:S(2)}) collective-permute-start(f32[1408,128]{1,0:T(8,128)} %shard_map.97), channel_id=1, source_target_pairs={{0,64},{64,0},{128,192},{192,128},{256,320},{320,256},{384,448},{4... | collective-permute-start | bytes 2162696 | tf_op jit(solution)/shard_map/ppermute | solution.py:27
  5.4 1.7 %shard_map.95 = (f32[112,128]{1,0:T(8,128)}, f32[112,128]{1,0:T(8,128)}) custom-call(f32[1,16,128,128]{3,2,1,0:T(8,128)} %inc.3, f32[1,16,128,128]{3,2,1,0:T(8,128)} %mul.7, f32[128,128]{1,0:T(8,128)} %std.1, f32[128,128]{1,0:T(8,128)} %kappa.1, f32[128,128]{1,0:T(8,128)} %weight.3, s32[128,128]{1,0:T(8,128)} %up.3, s32[128,128]{1,0:T(8,128)} %lev.3, ...), custom_call_target="tpu_custom_call" | custom-call | flops 1000 | bytes 1000 | tf_op jit(solution)/shard_map/pallas_call | solution.py:100
  7.1 1.9 %collective-permute-start = (f32[112,128]{1,0:T(8,128)}, f32[112,128]{1,0:T(8,128)S(1)}, u32[]{:S(2)}, u32[]{:S(2)}) collective-permute-start(f32[112,128]{1,0:T(8,128)} %get-tuple-element.8), channel_id=1, source_target_pairs={{0,1},{1,2},{2,3},{3,4},{4,5},{5,6},{6,7},{7,8},{8,9},{9,10},{10,1... | collective-permute-start | bytes 172040 | tf_op jit(solution)/shard_map/ppermute | solution.py:22
  9.0 0.0 copy-start.1
  9.0 0.0 copy-start.2
  9.0 11.8 %collective-permute-start.1 = (f32[112,128]{1,0:T(8,128)}, f32[112,128]{1,0:T(8,128)S(1)}, u32[]{:S(2)}, u32[]{:S(2)}) collective-permute-start(f32[112,128]{1,0:T(8,128)} %get-tuple-element.9), channel_id=1, source_target_pairs={{0,63},{1,0},{2,1},{3,2},{4,3},{5,4},{6,5},{7,6},{8,7},{9,8},{10,9... | collective-permute-start | bytes 172040 | tf_op jit(solution)/shard_map/ppermute | solution.py:22
  20.9 2.0 %shard_map.99 = f32[1088,128]{1,0:T(8,128)} custom-call(f32[2048,128]{1,0:T(8,128)} %bitcast.7, f32[2048,128]{1,0:T(8,128)} %bitcast.9), custom_call_target="tpu_custom_call" | custom-call | flops 1000 | bytes 1000 | tf_op jit(solution)/shard_map/pallas_call | solution.py:129
  22.8 3.2 %collective-permute-start.4 = (f32[1088,128]{1,0:T(8,128)}, f32[1088,128]{1,0:T(8,128)S(1)}, u32[]{:S(2)}, u32[]{:S(2)}) collective-permute-start(f32[1088,128]{1,0:T(8,128)} %shard_map.99), channel_id=1, source_target_pairs={{64,128},{128,64},{192,256},{256,192},{320,384},{384,320},{65,129}... | collective-permute-start | bytes 1671176 | tf_op jit(solution)/shard_map/ppermute | solution.py:33
  26.1 6.6 %collective-permute-done.before = f32[112,128]{1,0:T(8,128)S(1)} collective-permute-done((f32[112,128]{1,0:T(8,128)}, f32[112,128]{1,0:T(8,128)S(1)}, u32[]{:S(2)}, u32[]{:S(2)}) %collective-permute-start) | collective-permute-done | bytes 57376 | tf_op jit(solution)/shard_map/ppermute | solution.py:22
  32.7 0.0 collective-permute-done.1.after
  32.7 0.0 copy-done.1
  32.7 0.0 copy-done.2
  32.7 0.0 copy-start.6
  32.7 0.0 copy-start.7
  32.7 0.1 shard_map.98
  32.8 1.9 %collective-permute-start.5 = (f32[1024,128]{1,0:T(8,128)S(1)}, f32[1024,128]{1,0:T(8,128)S(1)}, u32[]{:S(2)}, u32[]{:S(2)}) collective-permute-start(f32[1024,128]{1,0:T(8,128)S(1)} %get-tuple-element.11), channel_id=1, source_target_pairs={{64,128},{128,64},{192,256},{256,192},{320,384},{384,320},{65,129}... | collective-permute-start | bytes 1572872 | tf_op jit(solution)/shard_map/ppermute | solution.py:33
  34.8 4.6 %collective-permute-start.3 = (f32[704,128]{1,0:T(8,128)S(1)}, f32[704,128]{1,0:T(8,128)S(1)}, u32[]{:S(2)}, u32[]{:S(2)}) collective-permute-start(f32[704,128]{1,0:T(8,128)S(1)} %get-tuple-element.10), channel_id=1, source_target_pairs={{0,64},{64,0},{128,192},{192,128},{256,320},{320,256},{384,448},{4... | collective-permute-start | bytes 1081352 | tf_op jit(solution)/shard_map/ppermute | solution.py:27
  39.3 0.0 copy-done
  39.3 0.1 fusion
  39.5 0.1 fusion.1.power
  39.6 0.0 copy-done.6
  39.6 0.0 copy-done.7
  39.6 0.0 copy-start.3
  39.6 0.0 copy-start.4
  39.6 0.0 copy-start.5
  39.6 8.4 %shard_map.96.base = f32[16,128,128]{2,1,0:T(8,128)S(1)} custom-call(f32[1,16,128,128]{3,2,1,0:T(8,128)S(1)} %copy-done.1, f32[1,16,128,128]{3,2,1,0:T(8,128)S(1)} %copy-done.2, f32[128,128]{1,0:T(8,128)S(1)} %copy-done.6, f32[128,128]{1,0:T(8,128)S(1)} %copy-done.7, f32[112,128]{1,0:T(8,128)S(1)} %collective-permute-done.before, ...), custom_call_target="tpu_custom_call" | custom-call | flops 1000 | bytes 1000 | tf_op jit(solution)/shard_map/pallas_call | solution.py:235
  48.1 0.0 collective-permute-done.4.first
  48.1 2.9 %collective-permute-done.5.rest = f32[1024,128]{1,0:T(8,128)S(1)} collective-permute-done((f32[1024,128]{1,0:T(8,128)S(1)}, f32[1024,128]{1,0:T(8,128)S(1)}, u32[]{:S(2)}, u32[]{:S(2)}) %collective-permute-start.5) | collective-permute-done | bytes 524320 | tf_op jit(solution)/shard_map/ppermute | solution.py:33
  51.0 0.0 copy-done.3
  51.0 0.0 copy-done.4
  51.0 0.0 copy-done.5
  51.0 1.7 %shard_map.100 = (f32[1,16,128,128]{3,2,1,0:T(8,128)}, f32[1,16,128,128]{3,2,1,0:T(8,128)}) custom-call(f32[16,128,128]{2,1,0:T(8,128)S(1)} %shard_map.96.base, f32[1,16,128,128]{3,2,1,0:T(8,128)S(1)} %copy-done.1, f32[1088,128]{1,0:T(8,128)S(1)} %collective-permute-done.4.first, f32[1024,128]{1,0:T(8,128)S(1)} %collective-permute-done.5.rest, ...), custom_call_target="tpu_custom_call" | custom-call | flops 1000 | bytes 1000 | tf_op jit(solution)/shard_map/pallas_call | solution.py:380
  52.7 2.2 %collective-permute-done.3.rest = f32[704,128]{1,0:T(8,128)S(1)} collective-permute-done((f32[704,128]{1,0:T(8,128)S(1)}, f32[704,128]{1,0:T(8,128)S(1)}, u32[]{:S(2)}, u32[]{:S(2)}) %collective-permute-start.3) | collective-permute-done | bytes 360480 | tf_op jit(solution)/shard_map/ppermute | solution.py:27
  54.9 0.0 collective-permute-done.2.first
  54.9 2.1 %shard_map.101 = (f32[1,16,128,128]{3,2,1,0:T(8,128)}, f32[1,16,128,128]{3,2,1,0:T(8,128)}) custom-call(f32[16,128,128]{2,1,0:T(8,128)S(1)} %shard_map.96.base, f32[1,16,128,128]{3,2,1,0:T(8,128)S(1)} %copy-done.1, f32[1408,128]{1,0:T(8,128)S(1)} %collective-permute-done.2.first, ...), custom_call_target="tpu_custom_call", output_to_operand_aliasing={{0}: (9, {}), {1}: (10, {})} | custom-call | flops 1000 | bytes 1000 | tf_op jit(solution)/shard_map/pallas_call | solution.py:380
Async XLA Ops:
  0.6 38.7 %copy-start = (f32[16,16]{1,0:T(8,128)S(1)}, f32[16,16]{1,0:T(8,128)}, u32[]{:S(2)}) copy-start(f32[16,16]{1,0:T(8,128)} %param.15) | copy-start | bytes 3076
  2.8 52.1 %collective-permute-start.2 = (f32[1408,128]{1,0:T(8,128)}, f32[1408,128]{1,0:T(8,128)S(1)}, u32[]{:S(2)}, u32[]{:S(2)}) collective-permute-start(f32[1408,128]{1,0:T(8,128)} %shard_map.97), channel_id=1, source_target_pairs={{0,64},{64,0},{128,192},{192,128},{256,320},{320,256},{384,448},{4... | collective-permute-start | bytes 2162696 | tf_op jit(solution)/shard_map/ppermute | solution.py:27
  7.1 25.6 %collective-permute-start = (f32[112,128]{1,0:T(8,128)}, f32[112,128]{1,0:T(8,128)S(1)}, u32[]{:S(2)}, u32[]{:S(2)}) collective-permute-start(f32[112,128]{1,0:T(8,128)} %get-tuple-element.8), channel_id=1, source_target_pairs={{0,1},{1,2},{2,3},{3,4},{4,5},{5,6},{6,7},{7,8},{8,9},{9,10},{10,1... | collective-permute-start | bytes 172040 | tf_op jit(solution)/shard_map/ppermute | solution.py:22
  9.0 23.7 %copy-start.1 = (f32[1,16,128,128]{3,2,1,0:T(8,128)S(1)}, f32[1,16,128,128]{3,2,1,0:T(8,128)}, u32[]{:S(2)}) copy-start(f32[1,16,128,128]{3,2,1,0:T(8,128)} %mul.7) | copy-start | bytes 3145732
  9.0 23.7 %copy-start.2 = (f32[1,16,128,128]{3,2,1,0:T(8,128)S(1)}, f32[1,16,128,128]{3,2,1,0:T(8,128)}, u32[]{:S(2)}) copy-start(f32[1,16,128,128]{3,2,1,0:T(8,128)} %inc.3) | copy-start | bytes 3145732
  9.0 23.7 %collective-permute-start.1 = (f32[112,128]{1,0:T(8,128)}, f32[112,128]{1,0:T(8,128)S(1)}, u32[]{:S(2)}, u32[]{:S(2)}) collective-permute-start(f32[112,128]{1,0:T(8,128)} %get-tuple-element.9), channel_id=1, source_target_pairs={{0,63},{1,0},{2,1},{3,2},{4,3},{5,4},{6,5},{7,6},{8,7},{9,8},{10,9... | collective-permute-start | bytes 172040 | tf_op jit(solution)/shard_map/ppermute | solution.py:22
  22.8 25.3 %collective-permute-start.4 = (f32[1088,128]{1,0:T(8,128)}, f32[1088,128]{1,0:T(8,128)S(1)}, u32[]{:S(2)}, u32[]{:S(2)}) collective-permute-start(f32[1088,128]{1,0:T(8,128)} %shard_map.99), channel_id=1, source_target_pairs={{64,128},{128,64},{192,256},{256,192},{320,384},{384,320},{65,129}... | collective-permute-start | bytes 1671176 | tf_op jit(solution)/shard_map/ppermute | solution.py:33
  32.7 6.9 %copy-start.6 = (f32[128,128]{1,0:T(8,128)S(1)}, f32[128,128]{1,0:T(8,128)}, u32[]{:S(2)}) copy-start(f32[128,128]{1,0:T(8,128)} %std.1) | copy-start | bytes 196612
  32.7 6.9 %copy-start.7 = (f32[128,128]{1,0:T(8,128)S(1)}, f32[128,128]{1,0:T(8,128)}, u32[]{:S(2)}) copy-start(f32[128,128]{1,0:T(8,128)} %kappa.1) | copy-start | bytes 196612
  32.8 18.1 %collective-permute-start.5 = (f32[1024,128]{1,0:T(8,128)S(1)}, f32[1024,128]{1,0:T(8,128)S(1)}, u32[]{:S(2)}, u32[]{:S(2)}) collective-permute-start(f32[1024,128]{1,0:T(8,128)S(1)} %get-tuple-element.11), channel_id=1, source_target_pairs={{64,128},{128,64},{192,256},{256,192},{320,384},{384,320},{65,129}... | collective-permute-start | bytes 1572872 | tf_op jit(solution)/shard_map/ppermute | solution.py:33
  34.8 20.1 %collective-permute-start.3 = (f32[704,128]{1,0:T(8,128)S(1)}, f32[704,128]{1,0:T(8,128)S(1)}, u32[]{:S(2)}, u32[]{:S(2)}) collective-permute-start(f32[704,128]{1,0:T(8,128)S(1)} %get-tuple-element.10), channel_id=1, source_target_pairs={{0,64},{64,0},{128,192},{192,128},{256,320},{320,256},{384,448},{4... | collective-permute-start | bytes 1081352 | tf_op jit(solution)/shard_map/ppermute | solution.py:27
  39.6 11.4 %copy-start.3 = (f32[128,128]{1,0:T(8,128)S(1)}, f32[128,128]{1,0:T(8,128)}, u32[]{:S(2)}) copy-start(f32[128,128]{1,0:T(8,128)} %weight.3) | copy-start | bytes 196612
  39.6 11.4 %copy-start.4 = (s32[128,128]{1,0:T(8,128)S(1)}, s32[128,128]{1,0:T(8,128)}, u32[]{:S(2)}) copy-start(s32[128,128]{1,0:T(8,128)} %up.3) | copy-start | bytes 196612
  39.6 11.3 %copy-start.5 = (s32[128,128]{1,0:T(8,128)S(1)}, s32[128,128]{1,0:T(8,128)}, u32[]{:S(2)}) copy-start(s32[128,128]{1,0:T(8,128)} %lev.3) | copy-start | bytes 196612

commit v5 on v4

--- a/solution.py
+++ b/solution.py
@@ -411,7 +411,9 @@
     _, levels, width, rows = multipliers.shape
     near_early, far_early = (n * levels * width // 2048 for n in (NEAR, FAR))
     inc_rows, mul_rows = increments.reshape(-1, rows), multipliers.reshape(-1, rows)
-    near_first = swap_in_pair(pick(inc_rows, mul_rows, near_early))
+    even = lax.rem(lax.axis_index("win"), 2) == 0
+    near_part = jnp.where(even, inc_rows[:near_early], mul_rows[:near_early])
+    near_first = swap_in_pair(near_part)
     far_first = across_pairs(pick(mul_rows, inc_rows, far_early))
     to_right, to_left = pack(increments, multipliers, std_dev, diffusivity, *columns)
     before = shift_tile(to_right, 1)

time: 57.4 us -> 56.5 us (0.984)
  Pallas kernels: 18.2 us -> 16.2 us
  other arithmetic: 0 us -> 1.41 us
    pallas_call x2 -> x1, Pallas kernels: 4.06 us -> 2.1 us  [pick(): pl.pallas_call(pick_kernel, in_specs=[pl.BlockSpec(memory_space=pl.ANY)]...]
    select_n x0 -> x1, other arithmetic: none -> 1.41 us  [per_device(): near_part = jnp.where(even, inc_rows[:near_early], mul_rows[:near_early])]
  transfers between devices with their start and end apart: 6 -> 6, of which waited for: 3 -> 3; matrix products, arithmetic and copies ran while one was open for 0% -> 0% of each run, Pallas kernels for 24% -> 25%
where the time goes in v5:
time: 56.5 us; the launch traced here: 56.1 us
  starting transfers between devices  25.9 us (46%)
  Pallas kernels  16.2 us (29%)
  waiting for transfers between devices  11.5 us (20%)
  other arithmetic  1.41 us (2%)
  between operations  0.81 us (1%)
    ppermute x2, starting transfers between devices, shift_tile(): lax.ppermute(value, 'tile', [(t, (t + by) % tiles) for t in range(tiles)])  13.6 us
    pallas_call x1, Pallas kernels, covar(): pl.pallas_call(covar_kernel, in_specs=[vmem] * 6 + [pl.BlockSpec(memory_s...  8.44 us
    ppermute x2, starting transfers between devices, swap_in_pair(): return lax.ppermute(value, 'win', [(k, k ^ 1) for k in range(wins)])  7.14 us
    ppermute x2, waiting for transfers between devices, shift_tile(): lax.ppermute(value, 'tile', [(t, (t + by) % tiles) for t in range(tiles)])  6.43 us
    ppermute x2, starting transfers between devices, across_pairs(): return lax.ppermute(value, 'win', pairs)  5.15 us
    pallas_call x2, Pallas kernels, final(): pl.pallas_call(functools.partial(final_kernel, primal_on_even, bool(done)...  3.83 us
    ppermute x2, waiting for transfers between devices, across_pairs(): return lax.ppermute(value, 'win', pairs)  2.88 us
    ppermute x2, waiting for transfers between devices, swap_in_pair(): return lax.ppermute(value, 'win', [(k, k ^ 1) for k in range(wins)])  2.2 us
  transfers between devices with their start and end apart: 6, of which 3 were waited for; matrix products, arithmetic and copies ran while one was open for 0% of the time, Pallas kernels for 25%

profile of v5, /device:TPU:52, one launch (start us, length us, event | category | flops | bytes accessed | tf_op | source)
XLA Modules:
  0.0 56.1 jit_solution(13746190189952549975)
XLA Ops:
  0.6 0.0 copy-start
  0.7 1.4 %slice_select_fusion = f32[1,11,128,128]{3,2,1,0:T(8,128)S(1)} fusion(f32[1,16,128,128]{3,2,1,0:T(8,128)} %mul.7, f32[1,16,128,128]{3,2,1,0:T(8,128)} %inc.3, pred[]{:T(512)S(6)} %eq.3), kind=kLoop, calls=%fused_computation | loop fusion | flops 180224 | bytes 2162689 | tf_op jit(solution)/shard_map/jit(_where)/select_n | solution.py:415
  2.1 2.6 %collective-permute-start.2 = (f32[1408,128]{1,0:T(8,128)S(1)}, f32[1408,128]{1,0:T(8,128)S(1)}, u32[]{:S(2)}, u32[]{:S(2)}) collective-permute-start(f32[1408,128]{1,0:T(8,128)S(1)} %bitcast.9), channel_id=1, source_target_pairs={{0,64},{64,0},{128,192},{192,128},{256,320},{320,256},{384,448},{4... | collective-permute-start | bytes 2162696 | tf_op jit(solution)/shard_map/ppermute | solution.py:27
  4.7 1.7 %shard_map.95 = (f32[112,128]{1,0:T(8,128)}, f32[112,128]{1,0:T(8,128)}) custom-call(f32[1,16,128,128]{3,2,1,0:T(8,128)} %inc.3, f32[1,16,128,128]{3,2,1,0:T(8,128)} %mul.7, f32[128,128]{1,0:T(8,128)} %std.1, f32[128,128]{1,0:T(8,128)} %kappa.1, f32[128,128]{1,0:T(8,128)} %weight.3, s32[128,128]{1,0:T(8,128)} %up.3, s32[128,128]{1,0:T(8,128)} %lev.3, ...), custom_call_target="tpu_custom_call" | custom-call | flops 1000 | bytes 1000 | tf_op jit(solution)/shard_map/pallas_call | solution.py:100
  6.4 1.9 %collective-permute-start = (f32[112,128]{1,0:T(8,128)}, f32[112,128]{1,0:T(8,128)S(1)}, u32[]{:S(2)}, u32[]{:S(2)}) collective-permute-start(f32[112,128]{1,0:T(8,128)} %get-tuple-element.8), channel_id=1, source_target_pairs={{0,1},{1,2},{2,3},{3,4},{4,5},{5,6},{6,7},{7,8},{8,9},{9,10},{10,1... | collective-permute-start | bytes 172040 | tf_op jit(solution)/shard_map/ppermute | solution.py:22
  8.3 11.7 %collective-permute-start.1 = (f32[112,128]{1,0:T(8,128)}, f32[112,128]{1,0:T(8,128)S(1)}, u32[]{:S(2)}, u32[]{:S(2)}) collective-permute-start(f32[112,128]{1,0:T(8,128)} %get-tuple-element.9), channel_id=1, source_target_pairs={{0,63},{1,0},{2,1},{3,2},{4,3},{5,4},{6,5},{7,6},{8,7},{9,8},{10,9... | collective-permute-start | bytes 172040 | tf_op jit(solution)/shard_map/ppermute | solution.py:22
  20.0 0.0 copy-start.1
  20.0 0.0 copy-start.2
  20.0 2.1 %shard_map.98 = f32[1088,128]{1,0:T(8,128)} custom-call(f32[2048,128]{1,0:T(8,128)} %bitcast.7, f32[2048,128]{1,0:T(8,128)} %bitcast.8), custom_call_target="tpu_custom_call" | custom-call | flops 1000 | bytes 1000 | tf_op jit(solution)/shard_map/pallas_call | solution.py:129
  22.1 3.2 %collective-permute-start.4 = (f32[1088,128]{1,0:T(8,128)}, f32[1088,128]{1,0:T(8,128)S(1)}, u32[]{:S(2)}, u32[]{:S(2)}) collective-permute-start(f32[1088,128]{1,0:T(8,128)} %shard_map.98), channel_id=1, source_target_pairs={{64,128},{128,64},{192,256},{256,192},{320,384},{384,320},{65,129}... | collective-permute-start | bytes 1671176 | tf_op jit(solution)/shard_map/ppermute | solution.py:33
  25.4 6.4 %collective-permute-done.before = f32[112,128]{1,0:T(8,128)S(1)} collective-permute-done((f32[112,128]{1,0:T(8,128)}, f32[112,128]{1,0:T(8,128)S(1)}, u32[]{:S(2)}, u32[]{:S(2)}) %collective-permute-start) | collective-permute-done | bytes 57376 | tf_op jit(solution)/shard_map/ppermute | solution.py:22
  31.8 0.0 collective-permute-done.1.after
  31.8 0.0 copy-done.1
  31.8 0.0 copy-done.2
  31.8 0.0 copy-start.6
  31.8 0.0 copy-start.7
  31.8 0.1 shard_map.97
  31.9 1.9 %collective-permute-start.5 = (f32[1024,128]{1,0:T(8,128)S(1)}, f32[1024,128]{1,0:T(8,128)S(1)}, u32[]{:S(2)}, u32[]{:S(2)}) collective-permute-start(f32[1024,128]{1,0:T(8,128)S(1)} %get-tuple-element.11), channel_id=1, source_target_pairs={{64,128},{128,64},{192,256},{256,192},{320,384},{384,320},{65,129}... | collective-permute-start | bytes 1572872 | tf_op jit(solution)/shard_map/ppermute | solution.py:33
  33.8 4.6 %collective-permute-start.3 = (f32[704,128]{1,0:T(8,128)S(1)}, f32[704,128]{1,0:T(8,128)S(1)}, u32[]{:S(2)}, u32[]{:S(2)}) collective-permute-start(f32[704,128]{1,0:T(8,128)S(1)} %get-tuple-element.10), channel_id=1, source_target_pairs={{0,64},{64,0},{128,192},{192,128},{256,320},{320,256},{384,448},{4... | collective-permute-start | bytes 1081352 | tf_op jit(solution)/shard_map/ppermute | solution.py:27
  38.4 0.0 copy-done
  38.4 0.1 fusion
  38.5 0.1 fusion.1.power
  38.7 0.0 copy-done.6
  38.7 0.0 copy-done.7
  38.7 0.0 copy-start.3
  38.7 0.0 copy-start.4
  38.7 0.0 copy-start.5
  38.7 8.4 %shard_map.96.base = f32[16,128,128]{2,1,0:T(8,128)S(1)} custom-call(f32[1,16,128,128]{3,2,1,0:T(8,128)S(1)} %copy-done.1, f32[1,16,128,128]{3,2,1,0:T(8,128)S(1)} %copy-done.2, f32[128,128]{1,0:T(8,128)S(1)} %copy-done.6, f32[128,128]{1,0:T(8,128)S(1)} %copy-done.7, f32[112,128]{1,0:T(8,128)S(1)} %collective-permute-done.before, ...), custom_call_target="tpu_custom_call" | custom-call | flops 1000 | bytes 1000 | tf_op jit(solution)/shard_map/pallas_call | solution.py:235
  47.2 0.0 collective-permute-done.4.first
  47.2 2.9 %collective-permute-done.5.rest = f32[1024,128]{1,0:T(8,128)S(1)} collective-permute-done((f32[1024,128]{1,0:T(8,128)S(1)}, f32[1024,128]{1,0:T(8,128)S(1)}, u32[]{:S(2)}, u32[]{:S(2)}) %collective-permute-start.5) | collective-permute-done | bytes 524320 | tf_op jit(solution)/shard_map/ppermute | solution.py:33
  50.1 0.0 copy-done.3
  50.1 0.0 copy-done.4
  50.1 0.0 copy-done.5
  50.1 1.7 %shard_map.99 = (f32[1,16,128,128]{3,2,1,0:T(8,128)}, f32[1,16,128,128]{3,2,1,0:T(8,128)}) custom-call(f32[16,128,128]{2,1,0:T(8,128)S(1)} %shard_map.96.base, f32[1,16,128,128]{3,2,1,0:T(8,128)S(1)} %copy-done.1, f32[1088,128]{1,0:T(8,128)S(1)} %collective-permute-done.4.first, f32[1024,128]{1,0:T(8,128)S(1)} %collective-permute-done.5.rest, ...), custom_call_target="tpu_custom_call" | custom-call | flops 1000 | bytes 1000 | tf_op jit(solution)/shard_map/pallas_call | solution.py:380
  51.8 2.2 %collective-permute-done.3.rest = f32[704,128]{1,0:T(8,128)S(1)} collective-permute-done((f32[704,128]{1,0:T(8,128)S(1)}, f32[704,128]{1,0:T(8,128)S(1)}, u32[]{:S(2)}, u32[]{:S(2)}) %collective-permute-start.3) | collective-permute-done | bytes 360480 | tf_op jit(solution)/shard_map/ppermute | solution.py:27
  54.0 0.0 collective-permute-done.2.first
  54.0 2.2 %shard_map.100 = (f32[1,16,128,128]{3,2,1,0:T(8,128)}, f32[1,16,128,128]{3,2,1,0:T(8,128)}) custom-call(f32[16,128,128]{2,1,0:T(8,128)S(1)} %shard_map.96.base, f32[1,16,128,128]{3,2,1,0:T(8,128)S(1)} %copy-done.1, f32[1408,128]{1,0:T(8,128)S(1)} %collective-permute-done.2.first, ...), custom_call_target="tpu_custom_call", output_to_operand_aliasing={{0}: (9, {}), {1}: (10, {})} | custom-call | flops 1000 | bytes 1000 | tf_op jit(solution)/shard_map/pallas_call | solution.py:380
Async XLA Ops:
  0.6 37.8 %copy-start = (f32[16,16]{1,0:T(8,128)S(1)}, f32[16,16]{1,0:T(8,128)}, u32[]{:S(2)}) copy-start(f32[16,16]{1,0:T(8,128)} %param.15) | copy-start | bytes 3076
  2.1 51.9 %collective-permute-start.2 = (f32[1408,128]{1,0:T(8,128)S(1)}, f32[1408,128]{1,0:T(8,128)S(1)}, u32[]{:S(2)}, u32[]{:S(2)}) collective-permute-start(f32[1408,128]{1,0:T(8,128)S(1)} %bitcast.9), channel_id=1, source_target_pairs={{0,64},{64,0},{128,192},{192,128},{256,320},{320,256},{384,448},{4... | collective-permute-start | bytes 2162696 | tf_op jit(solution)/shard_map/ppermute | solution.py:27
  6.4 25.4 %collective-permute-start = (f32[112,128]{1,0:T(8,128)}, f32[112,128]{1,0:T(8,128)S(1)}, u32[]{:S(2)}, u32[]{:S(2)}) collective-permute-start(f32[112,128]{1,0:T(8,128)} %get-tuple-element.8), channel_id=1, source_target_pairs={{0,1},{1,2},{2,3},{3,4},{4,5},{5,6},{6,7},{7,8},{8,9},{9,10},{10,1... | collective-permute-start | bytes 172040 | tf_op jit(solution)/shard_map/ppermute | solution.py:22
  8.3 23.5 %collective-permute-start.1 = (f32[112,128]{1,0:T(8,128)}, f32[112,128]{1,0:T(8,128)S(1)}, u32[]{:S(2)}, u32[]{:S(2)}) collective-permute-start(f32[112,128]{1,0:T(8,128)} %get-tuple-element.9), channel_id=1, source_target_pairs={{0,63},{1,0},{2,1},{3,2},{4,3},{5,4},{6,5},{7,6},{8,7},{9,8},{10,9... | collective-permute-start | bytes 172040 | tf_op jit(solution)/shard_map/ppermute | solution.py:22
  20.0 11.8 %copy-start.1 = (f32[1,16,128,128]{3,2,1,0:T(8,128)S(1)}, f32[1,16,128,128]{3,2,1,0:T(8,128)}, u32[]{:S(2)}) copy-start(f32[1,16,128,128]{3,2,1,0:T(8,128)} %mul.7) | copy-start | bytes 3145732
  20.0 11.8 %copy-start.2 = (f32[1,16,128,128]{3,2,1,0:T(8,128)S(1)}, f32[1,16,128,128]{3,2,1,0:T(8,128)}, u32[]{:S(2)}) copy-start(f32[1,16,128,128]{3,2,1,0:T(8,128)} %inc.3) | copy-start | bytes 3145732
  22.1 25.1 %collective-permute-start.4 = (f32[1088,128]{1,0:T(8,128)}, f32[1088,128]{1,0:T(8,128)S(1)}, u32[]{:S(2)}, u32[]{:S(2)}) collective-permute-start(f32[1088,128]{1,0:T(8,128)} %shard_map.98), channel_id=1, source_target_pairs={{64,128},{128,64},{192,256},{256,192},{320,384},{384,320},{65,129}... | collective-permute-start | bytes 1671176 | tf_op jit(solution)/shard_map/ppermute | solution.py:33
  31.8 6.9 %copy-start.6 = (f32[128,128]{1,0:T(8,128)S(1)}, f32[128,128]{1,0:T(8,128)}, u32[]{:S(2)}) copy-start(f32[128,128]{1,0:T(8,128)} %std.1) | copy-start | bytes 196612
  31.8 6.9 %copy-start.7 = (f32[128,128]{1,0:T(8,128)S(1)}, f32[128,128]{1,0:T(8,128)}, u32[]{:S(2)}) copy-start(f32[128,128]{1,0:T(8,128)} %kappa.1) | copy-start | bytes 196612
  31.9 18.2 %collective-permute-start.5 = (f32[1024,128]{1,0:T(8,128)S(1)}, f32[1024,128]{1,0:T(8,128)S(1)}, u32[]{:S(2)}, u32[]{:S(2)}) collective-permute-start(f32[1024,128]{1,0:T(8,128)S(1)} %get-tuple-element.11), channel_id=1, source_target_pairs={{64,128},{128,64},{192,256},{256,192},{320,384},{384,320},{65,129}... | collective-permute-start | bytes 1572872 | tf_op jit(solution)/shard_map/ppermute | solution.py:33
  33.8 20.1 %collective-permute-start.3 = (f32[704,128]{1,0:T(8,128)S(1)}, f32[704,128]{1,0:T(8,128)S(1)}, u32[]{:S(2)}, u32[]{:S(2)}) collective-permute-start(f32[704,128]{1,0:T(8,128)S(1)} %get-tuple-element.10), channel_id=1, source_target_pairs={{0,64},{64,0},{128,192},{192,128},{256,320},{320,256},{384,448},{4... | collective-permute-start | bytes 1081352 | tf_op jit(solution)/shard_map/ppermute | solution.py:27
  38.7 11.4 %copy-start.3 = (f32[128,128]{1,0:T(8,128)S(1)}, f32[128,128]{1,0:T(8,128)}, u32[]{:S(2)}) copy-start(f32[128,128]{1,0:T(8,128)} %weight.3) | copy-start | bytes 196612
  38.7 11.4 %copy-start.4 = (s32[128,128]{1,0:T(8,128)S(1)}, s32[128,128]{1,0:T(8,128)}, u32[]{:S(2)}) copy-start(s32[128,128]{1,0:T(8,128)} %up.3) | copy-start | bytes 196612
  38.7 11.4 %copy-start.5 = (s32[128,128]{1,0:T(8,128)S(1)}, s32[128,128]{1,0:T(8,128)}, u32[]{:S(2)}) copy-start(s32[128,128]{1,0:T(8,128)} %lev.3) | copy-start | bytes 196612

commit v6 on v5

--- a/solution.py
+++ b/solution.py
@@ -108,31 +108,21 @@
     )(*(arrays * 2))
 
 
-def pick_kernel(even_source, odd_source, out, sems):
-    size = out.shape[0] // GROUPS
-
+def pick_kernel(even_source, odd_source, out):
     def copy(source):
-        parts = [pl.ds(g * size, size) for g in range(GROUPS)]
-        copies = [
-            pltpu.make_async_copy(source.at[part], out.at[part], sems.at[g])
-            for g, part in enumerate(parts)
-        ]
-        for moving in copies:
-            moving.start()
-        for moving in copies:
-            moving.wait()
+        out[...] = source[: out.shape[0]]
 
     on_even(lambda: copy(even_source), lambda: copy(odd_source))
 
 
 def pick(even_source, odd_source, count):
+    vmem = pl.BlockSpec(memory_space=pltpu.VMEM)
     return pl.pallas_call(
         pick_kernel,
-        in_specs=[pl.BlockSpec(memory_space=pl.ANY)] * 2,
-        out_specs=pl.BlockSpec(memory_space=pltpu.VMEM),
+        in_specs=[vmem] * 2,
+        out_specs=vmem,
         out_shape=jax.ShapeDtypeStruct((count, even_source.shape[1]), jnp.float32),
-        scratch_shapes=[pltpu.SemaphoreType.DMA((GROUPS,))],
-        compiler_params=pltpu.CompilerParams(vmem_limit_bytes=VMEM_WHOLE),
+        compiler_params=params(),
         cost_estimate=cost(1000, 1000),
     )(even_source, odd_source)
 
@@ -247,154 +237,236 @@
     )(mul, inc, std, kappa, before, after, power)
 
 
-def fill_field(field, width, *pieces):
+def fill_field(field, width, first, rest, known):
     levels = field.shape[0] - 2
-    rest, half = pieces[-1], REACH * levels
-    base = rest.shape[0] - 2 * half
+    early = first.shape[0]
     zero = jnp.zeros_like(field[0])
     field[0] = zero
     field[levels + 1] = zero
-    start = 0
-    for piece in pieces:
-        stop = start + (base if piece is rest else piece.shape[0])
-        for l in range(levels):
-            begin, end = max(l * width, start), min((l + 1) * width, stop)
-            if begin < end:
-                part = slice(PAD + begin - l * width, PAD + end - l * width)
-                field[l + 1, part] = piece[begin - start : end - start]
-        start = stop
+    half = REACH * levels
+    base = levels * width - early
     for l in range(levels):
-        near = slice(base + REACH * l, base + REACH * (l + 1))
         field[l + 1, :PAD] = zero[:PAD]
         field[l + 1, PAD + width :] = zero[:PAD]
-        field[l + 1, PAD - REACH : PAD] = rest[near]
-        far = rest[near.start + half : near.stop + half]
-        field[l + 1, PAD + width : PAD + width + REACH] = far
-
-
-def in_groups(levels, body, staged, out, sems):
-    size = levels // GROUPS
-    copies = []
-    for g in range(GROUPS):
-        lax.fori_loop(g * size, (g + 1) * size, lambda l, carry: body(l) or carry, 0)
-        part = pl.ds(g * size, size)
-        copy = pltpu.make_async_copy(staged.at[part], out.at[0, part], sems.at[g])
-        copy.start()
-        copies.append(copy)
-    for copy in copies:
-        copy.wait()
-
-
-def primal_levels(base, weight, up, lev, field, level_field, staged, out, sems):
-    levels, width, rows = base.shape
-    zero = jnp.zeros((width, rows), jnp.float32)
+        spans = [(0, width)]
+        if l < known - 1:
+            spans = [(0, 2 * PAD), (width - 2 * PAD, width)]
+        for c0, c1 in spans:
+            begin, end = l * width + c0, l * width + c1
+            cut = min(max(early, begin), end)
+            if cut > begin:
+                field[l + 1, PAD + c0 : PAD + c0 + cut - begin] = first[begin:cut]
+            if cut < end and rest is not None:
+                field[l + 1, PAD + c1 - (end - cut) : PAD + c1] = rest[cut - early : end - early]
+        if rest is not None:
+            near = slice(base + REACH * l, base + REACH * (l + 1))
+            field[l + 1, PAD - REACH : PAD] = rest[near]
+            far = rest[near.start + half : near.stop + half]
+            field[l + 1, PAD + width : PAD + width + REACH] = far
+
+
+def primal_setup(levels, width, refs):
+    level_field = refs["level_field"]
+    zero = jnp.zeros_like(level_field[0])
     level_field[0] = zero
     level_field[levels + 1] = zero
 
-    def one_level(l, carry):
-        step = up[...]
-        total = field[l + 1, PAD : PAD + width]
+
+def primal_levels(lo, hi, c0, c1, refs):
+    base, weight, up, lev = (refs[name] for name in ("base", "weight", "up", "lev"))
+    field, level_field, staged = (refs[name] for name in ("field", "level_field", "staged"))
+    levels = base.shape[0]
+    cols = slice(c0, c1)
+
+    def shift(l, carry):
+        step = up[cols]
+        total = field[l + 1, PAD + c0 : PAD + c1]
         for j in (-2, -1, 1, 2):
-            total = jnp.where(step == j, field[l + 1, PAD + j : PAD + j + width], total)
-        level_field[l + 1] = total
+            total = jnp.where(step == j, field[l + 1, PAD + c0 + j : PAD + c1 + j], total)
+        level_field[l + 1, cols] = total
         return carry
 
-    lax.fori_loop(0, levels, one_level, 0)
+    lax.fori_loop(max(lo - 1, 0), min(hi + 1, levels), shift, 0)
 
     def combine(l):
-        pick = lev[...]
+        pick = lev[cols]
         departed = jnp.where(
             pick == 0,
-            level_field[l + 1],
-            jnp.where(pick == 1, level_field[l + 2], level_field[l]),
+            level_field[l + 1, cols],
+            jnp.where(pick == 1, level_field[l + 2, cols], level_field[l, cols]),
         )
-        center = field[l + 1, PAD : PAD + width]
-        staged[l] = base[l] - ((1.0 - weight[...]) * center + weight[...] * departed)
-
-    in_groups(levels, combine, staged, out, sems)
-
-
-def dual_levels(
-    mul, before, after, weight, up, lev, field, weight_ext, up_ext, lev_ext, staged, out, sems
-):
-    _, levels, width, rows = mul.shape
-    tall = width + 2 * PAD
+        center = field[l + 1, PAD + c0 : PAD + c1]
+        share = weight[cols]
+        staged[l, cols] = base[l, cols] - ((1.0 - share) * center + share * departed)
+
+    return combine
+
+
+def dual_setup(levels, width, refs):
     spot = Rows(levels)
-    weight_ext[...] = jnp.zeros_like(weight_ext)
-    up_ext[...] = jnp.zeros_like(up_ext)
-    lev_ext[...] = jnp.zeros_like(lev_ext)
-    weight_ext[PAD : PAD + width] = weight[...]
-    up_ext[PAD : PAD + width] = up[...]
-    lev_ext[PAD : PAD + width] = lev[...]
     left, right = slice(PAD - REACH, PAD), slice(PAD + width, PAD + width + REACH)
-    for side, part in ((before, left), (after, right)):
-        weight_ext[part] = side[spot.weight]
+    for name in ("weight", "up", "lev"):
+        extended = refs[name + "_ext"]
+        extended[...] = jnp.zeros_like(extended)
+        extended[PAD : PAD + width] = refs[name][...]
+    for side, part in ((refs["before"], left), (refs["after"], right)):
+        refs["weight_ext"][part] = side[spot.weight]
         code = side[spot.code]
         step = jnp.floor((code + 1.5) * (1.0 / 3.0))
-        up_ext[part] = step.astype(jnp.int32)
-        lev_ext[part] = (code - 3.0 * step).astype(jnp.int32)
+        refs["up_ext"][part] = step.astype(jnp.int32)
+        refs["lev_ext"][part] = (code - 3.0 * step).astype(jnp.int32)
+
+
+def dual_levels(lo, hi, c0, c1, refs):
+    mul, weight, field, staged = (refs[name] for name in ("mul", "weight", "field", "staged"))
+    cols, around = slice(c0, c1), slice(c0, c1 + 2 * PAD)
+    tall = c1 - c0 + 2 * PAD
 
     def one_level(l):
-        pick = lev_ext[...]
+        pick = refs["lev_ext"][around]
         lifted = jnp.where(
-            pick == 0, field[l + 1], jnp.where(pick == 1, field[l], field[l + 2])
+            pick == 0,
+            field[l + 1, around],
+            jnp.where(pick == 1, field[l, around], field[l + 2, around]),
         )
-        source = weight_ext[...] * lifted
-        step = up_ext[...]
+        source = refs["weight_ext"][around] * lifted
+        step = refs["up_ext"][around]
         total = jnp.where(step == 0, source, 0.0)
         for j in (-2, -1, 1, 2):
             total = total + pltpu.roll(jnp.where(step == j, source, 0.0), j % tall, 0)
-        returned = total[PAD : PAD + width]
-        center = field[l + 1, PAD : PAD + width]
-        staged[l] = mul[0, l] - ((1.0 - weight[...]) * center + returned)
-
-    in_groups(levels, one_level, staged, out, sems)
-
-
-def final_kernel(primal_on_even, last, base, mul, first, rest, before, after, weight, up, lev, *refs):
-    if last:
-        refs = refs[2:]
-    primal, dual, field, level_field, weight_ext, up_ext, lev_ext, staged, sems = refs
-    fill_field(field, mul.shape[2], first, rest)
-
-    def make_primal():
-        primal_levels(base, weight, up, lev, field, level_field, staged, primal, sems)
-
-    def make_dual():
-        dual_levels(
-            mul, before, after, weight, up, lev, field, weight_ext, up_ext, lev_ext,
-            staged, dual, sems,
-        )
-
+        returned = total[PAD : PAD + c1 - c0]
+        center = field[l + 1, PAD + c0 : PAD + c1]
+        staged[l, cols] = mul[0, l, cols] - ((1.0 - weight[cols]) * center + returned)
+
+    return one_level
+
+
+def run_levels(lo, hi, body):
+    lax.fori_loop(lo, hi, lambda l, carry: body(l) or carry, 0)
+
+
+def produce(setup, make, known, refs, out, partial, sems):
+    levels, width = refs["base"].shape[:2]
+    fill_field(refs["field"], width, refs["first"], refs["rest"], known)
+    staged, copies = refs["staged"], []
+
+    def send(source, target):
+        copy = pltpu.make_async_copy(source, target, sems.at[len(copies)])
+        copy.start()
+        copies.append(copy)
+
+    if known:
+        send(partial, out.at[0, pl.ds(0, known)])
+    setup(levels, width, refs)
+    body = make(known, levels, 0, width, refs)
+    size = (levels - known) // 2
+    for start in (known, known + size):
+        stop = levels if start > known else start + size
+        run_levels(start, stop, body)
+        part = pl.ds(start, stop - start)
+        send(staged.at[part], out.at[0, part])
+    if known:
+        spans = ((0, PAD), (width - PAD, width))
+        for c0, c1 in spans:
+            run_levels(0, known, make(0, known, c0, c1, refs))
+        copies[0].wait()
+        for c0, _ in spans:
+            part, cols = pl.ds(0, known), pl.ds(c0, PAD)
+            send(staged.at[part, cols], out.at[0, part, cols])
+    for copy in copies[1 if known else 0 :]:
+        copy.wait()
+
+
+NAMES = ("base", "mul", "first", "rest", "before", "after", "weight", "up", "lev")
+SCRATCH = ("field", "level_field", "weight_ext", "up_ext", "lev_ext", "staged")
+
+
+def by_parity(primal_on_even, make_primal, make_dual):
     if primal_on_even:
         on_even(make_primal, make_dual)
     else:
         on_even(make_dual, make_primal)
 
 
-def final(primal_on_even, base, mul, pieces, before, after, columns, done=()):
+def final_kernel(primal_on_even, known, *refs):
+    named = dict(zip(NAMES, refs))
+    refs = refs[len(NAMES) :]
+    partial = None
+    if known:
+        partial, refs = refs[0], refs[3:]
+    primal, dual, *scratch, sems = refs
+    named.update(zip(SCRATCH, scratch))
+    by_parity(
+        primal_on_even,
+        lambda: produce(primal_setup, primal_levels, known, named, primal, partial, sems),
+        lambda: produce(dual_setup, dual_levels, known, named, dual, partial, sems),
+    )
+
+
+def scratch_shapes(levels, width, rows):
+    tall = width + 2 * PAD
+    return [
+        pltpu.VMEM((levels + 2, tall, rows), jnp.float32),
+        pltpu.VMEM((levels + 2, width, rows), jnp.float32),
+        pltpu.VMEM((tall, rows), jnp.float32),
+        pltpu.VMEM((tall, rows), jnp.int32),
+        pltpu.VMEM((tall, rows), jnp.int32),
+        pltpu.VMEM((levels, width, rows), jnp.float32),
+        pltpu.SemaphoreType.DMA((5,)),
+    ]
+
+
+def final(primal_on_even, base, mul, pieces, before, after, columns, partial=None, done=()):
     _, levels, width, rows = mul.shape
     vmem = pl.BlockSpec(memory_space=pltpu.VMEM)
     anywhere = pl.BlockSpec(memory_space=pl.ANY)
-    tall = width + 2 * PAD
+    known = 0 if partial is None else partial.shape[0]
+    extra = () if partial is None else (partial,)
     return pl.pallas_call(
-        functools.partial(final_kernel, primal_on_even, bool(done)),
-        in_specs=[vmem] * 9 + [anywhere] * len(done),
+        functools.partial(final_kernel, primal_on_even, known),
+        in_specs=[vmem] * (9 + len(extra)) + [anywhere] * len(done),
         out_specs=[anywhere] * 2,
         out_shape=[jax.ShapeDtypeStruct(mul.shape, jnp.float32)] * 2,
-        input_output_aliases={9: 0, 10: 1} if done else {},
-        scratch_shapes=[
-            pltpu.VMEM((levels + 2, tall, rows), jnp.float32),
-            pltpu.VMEM((levels + 2, width, rows), jnp.float32),
-            pltpu.VMEM((tall, rows), jnp.float32),
-            pltpu.VMEM((tall, rows), jnp.int32),
-            pltpu.VMEM((tall, rows), jnp.int32),
-            pltpu.VMEM((levels, width, rows), jnp.float32),
-            pltpu.SemaphoreType.DMA((GROUPS,)),
-        ],
+        input_output_aliases={10: 0, 11: 1} if done else {},
+        scratch_shapes=scratch_shapes(levels, width, rows),
         compiler_params=params(),
         cost_estimate=cost(1000, 1000),
-    )(base, mul, *pieces, before, after, *columns, *done)
+    )(base, mul, *pieces, before, after, *columns, *extra, *done)
+
+
+def partial_kernel(primal_on_even, *refs):
+    names = [name for name in NAMES if name != "rest"]
+    named = dict(zip(names, refs), rest=None)
+    out, *scratch, _ = refs[len(names) :]
+    named.update(zip(SCRATCH, scratch))
+    named["staged"] = out
+    levels, width = named["base"].shape[:2]
+
+    def run(setup, make):
+        fill_field(named["field"], width, named["first"], None, 0)
+        setup(levels, width, named)
+        run_levels(0, out.shape[0], make(0, out.shape[0], 0, width, named))
+
+    by_parity(
+        primal_on_even,
+        lambda: run(primal_setup, primal_levels),
+        lambda: run(dual_setup, dual_levels),
+    )
+
+
+def partial_final(primal_on_even, base, mul, first, before, after, columns):
+    _, levels, width, rows = mul.shape
+    vmem = pl.BlockSpec(memory_space=pltpu.VMEM)
+    known = first.shape[0] // width - 1
+    return pl.pallas_call(
+        functools.partial(partial_kernel, primal_on_even),
+        in_specs=[vmem] * 8,
+        out_specs=vmem,
+        out_shape=jax.ShapeDtypeStruct((known, width, rows), jnp.float32),
+        scratch_shapes=scratch_shapes(levels, width, rows),
+        compiler_params=params(),
+        cost_estimate=cost(1000, 1000),
+    )(base, mul, first, before, after, *columns)
 
 
 def per_device(
@@ -426,9 +498,12 @@
     power = jnp.dot(vertical_inverse, vertical_inverse, **exact)
     power = jnp.dot(power, power, **exact)
     base = covar(multipliers, increments, std_dev, diffusivity, before, after, power)
-    done = final(True, base, multipliers, (far_first, far_rest), before, after, columns)
+    partial = partial_final(False, base, multipliers, near_first, before, after, columns)
+    first_lev, partial = lax.optimization_barrier((level_offset, partial))
+    columns_then = (departure_weight, upstream, first_lev)
+    done = final(True, base, multipliers, (far_first, far_rest), before, after, columns_then)
     primal, dual = final(
-        False, base, multipliers, (near_first, near_rest), before, after, columns, done
+        False, base, multipliers, (near_first, near_rest), before, after, columns, partial, done
     )
     return (primal, dual)
 

time: 56.5 us -> 56 us (level)
  Pallas kernels: 16.2 us -> 14.6 us
  waiting for transfers between devices: 11.5 us -> 12.5 us
    ppermute x2, waiting for transfers between devices: 6.43 us -> 8.48 us  [shift_tile(): lax.ppermute(value, 'tile', [(t, (t + by) % tiles) for t in range(tiles)])]
    pallas_call x3 -> x4, Pallas kernels: 5.93 us -> 4.3 us  [the longest x2 3.31 us: final(): pl.pallas_call(functools.partial(final_kernel, primal_on_even, known), in...]
    ppermute x2, waiting for transfers between devices: 2.88 us -> 1.52 us  [across_pairs(): return lax.ppermute(value, 'win', pairs)]
  transfers between devices with their start and end apart: 6 -> 6, of which waited for: 3 -> 3; matrix products, arithmetic and copies ran while one was open for 0% -> 0% of each run, Pallas kernels for 25% -> 23%
where the time goes in v6:
time: 56 us; the launch traced here: 55.6 us
  starting transfers between devices  26 us (46%)
  Pallas kernels  14.6 us (26%)
  waiting for transfers between devices  12.5 us (22%)
  other arithmetic  1.41 us (3%)
  between operations  0.84 us (2%)
    ppermute x2, starting transfers between devices, shift_tile(): lax.ppermute(value, 'tile', [(t, (t + by) % tiles) for t in range(tiles)])  13.6 us
    ppermute x2, waiting for transfers between devices, shift_tile(): lax.ppermute(value, 'tile', [(t, (t + by) % tiles) for t in range(tiles)])  8.48 us
    pallas_call x1, Pallas kernels, covar(): pl.pallas_call(covar_kernel, in_specs=[vmem] * 6 + [pl.BlockSpec(memory_s...  8.45 us
    ppermute x2, starting transfers between devices, swap_in_pair(): return lax.ppermute(value, 'win', [(k, k ^ 1) for k in range(wins)])  7.27 us
    ppermute x2, starting transfers between devices, across_pairs(): return lax.ppermute(value, 'win', pairs)  5.15 us
    pallas_call x2, Pallas kernels, final(): pl.pallas_call(functools.partial(final_kernel, primal_on_even, known), in...  3.31 us
    ppermute x2, waiting for transfers between devices, swap_in_pair(): return lax.ppermute(value, 'win', [(k, k ^ 1) for k in range(wins)])  2.5 us
    pallas_call x1, Pallas kernels, pack(): pl.pallas_call(functools.partial(pack_both, levels), grid=(1,), in_specs=...  1.73 us
  transfers between devices with their start and end apart: 6, of which 3 were waited for; matrix products, arithmetic and copies ran while one was open for 0% of the time, Pallas kernels for 23%

profile of v6, /device:TPU:52, one launch (start us, length us, event | category | flops | bytes accessed | tf_op | source)
XLA Modules:
  0.0 55.6 jit_solution(15955822496244592590)
XLA Ops:
  0.6 0.0 copy-start
  0.7 1.4 %slice_select_fusion = f32[1,11,128,128]{3,2,1,0:T(8,128)S(1)} fusion(f32[1,16,128,128]{3,2,1,0:T(8,128)} %refs_1_.7, f32[1,16,128,128]{3,2,1,0:T(8,128)} %inc.3, pred[]{:T(512)S(6)} %eq.3), kind=kLoop, calls=%fused_computation | loop fusion | flops 180224 | bytes 2162689 | tf_op jit(solution)/shard_map/jit(_where)/select_n | solution.py:487
  2.1 0.0 copy-start.1
  2.1 0.0 copy-start.2
  2.1 2.7 %collective-permute-start.2 = (f32[1408,128]{1,0:T(8,128)S(1)}, f32[1408,128]{1,0:T(8,128)S(1)}, u32[]{:S(2)}, u32[]{:S(2)}) collective-permute-start(f32[1408,128]{1,0:T(8,128)S(1)} %bitcast.9), channel_id=1, source_target_pairs={{0,64},{64,0},{128,192},{192,128},{256,320},{320,256},{384,448},{4... | collective-permute-start | bytes 2162696 | tf_op jit(solution)/shard_map/ppermute | solution.py:27
  4.8 1.7 %shard_map.95 = (f32[112,128]{1,0:T(8,128)}, f32[112,128]{1,0:T(8,128)}) custom-call(f32[1,16,128,128]{3,2,1,0:T(8,128)} %inc.3, f32[1,16,128,128]{3,2,1,0:T(8,128)} %refs_1_.7, f32[128,128]{1,0:T(8,128)} %std.1, f32[128,128]{1,0:T(8,128)} %kappa.1, f32[128,128]{1,0:T(8,128)} %refs_6_.7, s32[128,128]{1,0:T(8,128)} %refs_7_.7, s32[128,128]{1,0:T(8,128)} %refs_8_.4, ...), custom_call_target="tpu_custom_call" | custom-call | flops 1000 | bytes 1000 | tf_op jit(solution)/shard_map/pallas_call | solution.py:100
  6.5 1.9 %collective-permute-start = (f32[112,128]{1,0:T(8,128)}, f32[112,128]{1,0:T(8,128)S(1)}, u32[]{:S(2)}, u32[]{:S(2)}) collective-permute-start(f32[112,128]{1,0:T(8,128)} %get-tuple-element.10), channel_id=1, source_target_pairs={{0,1},{1,2},{2,3},{3,4},{4,5},{5,6},{6,7},{7,8},{8,9},{9,10},{10,1... | collective-permute-start | bytes 172040 | tf_op jit(solution)/shard_map/ppermute | solution.py:22
  8.5 11.7 %collective-permute-start.1 = (f32[112,128]{1,0:T(8,128)}, f32[112,128]{1,0:T(8,128)S(1)}, u32[]{:S(2)}, u32[]{:S(2)}) collective-permute-start(f32[112,128]{1,0:T(8,128)} %get-tuple-element.11), channel_id=1, source_target_pairs={{0,63},{1,0},{2,1},{3,2},{4,3},{5,4},{6,5},{7,6},{8,7},{9,8},{10,9... | collective-permute-start | bytes 172040 | tf_op jit(solution)/shard_map/ppermute | solution.py:22
  20.1 0.0 copy-done.1
  20.2 0.0 copy-done.2
  20.2 0.1 shard_map.99
  20.2 3.2 %collective-permute-start.4 = (f32[1088,128]{1,0:T(8,128)S(1)}, f32[1088,128]{1,0:T(8,128)S(1)}, u32[]{:S(2)}, u32[]{:S(2)}) collective-permute-start(f32[1088,128]{1,0:T(8,128)S(1)} %shard_map.99), channel_id=1, source_target_pairs={{64,128},{128,64},{192,256},{256,192},{320,384},{384,320},{65,129}... | collective-permute-start | bytes 1671176 | tf_op jit(solution)/shard_map/ppermute | solution.py:33
  23.5 8.5 %collective-permute-done.before.refs_3_.refs_4_ = f32[112,128]{1,0:T(8,128)S(1)} collective-permute-done((f32[112,128]{1,0:T(8,128)}, f32[112,128]{1,0:T(8,128)S(1)}, u32[]{:S(2)}, u32[]{:S(2)}) %collective-permute-start) | collective-permute-done | bytes 57376 | tf_op jit(solution)/shard_map/ppermute | solution.py:22
  31.9 0.0 collective-permute-done.1.after.refs_4_.refs_5_
  31.9 0.0 copy-start.6
  31.9 0.0 copy-start.7
  31.9 0.1 shard_map.97
  32.0 1.9 %collective-permute-start.5 = (f32[1024,128]{1,0:T(8,128)S(1)}, f32[1024,128]{1,0:T(8,128)S(1)}, u32[]{:S(2)}, u32[]{:S(2)}) collective-permute-start(f32[1024,128]{1,0:T(8,128)S(1)} %get-tuple-element.14), channel_id=1, source_target_pairs={{64,128},{128,64},{192,256},{256,192},{320,384},{384,320},{65,129}... | collective-permute-start | bytes 1572872 | tf_op jit(solution)/shard_map/ppermute | solution.py:33
  34.0 4.6 %collective-permute-start.3 = (f32[704,128]{1,0:T(8,128)S(1)}, f32[704,128]{1,0:T(8,128)S(1)}, u32[]{:S(2)}, u32[]{:S(2)}) collective-permute-start(f32[704,128]{1,0:T(8,128)S(1)} %get-tuple-element.12), channel_id=1, source_target_pairs={{0,64},{64,0},{128,192},{192,128},{256,320},{320,256},{384,448},{4... | collective-permute-start | bytes 1081352 | tf_op jit(solution)/shard_map/ppermute | solution.py:27
  38.5 0.0 copy-done
  38.5 0.1 fusion
  38.7 0.1 fusion.1.power
  38.8 0.0 copy-done.6
  38.8 0.0 copy-done.7
  38.8 0.0 copy-start.3
  38.8 0.0 copy-start.4
  38.8 0.0 copy-start.5
  38.9 8.4 %shard_map.96.refs_0_ = f32[16,128,128]{2,1,0:T(8,128)S(1)} custom-call(f32[1,16,128,128]{3,2,1,0:T(8,128)S(1)} %copy-done.1, f32[1,16,128,128]{3,2,1,0:T(8,128)S(1)} %copy-done.2, f32[128,128]{1,0:T(8,128)S(1)} %copy-done.6, f32[128,128]{1,0:T(8,128)S(1)} %copy-done.7, f32[112,128]{1,0:T(8,128)S(1)} %collective-permute-done.before.refs_3_.refs_4_, ...), custom_call_target="tpu_custom_call" | custom-call | flops 1000 | bytes 1000 | tf_op jit(solution)/shard_map/pallas_call | solution.py:225
  47.3 0.0 collective-permute-done.2.refs_2_
  47.3 0.0 copy-done.3
  47.3 0.0 copy-done.4
  47.3 0.0 copy-done.5
  47.3 0.9 %shard_map.98.refs_9_ = f32[10,128,128]{2,1,0:T(8,128)S(1)} custom-call(f32[16,128,128]{2,1,0:T(8,128)S(1)} %shard_map.96.refs_0_, f32[1,16,128,128]{3,2,1,0:T(8,128)S(1)} %copy-done.1, f32[1408,128]{1,0:T(8,128)S(1)} %collective-permute-done.2.refs_2_, f32[112,128]{1,0:T(8,128)S(1)} %collective-permute-done.before.refs_3_.refs_4_, ...), custom_call_target="tpu_custom_call" | custom-call | flops 1000 | bytes 1000 | tf_op jit(solution)/shard_map/pallas_call | solution.py:461
  48.3 0.0 collective-permute-done.4.refs_2_
  48.3 1.5 %collective-permute-done.5.refs_3_ = f32[1024,128]{1,0:T(8,128)S(1)} collective-permute-done((f32[1024,128]{1,0:T(8,128)S(1)}, f32[1024,128]{1,0:T(8,128)S(1)}, u32[]{:S(2)}, u32[]{:S(2)}) %collective-permute-start.5) | collective-permute-done | bytes 524320 | tf_op jit(solution)/shard_map/ppermute | solution.py:33
  49.8 1.8 %shard_map.100 = (f32[1,16,128,128]{3,2,1,0:T(8,128)}, f32[1,16,128,128]{3,2,1,0:T(8,128)}) custom-call(f32[16,128,128]{2,1,0:T(8,128)S(1)} %shard_map.96.refs_0_, f32[1,16,128,128]{3,2,1,0:T(8,128)S(1)} %copy-done.1, f32[1088,128]{1,0:T(8,128)S(1)} %collective-permute-done.4.refs_2_, f32[1024,128]{1,0:T(8,128)S(1)} %collective-permute-done.5.refs_3_, ...), custom_call_target="tpu_custom_call" | custom-call | flops 1000 | bytes 1000 | tf_op jit(solution)/shard_map/pallas_call | solution.py:425
  51.6 2.5 %collective-permute-done.3.refs_3_ = f32[704,128]{1,0:T(8,128)S(1)} collective-permute-done((f32[704,128]{1,0:T(8,128)S(1)}, f32[704,128]{1,0:T(8,128)S(1)}, u32[]{:S(2)}, u32[]{:S(2)}) %collective-permute-start.3) | collective-permute-done | bytes 360480 | tf_op jit(solution)/shard_map/ppermute | solution.py:27
  54.1 1.5 %shard_map.101 = (f32[1,16,128,128]{3,2,1,0:T(8,128)}, f32[1,16,128,128]{3,2,1,0:T(8,128)}) custom-call(f32[16,128,128]{2,1,0:T(8,128)S(1)} %shard_map.96.refs_0_, f32[1,16,128,128]{3,2,1,0:T(8,128)S(1)} %copy-done.1, f32[1408,128]{1,0:T(8,128)S(1)} %collective-permute-done.2.refs_2_, ...), custom_call_target="tpu_custom_call", output_to_operand_aliasing={{0}: (10, {}), {1}: (11, {})} | custom-call | flops 1000 | bytes 1000 | tf_op jit(solution)/shard_map/pallas_call | solution.py:425
Async XLA Ops:
  0.6 37.9 %copy-start = (f32[16,16]{1,0:T(8,128)S(1)}, f32[16,16]{1,0:T(8,128)}, u32[]{:S(2)}) copy-start(f32[16,16]{1,0:T(8,128)} %param.15) | copy-start | bytes 3076
  2.1 18.1 %copy-start.1 = (f32[1,16,128,128]{3,2,1,0:T(8,128)S(1)}, f32[1,16,128,128]{3,2,1,0:T(8,128)}, u32[]{:S(2)}) copy-start(f32[1,16,128,128]{3,2,1,0:T(8,128)} %refs_1_.7) | copy-start | bytes 3145732
  2.1 18.1 %copy-start.2 = (f32[1,16,128,128]{3,2,1,0:T(8,128)S(1)}, f32[1,16,128,128]{3,2,1,0:T(8,128)}, u32[]{:S(2)}) copy-start(f32[1,16,128,128]{3,2,1,0:T(8,128)} %inc.3) | copy-start | bytes 3145732
  2.1 45.2 %collective-permute-start.2 = (f32[1408,128]{1,0:T(8,128)S(1)}, f32[1408,128]{1,0:T(8,128)S(1)}, u32[]{:S(2)}, u32[]{:S(2)}) collective-permute-start(f32[1408,128]{1,0:T(8,128)S(1)} %bitcast.9), channel_id=1, source_target_pairs={{0,64},{64,0},{128,192},{192,128},{256,320},{320,256},{384,448},{4... | collective-permute-start | bytes 2162696 | tf_op jit(solution)/shard_map/ppermute | solution.py:27
  6.5 25.4 %collective-permute-start = (f32[112,128]{1,0:T(8,128)}, f32[112,128]{1,0:T(8,128)S(1)}, u32[]{:S(2)}, u32[]{:S(2)}) collective-permute-start(f32[112,128]{1,0:T(8,128)} %get-tuple-element.10), channel_id=1, source_target_pairs={{0,1},{1,2},{2,3},{3,4},{4,5},{5,6},{6,7},{7,8},{8,9},{9,10},{10,1... | collective-permute-start | bytes 172040 | tf_op jit(solution)/shard_map/ppermute | solution.py:22
  8.5 23.5 %collective-permute-start.1 = (f32[112,128]{1,0:T(8,128)}, f32[112,128]{1,0:T(8,128)S(1)}, u32[]{:S(2)}, u32[]{:S(2)}) collective-permute-start(f32[112,128]{1,0:T(8,128)} %get-tuple-element.11), channel_id=1, source_target_pairs={{0,63},{1,0},{2,1},{3,2},{4,3},{5,4},{6,5},{7,6},{8,7},{9,8},{10,9... | collective-permute-start | bytes 172040 | tf_op jit(solution)/shard_map/ppermute | solution.py:22
  20.2 28.1 %collective-permute-start.4 = (f32[1088,128]{1,0:T(8,128)S(1)}, f32[1088,128]{1,0:T(8,128)S(1)}, u32[]{:S(2)}, u32[]{:S(2)}) collective-permute-start(f32[1088,128]{1,0:T(8,128)S(1)} %shard_map.99), channel_id=1, source_target_pairs={{64,128},{128,64},{192,256},{256,192},{320,384},{384,320},{65,129}... | collective-permute-start | bytes 1671176 | tf_op jit(solution)/shard_map/ppermute | solution.py:33
  31.9 6.9 %copy-start.6 = (f32[128,128]{1,0:T(8,128)S(1)}, f32[128,128]{1,0:T(8,128)}, u32[]{:S(2)}) copy-start(f32[128,128]{1,0:T(8,128)} %std.1) | copy-start | bytes 196612
  31.9 6.9 %copy-start.7 = (f32[128,128]{1,0:T(8,128)S(1)}, f32[128,128]{1,0:T(8,128)}, u32[]{:S(2)}) copy-start(f32[128,128]{1,0:T(8,128)} %kappa.1) | copy-start | bytes 196612
  32.0 17.8 %collective-permute-start.5 = (f32[1024,128]{1,0:T(8,128)S(1)}, f32[1024,128]{1,0:T(8,128)S(1)}, u32[]{:S(2)}, u32[]{:S(2)}) collective-permute-start(f32[1024,128]{1,0:T(8,128)S(1)} %get-tuple-element.14), channel_id=1, source_target_pairs={{64,128},{128,64},{192,256},{256,192},{320,384},{384,320},{65,129}... | collective-permute-start | bytes 1572872 | tf_op jit(solution)/shard_map/ppermute | solution.py:33
  34.0 20.1 %collective-permute-start.3 = (f32[704,128]{1,0:T(8,128)S(1)}, f32[704,128]{1,0:T(8,128)S(1)}, u32[]{:S(2)}, u32[]{:S(2)}) collective-permute-start(f32[704,128]{1,0:T(8,128)S(1)} %get-tuple-element.12), channel_id=1, source_target_pairs={{0,64},{64,0},{128,192},{192,128},{256,320},{320,256},{384,448},{4... | collective-permute-start | bytes 1081352 | tf_op jit(solution)/shard_map/ppermute | solution.py:27
  38.8 8.5 %copy-start.3 = (f32[128,128]{1,0:T(8,128)S(1)}, f32[128,128]{1,0:T(8,128)}, u32[]{:S(2)}) copy-start(f32[128,128]{1,0:T(8,128)} %refs_6_.7) | copy-start | bytes 196612
  38.8 8.5 %copy-start.4 = (s32[128,128]{1,0:T(8,128)S(1)}, s32[128,128]{1,0:T(8,128)}, u32[]{:S(2)}) copy-start(s32[128,128]{1,0:T(8,128)} %refs_7_.7) | copy-start | bytes 196612
  38.8 8.5 %copy-start.5 = (s32[128,128]{1,0:T(8,128)S(1)}, s32[128,128]{1,0:T(8,128)}, u32[]{:S(2)}) copy-start(s32[128,128]{1,0:T(8,128)} %refs_8_.4) | copy-start | bytes 196612

commit v7 on v6

--- a/solution.py
+++ b/solution.py
@@ -10,7 +10,7 @@
 SWEEPS = 4
 REACH = 2
 PAD = 8
-NEAR = 1408
+NEAR = 1536
 FAR = 1088
 GROUPS = 4
 VMEM_LIMIT = 40 * 1024 * 1024

time: 56 us -> 57.1 us (1.020)
  the two profiles are of different devices: /device:TPU:52 before, /device:TPU:510 now
where the time goes in v7:
time: 57.1 us; the launch traced here: 56.8 us
  waiting for transfers between devices  21.5 us (38%)
  starting transfers between devices  17 us (30%)
  Pallas kernels  14.8 us (26%)
  other arithmetic  2.34 us (4%)
  between operations  0.84 us (1%)
    ppermute x2, waiting for transfers between devices, swap_in_pair(): return lax.ppermute(value, 'win', [(k, k ^ 1) for k in range(wins)])  20.1 us
    ppermute x2, starting transfers between devices, swap_in_pair(): return lax.ppermute(value, 'win', [(k, k ^ 1) for k in range(wins)])  10 us
    pallas_call x1, Pallas kernels, covar(): pl.pallas_call(covar_kernel, in_specs=[vmem] * 6 + [pl.BlockSpec(memory_s...  8.45 us
    ppermute x2, starting transfers between devices, shift_tile(): lax.ppermute(value, 'tile', [(t, (t + by) % tiles) for t in range(tiles)])  5.55 us
    pallas_call x2, Pallas kernels, final(): pl.pallas_call(functools.partial(final_kernel, primal_on_even, known), in...  3.78 us
    select_n x1, other arithmetic, per_device(): near_part = jnp.where(even, inc_rows[:near_early], mul_rows[:near_early])  2.34 us
    pallas_call x1, Pallas kernels, pack(): pl.pallas_call(functools.partial(pack_both, levels), grid=(1,), in_specs=...  1.73 us
    ppermute x2, starting transfers between devices, across_pairs(): return lax.ppermute(value, 'win', pairs)  1.39 us
  transfers between devices with their start and end apart: 6, of which 2 were waited for; matrix products, arithmetic and copies ran while one was open for 0% of the time, Pallas kernels for 23%

profile of v7, /device:TPU:510, one launch (start us, length us, event | category | flops | bytes accessed | tf_op | source)
XLA Modules:
  0.0 56.8 jit_solution(2668873063130846152)
XLA Ops:
  0.6 0.0 copy-start
  0.7 2.3 %slice_select_fusion = f32[1,12,128,128]{3,2,1,0:T(8,128)} fusion(f32[1,16,128,128]{3,2,1,0:T(8,128)} %refs_1_.7, f32[1,16,128,128]{3,2,1,0:T(8,128)} %inc.3, pred[]{:T(512)S(6)} %eq.3), kind=kLoop, calls=%fused_computation | loop fusion | flops 196608 | bytes 2359297 | tf_op jit(solution)/shard_map/jit(_where)/select_n | solution.py:487
  3.0 0.0 copy-start.1
  3.0 0.0 copy-start.2
  3.0 3.4 %collective-permute-start.2 = (f32[1536,128]{1,0:T(8,128)}, f32[1536,128]{1,0:T(8,128)S(1)}, u32[]{:S(2)}, u32[]{:S(2)}) collective-permute-start(f32[1536,128]{1,0:T(8,128)} %bitcast), channel_id=1, source_target_pairs={{0,64},{64,0},{128,192},{192,128},{256,320},{320,256},{384,448},{4... | collective-permute-start | bytes 2359304 | tf_op jit(solution)/shard_map/ppermute | solution.py:27
  6.4 1.7 %shard_map.95 = (f32[112,128]{1,0:T(8,128)}, f32[112,128]{1,0:T(8,128)}) custom-call(f32[1,16,128,128]{3,2,1,0:T(8,128)} %inc.3, f32[1,16,128,128]{3,2,1,0:T(8,128)} %refs_1_.7, f32[128,128]{1,0:T(8,128)} %std.1, f32[128,128]{1,0:T(8,128)} %kappa.1, f32[128,128]{1,0:T(8,128)} %refs_6_.7, s32[128,128]{1,0:T(8,128)} %refs_7_.7, s32[128,128]{1,0:T(8,128)} %refs_8_.4, ...), custom_call_target="tpu_custom_call" | custom-call | flops 1000 | bytes 1000 | tf_op jit(solution)/shard_map/pallas_call | solution.py:100
  8.1 1.9 %collective-permute-start = (f32[112,128]{1,0:T(8,128)}, f32[112,128]{1,0:T(8,128)S(1)}, u32[]{:S(2)}, u32[]{:S(2)}) collective-permute-start(f32[112,128]{1,0:T(8,128)} %get-tuple-element.10), channel_id=1, source_target_pairs={{0,1},{1,2},{2,3},{3,4},{4,5},{5,6},{6,7},{7,8},{8,9},{9,10},{10,1... | collective-permute-start | bytes 172040 | tf_op jit(solution)/shard_map/ppermute | solution.py:22
  10.0 3.6 %collective-permute-start.1 = (f32[112,128]{1,0:T(8,128)}, f32[112,128]{1,0:T(8,128)S(1)}, u32[]{:S(2)}, u32[]{:S(2)}) collective-permute-start(f32[112,128]{1,0:T(8,128)} %get-tuple-element.11), channel_id=1, source_target_pairs={{0,63},{1,0},{2,1},{3,2},{4,3},{5,4},{6,5},{7,6},{8,7},{9,8},{10,9... | collective-permute-start | bytes 172040 | tf_op jit(solution)/shard_map/ppermute | solution.py:22
  13.7 0.0 copy-done.1
  13.7 0.0 copy-done.2
  13.7 0.1 shard_map.99
  13.8 0.7 %collective-permute-start.4 = (f32[1088,128]{1,0:T(8,128)S(1)}, f32[1088,128]{1,0:T(8,128)S(1)}, u32[]{:S(2)}, u32[]{:S(2)}) collective-permute-start(f32[1088,128]{1,0:T(8,128)S(1)} %shard_map.99), channel_id=1, source_target_pairs={{64,128},{128,64},{192,256},{256,192},{320,384},{384,320},{65,129}... | collective-permute-start | bytes 1671176 | tf_op jit(solution)/shard_map/ppermute | solution.py:33
  14.5 0.0 collective-permute-done.before.refs_3_.refs_4_
  14.5 1.3 %collective-permute-done.1.after.refs_4_.refs_5_ = f32[112,128]{1,0:T(8,128)S(1)} collective-permute-done((f32[112,128]{1,0:T(8,128)}, f32[112,128]{1,0:T(8,128)S(1)}, u32[]{:S(2)}, u32[]{:S(2)}) %collective-permute-start.1) | collective-permute-done | bytes 57376 | tf_op jit(solution)/shard_map/ppermute | solution.py:22
  15.8 0.0 copy-start.6
  15.8 0.0 copy-start.7
  15.8 0.1 shard_map.97
  15.9 0.7 %collective-permute-start.5 = (f32[1024,128]{1,0:T(8,128)S(1)}, f32[1024,128]{1,0:T(8,128)S(1)}, u32[]{:S(2)}, u32[]{:S(2)}) collective-permute-start(f32[1024,128]{1,0:T(8,128)S(1)} %get-tuple-element.14), channel_id=1, source_target_pairs={{64,128},{128,64},{192,256},{256,192},{320,384},{384,320},{65,129}... | collective-permute-start | bytes 1572872 | tf_op jit(solution)/shard_map/ppermute | solution.py:33
  16.6 6.7 %collective-permute-start.3 = (f32[576,128]{1,0:T(8,128)S(1)}, f32[576,128]{1,0:T(8,128)S(1)}, u32[]{:S(2)}, u32[]{:S(2)}) collective-permute-start(f32[576,128]{1,0:T(8,128)S(1)} %get-tuple-element.12), channel_id=1, source_target_pairs={{0,64},{64,0},{128,192},{192,128},{256,320},{320,256},{384,448},{4... | collective-permute-start | bytes 884744 | tf_op jit(solution)/shard_map/ppermute | solution.py:27
  23.2 0.0 copy-done
  23.3 0.1 fusion
  23.4 0.1 fusion.1.power
  23.5 0.0 copy-done.6
  23.5 0.0 copy-done.7
  23.5 0.0 copy-start.3
  23.6 0.0 copy-start.4
  23.6 0.0 copy-start.5
  23.6 8.4 %shard_map.96.refs_0_ = f32[16,128,128]{2,1,0:T(8,128)S(1)} custom-call(f32[1,16,128,128]{3,2,1,0:T(8,128)S(1)} %copy-done.1, f32[1,16,128,128]{3,2,1,0:T(8,128)S(1)} %copy-done.2, f32[128,128]{1,0:T(8,128)S(1)} %copy-done.6, f32[128,128]{1,0:T(8,128)S(1)} %copy-done.7, f32[112,128]{1,0:T(8,128)S(1)} %collective-permute-done.before.refs_3_.refs_4_, ...), custom_call_target="tpu_custom_call" | custom-call | flops 1000 | bytes 1000 | tf_op jit(solution)/shard_map/pallas_call | solution.py:225
  32.0 0.0 collective-permute-done.2.refs_2_
  32.0 0.0 copy-done.3
  32.0 0.0 copy-done.4
  32.1 0.0 copy-done.5
  32.1 0.7 %shard_map.98.refs_9_ = f32[11,128,128]{2,1,0:T(8,128)S(1)} custom-call(f32[16,128,128]{2,1,0:T(8,128)S(1)} %shard_map.96.refs_0_, f32[1,16,128,128]{3,2,1,0:T(8,128)S(1)} %copy-done.1, f32[1536,128]{1,0:T(8,128)S(1)} %collective-permute-done.2.refs_2_, f32[112,128]{1,0:T(8,128)S(1)} %collective-permute-done.before.refs_3_.refs_4_, ...), custom_call_target="tpu_custom_call" | custom-call | flops 1000 | bytes 1000 | tf_op jit(solution)/shard_map/pallas_call | solution.py:461
  32.8 0.0 collective-permute-done.4.refs_2_
  32.8 0.0 collective-permute-done.5.refs_3_
  32.8 2.2 %shard_map.100 = (f32[1,16,128,128]{3,2,1,0:T(8,128)}, f32[1,16,128,128]{3,2,1,0:T(8,128)}) custom-call(f32[16,128,128]{2,1,0:T(8,128)S(1)} %shard_map.96.refs_0_, f32[1,16,128,128]{3,2,1,0:T(8,128)S(1)} %copy-done.1, f32[1088,128]{1,0:T(8,128)S(1)} %collective-permute-done.4.refs_2_, f32[1024,128]{1,0:T(8,128)S(1)} %collective-permute-done.5.refs_3_, ...), custom_call_target="tpu_custom_call" | custom-call | flops 1000 | bytes 1000 | tf_op jit(solution)/shard_map/pallas_call | solution.py:425
  35.1 20.1 %collective-permute-done.3.refs_3_ = f32[576,128]{1,0:T(8,128)S(1)} collective-permute-done((f32[576,128]{1,0:T(8,128)S(1)}, f32[576,128]{1,0:T(8,128)S(1)}, u32[]{:S(2)}, u32[]{:S(2)}) %collective-permute-start.3) | collective-permute-done | bytes 294944 | tf_op jit(solution)/shard_map/ppermute | solution.py:27
  55.2 1.5 %shard_map.101 = (f32[1,16,128,128]{3,2,1,0:T(8,128)}, f32[1,16,128,128]{3,2,1,0:T(8,128)}) custom-call(f32[16,128,128]{2,1,0:T(8,128)S(1)} %shard_map.96.refs_0_, f32[1,16,128,128]{3,2,1,0:T(8,128)S(1)} %copy-done.1, f32[1536,128]{1,0:T(8,128)S(1)} %collective-permute-done.2.refs_2_, ...), custom_call_target="tpu_custom_call", output_to_operand_aliasing={{0}: (10, {}), {1}: (11, {})} | custom-call | flops 1000 | bytes 1000 | tf_op jit(solution)/shard_map/pallas_call | solution.py:425
Async XLA Ops:
  0.6 22.6 %copy-start = (f32[16,16]{1,0:T(8,128)S(1)}, f32[16,16]{1,0:T(8,128)}, u32[]{:S(2)}) copy-start(f32[16,16]{1,0:T(8,128)} %param.15) | copy-start | bytes 3076
  3.0 10.7 %copy-start.1 = (f32[1,16,128,128]{3,2,1,0:T(8,128)S(1)}, f32[1,16,128,128]{3,2,1,0:T(8,128)}, u32[]{:S(2)}) copy-start(f32[1,16,128,128]{3,2,1,0:T(8,128)} %refs_1_.7) | copy-start | bytes 3145732
  3.0 10.7 %copy-start.2 = (f32[1,16,128,128]{3,2,1,0:T(8,128)S(1)}, f32[1,16,128,128]{3,2,1,0:T(8,128)}, u32[]{:S(2)}) copy-start(f32[1,16,128,128]{3,2,1,0:T(8,128)} %inc.3) | copy-start | bytes 3145732
  3.0 29.0 %collective-permute-start.2 = (f32[1536,128]{1,0:T(8,128)}, f32[1536,128]{1,0:T(8,128)S(1)}, u32[]{:S(2)}, u32[]{:S(2)}) collective-permute-start(f32[1536,128]{1,0:T(8,128)} %bitcast), channel_id=1, source_target_pairs={{0,64},{64,0},{128,192},{192,128},{256,320},{320,256},{384,448},{4... | collective-permute-start | bytes 2359304 | tf_op jit(solution)/shard_map/ppermute | solution.py:27
  8.1 6.4 %collective-permute-start = (f32[112,128]{1,0:T(8,128)}, f32[112,128]{1,0:T(8,128)S(1)}, u32[]{:S(2)}, u32[]{:S(2)}) collective-permute-start(f32[112,128]{1,0:T(8,128)} %get-tuple-element.10), channel_id=1, source_target_pairs={{0,1},{1,2},{2,3},{3,4},{4,5},{5,6},{6,7},{7,8},{8,9},{9,10},{10,1... | collective-permute-start | bytes 172040 | tf_op jit(solution)/shard_map/ppermute | solution.py:22
  10.0 5.8 %collective-permute-start.1 = (f32[112,128]{1,0:T(8,128)}, f32[112,128]{1,0:T(8,128)S(1)}, u32[]{:S(2)}, u32[]{:S(2)}) collective-permute-start(f32[112,128]{1,0:T(8,128)} %get-tuple-element.11), channel_id=1, source_target_pairs={{0,63},{1,0},{2,1},{3,2},{4,3},{5,4},{6,5},{7,6},{8,7},{9,8},{10,9... | collective-permute-start | bytes 172040 | tf_op jit(solution)/shard_map/ppermute | solution.py:22
  13.8 19.1 %collective-permute-start.4 = (f32[1088,128]{1,0:T(8,128)S(1)}, f32[1088,128]{1,0:T(8,128)S(1)}, u32[]{:S(2)}, u32[]{:S(2)}) collective-permute-start(f32[1088,128]{1,0:T(8,128)S(1)} %shard_map.99), channel_id=1, source_target_pairs={{64,128},{128,64},{192,256},{256,192},{320,384},{384,320},{65,129}... | collective-permute-start | bytes 1671176 | tf_op jit(solution)/shard_map/ppermute | solution.py:33
  15.8 7.7 %copy-start.6 = (f32[128,128]{1,0:T(8,128)S(1)}, f32[128,128]{1,0:T(8,128)}, u32[]{:S(2)}) copy-start(f32[128,128]{1,0:T(8,128)} %std.1) | copy-start | bytes 196612
  15.8 7.7 %copy-start.7 = (f32[128,128]{1,0:T(8,128)S(1)}, f32[128,128]{1,0:T(8,128)}, u32[]{:S(2)}) copy-start(f32[128,128]{1,0:T(8,128)} %kappa.1) | copy-start | bytes 196612
  15.9 17.0 %collective-permute-start.5 = (f32[1024,128]{1,0:T(8,128)S(1)}, f32[1024,128]{1,0:T(8,128)S(1)}, u32[]{:S(2)}, u32[]{:S(2)}) collective-permute-start(f32[1024,128]{1,0:T(8,128)S(1)} %get-tuple-element.14), channel_id=1, source_target_pairs={{64,128},{128,64},{192,256},{256,192},{320,384},{384,320},{65,129}... | collective-permute-start | bytes 1572872 | tf_op jit(solution)/shard_map/ppermute | solution.py:33
  16.6 38.7 %collective-permute-start.3 = (f32[576,128]{1,0:T(8,128)S(1)}, f32[576,128]{1,0:T(8,128)S(1)}, u32[]{:S(2)}, u32[]{:S(2)}) collective-permute-start(f32[576,128]{1,0:T(8,128)S(1)} %get-tuple-element.12), channel_id=1, source_target_pairs={{0,64},{64,0},{128,192},{192,128},{256,320},{320,256},{384,448},{4... | collective-permute-start | bytes 884744 | tf_op jit(solution)/shard_map/ppermute | solution.py:27
  23.5 8.5 %copy-start.3 = (f32[128,128]{1,0:T(8,128)S(1)}, f32[128,128]{1,0:T(8,128)}, u32[]{:S(2)}) copy-start(f32[128,128]{1,0:T(8,128)} %refs_6_.7) | copy-start | bytes 196612
  23.6 8.5 %copy-start.4 = (s32[128,128]{1,0:T(8,128)S(1)}, s32[128,128]{1,0:T(8,128)}, u32[]{:S(2)}) copy-start(s32[128,128]{1,0:T(8,128)} %refs_7_.7) | copy-start | bytes 196612
  23.6 8.5 %copy-start.5 = (s32[128,128]{1,0:T(8,128)S(1)}, s32[128,128]{1,0:T(8,128)}, u32[]{:S(2)}) copy-start(s32[128,128]{1,0:T(8,128)} %refs_8_.4) | copy-start | bytes 196612
